TPU v7x, 32 devices: a whole 2x2x4 slice. The times are simulated.
32 devices in a mesh: clip: 4 (over y, x), frame: 8 (over z, core).
Axes of the slice: x: 2, y: 2, z: 4, core: 2. Of those that a mesh axis runs over, the one named last changes fastest.
Arguments:
- latents: bfloat16 [4, 8, 512, 1152], P('clip', 'frame'), may hold values from -6 to 6
- cotangent: bfloat16 [4, 8, 512, 1152], P('clip', 'frame'), may hold values from -6 to 6
- text_tokens: bfloat16 [4, 4, 120, 4096], P('clip'), may hold values from -6 to 6
- text_lengths: int32 [4, 4], P('clip'), may hold values from 77 to 120, as said below
- clip_frames: int32 [4, 4], P('clip'), may hold values from 0 to 6, as said below
- timesteps: int32 [4, 4], P('clip'), may hold values from 0 to 999
- motion_free: int32 [4, 4], P('clip'), may hold values from 0 to 1
- modulation_weight: bfloat16 [1152, 6912], P('frame'), may hold values from -0.1875 to 0.1875
- modulation_bias: bfloat16 [6912], P('frame'), may hold values from -3 to 3
- spatial_input: bfloat16 [1152, 3456], P('frame'), may hold values from -0.1875 to 0.1875
- spatial_output: bfloat16 [1152, 1152], P('frame'), may hold values from -1 to 1
- spatial_bias: bfloat16 [1152], P('frame'), may hold values from -3 to 3
- text_projection: bfloat16 [4096, 1152], P('frame'), may hold values from -0.09375 to 0.09375
- cross_query: bfloat16 [1152, 1152], P('frame'), may hold values from -0.1875 to 0.1875
- cross_memory: bfloat16 [1152, 2304], P('frame'), may hold values from -0.1875 to 0.1875
- cross_output: bfloat16 [1152, 1152], P('frame'), may hold values from -0.75 to 0.75
- cross_bias: bfloat16 [1152], P('frame'), may hold values from -3 to 3
- expand_weight: bfloat16 [1152, 4608], P('frame'), may hold values from -0.1875 to 0.1875
- expand_bias: bfloat16 [4608], P('frame'), may hold values from -3 to 3
- reduce_weight: bfloat16 [4608, 1152], P('frame'), may hold values from -0.09375 to 0.09375
- reduce_bias: bfloat16 [1152], P('frame'), may hold values from -3 to 3
- temporal_gain: bfloat16 [1152], P('frame'), may hold values from 0.5 to 1.5
- temporal_shift: bfloat16 [1152], P('frame'), may hold values from -3 to 3
- temporal_input: bfloat16 [1152, 3456], P('frame'), may hold values from -0.1875 to 0.1875
- temporal_output: bfloat16 [1152, 1152], P('frame'), may hold values from -0.375 to 0.375
- temporal_bias: bfloat16 [1152], P('frame'), may hold values from -3 to 3
- temporal_gate: bfloat16 [1152], P('frame'), may hold values from -6 to 6
Outputs:
- block_output: bfloat16 [4, 8, 512, 1152], P('clip', 'frame')
- input_gradient: bfloat16 [4, 8, 512, 1152], P('clip', 'frame')
- gradient_modulation_weight: float32 [1152, 6912], P('frame')
- gradient_modulation_bias: float32 [6912], P('frame')
- gradient_spatial_input: float32 [1152, 3456], P('frame')
- gradient_spatial_output: float32 [1152, 1152], P('frame')
- gradient_spatial_bias: float32 [1152], P('frame')
- gradient_text_projection: float32 [4096, 1152], P('frame')
- gradient_cross_query: float32 [1152, 1152], P('frame')
- gradient_cross_memory: float32 [1152, 2304], P('frame')
- gradient_cross_output: float32 [1152, 1152], P('frame')
- gradient_cross_bias: float32 [1152], P('frame')
- gradient_expand_weight: float32 [1152, 4608], P('frame')
- gradient_expand_bias: float32 [4608], P('frame')
- gradient_reduce_weight: float32 [4608, 1152], P('frame')
- gradient_reduce_bias: float32 [1152], P('frame')
- gradient_temporal_gain: float32 [1152], P('frame')
- gradient_temporal_shift: float32 [1152], P('frame')
- gradient_temporal_input: float32 [1152, 3456], P('frame')
- gradient_temporal_output: float32 [1152, 1152], P('frame')
- gradient_temporal_bias: float32 [1152], P('frame')
- gradient_temporal_gate: float32 [1152], P('frame')
Inputs may be any that keep to these rules, and one draw needn't show every extreme that they name: `clip_frames`: each entry is a multiple of 2 frames; the entries of a group sum to 8, and every group holds a clip of 6 frames. `text_lengths`: A clip reads the first that many of its 120 text rows.
All inputs are finite; a program needn't handle non-finite values.
Results may differ from a plain program's by a relative error of at most 0.02875.
Values may be sent and summed in bfloat16 or wider, within the bound.
A program may use at most 384 MiB of HBM per device.

v0:
```python
import math

import jax
import jax.numpy as jnp
from jax import lax
from jax.sharding import PartitionSpec as P

HEADS = 16


eps_norm = 1e-06
big_negative = -1e30


def assign_clips(frame_counts, frame_count):
    slot_count = frame_counts.shape[0]
    slot_ids = jnp.arange(slot_count, dtype=jnp.int32)
    longest = jnp.max(frame_counts)
    long_slot = jnp.min(jnp.where(frame_counts == longest, slot_ids, slot_count))
    frame_ids = jnp.arange(frame_count, dtype=jnp.int32)
    long_gaps = jnp.maximum(longest - 1, 1)
    frame_gaps = frame_count - 1
    step_index = (frame_ids * long_gaps + frame_gaps - 1) // frame_gaps
    on_long = step_index * frame_gaps // long_gaps == frame_ids
    long_marks = on_long.astype(jnp.int32)
    before_count = jnp.cumsum(long_marks) - long_marks
    order_rank = frame_ids - before_count
    rest_counts = jnp.where(slot_ids == long_slot, 0, frame_counts)
    rest_ends = jnp.cumsum(rest_counts)
    rest_ids = jnp.sum((rest_ends[None, :] <= order_rank[:, None]).astype(jnp.int32), axis=1)
    return jnp.where(on_long, long_slot, rest_ids)


def normalize(values):
    average = jnp.mean(values, axis=-1, keepdims=True)
    centred = values - average
    spread = jnp.mean(centred * centred, axis=-1, keepdims=True)
    return centred * lax.rsqrt(spread + eps_norm)


def modulate(values, offset, scaling):
    return normalize(values) * (1.0 + scaling) + offset


def affine_norm(values, norm_gain, offset):
    return normalize(values) * norm_gain + offset


def smooth_gelu(values):
    return jax.nn.gelu(values, approximate=True)


def embed_time(time_steps, model_width):
    half_width = model_width // 2
    frequency = jnp.exp(-math.log(10000.0) * jnp.arange(half_width, dtype=jnp.float32) / half_width)
    angles = time_steps.astype(jnp.float32)[:, None] * frequency[None, :]
    return jax.nn.silu(jnp.concatenate([jnp.cos(angles), jnp.sin(angles)], axis=1))


def attend(queries, key_rows, values, valid_mask, att_scale):
    scores = (
        jnp.einsum("qbhd,kbhd->bhqk", queries, key_rows, preferred_element_type=jnp.float32)
        * att_scale
    )
    if valid_mask is not None:
        scores = jnp.where(valid_mask, scores, big_negative)
    largest = jnp.max(scores, axis=-1, keepdims=True)
    summed = jnp.sum(jnp.exp(scores - largest), axis=-1, keepdims=True)
    logsum = largest + jnp.log(summed)
    weights = jnp.exp(scores - logsum).astype(jnp.bfloat16)
    output = jnp.einsum("bhqk,kbhd->qbhd", weights, values, preferred_element_type=jnp.float32)
    return (output, logsum)


def attend_back(queries, key_rows, values, valid_mask, att_scale, logsum, upstream):
    scores = (
        jnp.einsum("qbhd,kbhd->bhqk", queries, key_rows, preferred_element_type=jnp.float32)
        * att_scale
    )
    if valid_mask is not None:
        scores = jnp.where(valid_mask, scores, big_negative)
    weights = jnp.exp(scores - logsum)
    back_weights = jnp.einsum(
        "qbhd,kbhd->bhqk", upstream, values, preferred_element_type=jnp.float32
    )
    back_values = jnp.einsum(
        "bhqk,qbhd->kbhd",
        weights.astype(jnp.bfloat16),
        upstream,
        preferred_element_type=jnp.float32,
    )
    inner_sum = jnp.sum(back_weights * weights, axis=-1, keepdims=True)
    back_scores = (weights * (back_weights - inner_sum)).astype(jnp.bfloat16)
    back_queries = (
        jnp.einsum("bhqk,kbhd->qbhd", back_scores, key_rows, preferred_element_type=jnp.float32)
        * att_scale
    )
    back_keys = (
        jnp.einsum("bhqk,qbhd->kbhd", back_scores, queries, preferred_element_type=jnp.float32)
        * att_scale
    )
    return (back_queries, back_keys, back_values)


def on_device(
    latents,
    cotangent,
    text_tokens,
    text_lengths,
    clip_frames,
    timesteps,
    motion_free,
    modulation_weight,
    modulation_bias,
    spatial_input,
    spatial_output,
    spatial_bias,
    text_projection,
    cross_query,
    cross_memory,
    cross_output,
    cross_bias,
    expand_weight,
    expand_bias,
    reduce_weight,
    reduce_bias,
    temporal_gain,
    temporal_shift,
    temporal_input,
    temporal_output,
    temporal_bias,
    temporal_gate,
):
    frame_count = lax.axis_size("frame")
    frame_index = lax.axis_index("frame")
    patch_count = latents.shape[2]
    model_width = latents.shape[3]
    head_size = model_width // HEADS
    att_scale = 1.0 / math.sqrt(head_size)
    slot_count = clip_frames.shape[1]
    text_count = text_tokens.shape[2]
    frame_ids = jnp.arange(frame_count, dtype=jnp.int32)
    clip_ids = assign_clips(clip_frames[0], frame_count)
    slot_ids = jnp.arange(slot_count, dtype=jnp.int32)
    own_clip = jnp.sum(jnp.where(frame_ids == frame_index, clip_ids, 0))
    own_onehot = (slot_ids == own_clip).astype(jnp.float32)
    own_keep = 1.0 - jnp.sum(jnp.where(slot_ids == own_clip, motion_free[0], 0)).astype(jnp.float32)
    own_length = jnp.sum(jnp.where(slot_ids == own_clip, text_lengths[0], 0))
    conditioning = embed_time(timesteps[0], model_width).astype(jnp.bfloat16)
    row_count = modulation_weight.shape[0]
    cond_rows = lax.dynamic_slice_in_dim(conditioning, frame_index * row_count, row_count, 1)
    bias_width = modulation_bias.shape[0]
    bias_placed = lax.dynamic_update_slice_in_dim(
        jnp.zeros((6 * model_width,), jnp.float32),
        modulation_bias.astype(jnp.float32),
        frame_index * bias_width,
        0,
    )
    modulation_part = (
        jnp.dot(cond_rows, modulation_weight, preferred_element_type=jnp.float32)
        + bias_placed[None, :]
    )
    share_rows = text_projection.shape[0]
    text_share = lax.dynamic_slice_in_dim(text_tokens[0], frame_index * share_rows, share_rows, 2)
    own_text = lax.dynamic_index_in_dim(text_tokens[0], own_clip, 0, keepdims=False)
    modulation = lax.psum(modulation_part, "frame")
    projection = lax.all_gather(text_projection, "frame", axis=0, tiled=True)
    context = jnp.dot(own_text, projection, preferred_element_type=jnp.float32)
    own_modulation = lax.dynamic_index_in_dim(modulation, own_clip, 0, keepdims=False)
    shift_attend, scale_attend, gate_attend, shift_feed, scale_feed, gate_feed = jnp.split(
        own_modulation, 6
    )
    (
        whole_input,
        whole_output,
        whole_bias,
        whole_query,
        whole_memory,
        whole_cross,
        whole_cross_bias,
        whole_expand,
        whole_expand_bias,
        whole_reduce,
        whole_reduce_bias,
        whole_gain,
        whole_shift,
        whole_temporal,
        whole_temporal_out,
        whole_temporal_bias,
        whole_gate,
    ) = (
        lax.all_gather(spatial_input, "frame", axis=0, tiled=True),
        lax.all_gather(spatial_output, "frame", axis=0, tiled=True),
        lax.all_gather(spatial_bias, "frame", axis=0, tiled=True),
        lax.all_gather(cross_query, "frame", axis=0, tiled=True),
        lax.all_gather(cross_memory, "frame", axis=0, tiled=True),
        lax.all_gather(cross_output, "frame", axis=0, tiled=True),
        lax.all_gather(cross_bias, "frame", axis=0, tiled=True),
        lax.all_gather(expand_weight, "frame", axis=0, tiled=True),
        lax.all_gather(expand_bias, "frame", axis=0, tiled=True),
        lax.all_gather(reduce_weight, "frame", axis=0, tiled=True),
        lax.all_gather(reduce_bias, "frame", axis=0, tiled=True),
        lax.all_gather(temporal_gain, "frame", axis=0, tiled=True),
        lax.all_gather(temporal_shift, "frame", axis=0, tiled=True),
        lax.all_gather(temporal_input, "frame", axis=0, tiled=True),
        lax.all_gather(temporal_output, "frame", axis=0, tiled=True),
        lax.all_gather(temporal_bias, "frame", axis=0, tiled=True),
        lax.all_gather(temporal_gate, "frame", axis=0, tiled=True),
    )
    tokens = latents[0, 0].astype(jnp.float32)
    normed_attend = modulate(tokens, shift_attend, scale_attend).astype(jnp.bfloat16)
    spatial_heads = jnp.dot(normed_attend, whole_input, preferred_element_type=jnp.float32).astype(
        jnp.bfloat16
    )
    spatial_heads = spatial_heads.reshape(patch_count, 1, 3, HEADS, head_size)
    spatial_att, spatial_logsum = attend(
        spatial_heads[:, :, 0], spatial_heads[:, :, 1], spatial_heads[:, :, 2], None, att_scale
    )
    spatial_low = spatial_att.reshape(patch_count, model_width).astype(jnp.bfloat16)
    branch_attend = jnp.dot(
        spatial_low, whole_output, preferred_element_type=jnp.float32
    ) + whole_bias.astype(jnp.float32)
    after_attend = tokens + gate_attend * branch_attend
    after_low = after_attend.astype(jnp.bfloat16)
    cross_heads = jnp.dot(after_low, whole_query, preferred_element_type=jnp.float32).astype(
        jnp.bfloat16
    )
    cross_heads = cross_heads.reshape(patch_count, 1, HEADS, head_size)
    context_low = context.astype(jnp.bfloat16)
    memory_heads = jnp.dot(context_low, whole_memory, preferred_element_type=jnp.float32).astype(
        jnp.bfloat16
    )
    memory_heads = memory_heads.reshape(text_count, 1, 2, HEADS, head_size)
    text_mask = (jnp.arange(text_count, dtype=jnp.int32) < own_length)[None, None, None, :]
    cross_att, cross_logsum = attend(
        cross_heads, memory_heads[:, :, 0], memory_heads[:, :, 1], text_mask, att_scale
    )
    cross_low = cross_att.reshape(patch_count, model_width).astype(jnp.bfloat16)
    branch_cross = jnp.dot(
        cross_low, whole_cross, preferred_element_type=jnp.float32
    ) + whole_cross_bias.astype(jnp.float32)
    after_cross = after_attend + branch_cross
    normed_feed = modulate(after_cross, shift_feed, scale_feed).astype(jnp.bfloat16)
    hidden_pre = jnp.dot(
        normed_feed, whole_expand, preferred_element_type=jnp.float32
    ) + whole_expand_bias.astype(jnp.float32)
    hidden_low = smooth_gelu(hidden_pre).astype(jnp.bfloat16)
    branch_feed = jnp.dot(
        hidden_low, whole_reduce, preferred_element_type=jnp.float32
    ) + whole_reduce_bias.astype(jnp.float32)
    after_feed = after_cross + gate_feed * branch_feed
    sent_low = after_feed.astype(jnp.bfloat16)
    time_mask = (clip_ids[:, None] == clip_ids[None, :])[None, None]
    gain_float = whole_gain.astype(jnp.float32)
    shift_float = whole_shift.astype(jnp.float32)
    columns = lax.all_to_all(sent_low[None], "frame", split_axis=1, concat_axis=0, tiled=True)
    frames_here = columns.shape[0]
    positions = columns.shape[1]
    normed_time = affine_norm(columns.astype(jnp.float32), gain_float, shift_float).astype(
        jnp.bfloat16
    )
    time_heads = jnp.einsum(
        "fpd,de->fpe", normed_time, whole_temporal, preferred_element_type=jnp.float32
    )
    time_heads = time_heads.astype(jnp.bfloat16).reshape(
        frames_here, positions, 3, HEADS, head_size
    )
    time_att, time_logsum = attend(
        time_heads[:, :, 0], time_heads[:, :, 1], time_heads[:, :, 2], time_mask, att_scale
    )
    time_low = time_att.reshape(frames_here, positions, model_width).astype(jnp.bfloat16)
    result = jnp.einsum(
        "fpd,de->fpe", time_low, whole_temporal_out, preferred_element_type=jnp.float32
    )
    result = result + whole_temporal_bias.astype(jnp.float32)
    result_low = result.astype(jnp.bfloat16)
    kept_state = (normed_time, time_heads, time_low, time_logsum)
    returned = lax.all_to_all(result_low, "frame", split_axis=0, concat_axis=1, tiled=True)
    temporal_value = returned[0].astype(jnp.float32)
    gate_keep = whole_gate.astype(jnp.float32) * own_keep
    block_output = (after_feed + gate_keep * temporal_value).astype(jnp.bfloat16)[None, None]
    upstream = cotangent[0, 0].astype(jnp.float32)
    back_gate = jnp.sum(upstream * temporal_value, axis=0) * own_keep
    back_sent = (upstream * gate_keep).astype(jnp.bfloat16)
    back_columns = lax.all_to_all(back_sent[None], "frame", split_axis=1, concat_axis=0, tiled=True)
    normed_time, time_heads, time_low, time_logsum = kept_state
    frames_here, positions = (columns.shape[0], columns.shape[1])
    back_temporal_bias = jnp.sum(back_columns.astype(jnp.float32), axis=(0, 1))
    back_temporal_out = jnp.einsum(
        "fpd,fpe->de", time_low, back_columns, preferred_element_type=jnp.float32
    )
    back_time_att = jnp.einsum(
        "fpe,de->fpd", back_columns, whole_temporal_out, preferred_element_type=jnp.float32
    )
    back_time_att = back_time_att.astype(jnp.bfloat16).reshape(
        frames_here, positions, HEADS, head_size
    )
    back_time_queries, back_time_keys, back_time_values = attend_back(
        time_heads[:, :, 0],
        time_heads[:, :, 1],
        time_heads[:, :, 2],
        time_mask,
        att_scale,
        time_logsum,
        back_time_att,
    )
    back_time_heads = jnp.stack([back_time_queries, back_time_keys, back_time_values], axis=2)
    back_time_heads = back_time_heads.reshape(frames_here, positions, 3 * model_width).astype(
        jnp.bfloat16
    )
    back_temporal = jnp.einsum(
        "fpd,fpe->de", normed_time, back_time_heads, preferred_element_type=jnp.float32
    )
    back_normed = jnp.einsum(
        "fpe,de->fpd", back_time_heads, whole_temporal, preferred_element_type=jnp.float32
    )
    unused_norm, norm_back = jax.vjp(
        affine_norm, columns.astype(jnp.float32), gain_float, shift_float
    )
    back_inputs, back_gain, back_shift = norm_back(back_normed)
    back_return = lax.all_to_all(
        back_inputs.astype(jnp.bfloat16), "frame", split_axis=0, concat_axis=1, tiled=True
    )
    back_feed_total = upstream + back_return[0].astype(jnp.float32)
    back_gate_feed = jnp.sum(back_feed_total * branch_feed, axis=0)
    back_branch_feed = (back_feed_total * gate_feed).astype(jnp.bfloat16)
    back_reduce_bias = jnp.sum(back_branch_feed.astype(jnp.float32), axis=0)
    back_reduce = jnp.einsum(
        "pf,pd->fd", hidden_low, back_branch_feed, preferred_element_type=jnp.float32
    )
    back_hidden = jnp.einsum(
        "pd,fd->pf", back_branch_feed, whole_reduce, preferred_element_type=jnp.float32
    )
    unused_gelu, gelu_back = jax.vjp(smooth_gelu, hidden_pre)
    back_pre = gelu_back(back_hidden)[0].astype(jnp.bfloat16)
    back_expand_bias = jnp.sum(back_pre.astype(jnp.float32), axis=0)
    back_expand = jnp.einsum("pd,pf->df", normed_feed, back_pre, preferred_element_type=jnp.float32)
    back_normed_feed = jnp.einsum(
        "pf,df->pd", back_pre, whole_expand, preferred_element_type=jnp.float32
    )
    unused_feed, feed_back = jax.vjp(modulate, after_cross, shift_feed, scale_feed)
    back_cross_in, back_shift_feed, back_scale_feed = feed_back(back_normed_feed)
    back_after_cross = back_feed_total + back_cross_in
    back_branch_cross = back_after_cross.astype(jnp.bfloat16)
    back_cross_bias = jnp.sum(back_branch_cross.astype(jnp.float32), axis=0)
    back_cross_output = jnp.einsum(
        "pd,pe->de", cross_low, back_branch_cross, preferred_element_type=jnp.float32
    )
    back_cross_att = jnp.einsum(
        "pe,de->pd", back_branch_cross, whole_cross, preferred_element_type=jnp.float32
    )
    back_cross_att = back_cross_att.astype(jnp.bfloat16).reshape(patch_count, 1, HEADS, head_size)
    back_cross_queries, back_memory_keys, back_memory_values = attend_back(
        cross_heads,
        memory_heads[:, :, 0],
        memory_heads[:, :, 1],
        text_mask,
        att_scale,
        cross_logsum,
        back_cross_att,
    )
    back_cross_heads = back_cross_queries.reshape(patch_count, model_width).astype(jnp.bfloat16)
    back_memory_heads = jnp.stack([back_memory_keys, back_memory_values], axis=2)
    back_memory_heads = back_memory_heads.reshape(text_count, 2 * model_width).astype(jnp.bfloat16)
    back_cross_query = jnp.einsum(
        "pd,pe->de", after_low, back_cross_heads, preferred_element_type=jnp.float32
    )
    back_cross_memory = jnp.einsum(
        "td,te->de", context_low, back_memory_heads, preferred_element_type=jnp.float32
    )
    back_context = jnp.einsum(
        "te,de->td", back_memory_heads, whole_memory, preferred_element_type=jnp.float32
    )
    back_after_attend = back_after_cross + jnp.einsum(
        "pe,de->pd", back_cross_heads, whole_query, preferred_element_type=jnp.float32
    )
    back_gate_attend = jnp.sum(back_after_attend * branch_attend, axis=0)
    back_branch_attend = (back_after_attend * gate_attend).astype(jnp.bfloat16)
    back_spatial_bias = jnp.sum(back_branch_attend.astype(jnp.float32), axis=0)
    back_spatial_output = jnp.einsum(
        "pd,pe->de", spatial_low, back_branch_attend, preferred_element_type=jnp.float32
    )
    back_spatial_att = jnp.einsum(
        "pe,de->pd", back_branch_attend, whole_output, preferred_element_type=jnp.float32
    )
    back_spatial_att = back_spatial_att.astype(jnp.bfloat16).reshape(
        patch_count, 1, HEADS, head_size
    )
    back_spatial_queries, back_spatial_keys, back_spatial_values = attend_back(
        spatial_heads[:, :, 0],
        spatial_heads[:, :, 1],
        spatial_heads[:, :, 2],
        None,
        att_scale,
        spatial_logsum,
        back_spatial_att,
    )
    back_spatial_heads = jnp.stack(
        [back_spatial_queries, back_spatial_keys, back_spatial_values], axis=2
    )
    back_spatial_heads = back_spatial_heads.reshape(patch_count, 3 * model_width).astype(
        jnp.bfloat16
    )
    back_spatial_input = jnp.einsum(
        "pd,pe->de", normed_attend, back_spatial_heads, preferred_element_type=jnp.float32
    )
    back_normed_attend = jnp.einsum(
        "pe,de->pd", back_spatial_heads, whole_input, preferred_element_type=jnp.float32
    )
    unused_attend, attend_norm_back = jax.vjp(modulate, tokens, shift_attend, scale_attend)
    back_tokens, back_shift_attend, back_scale_attend = attend_norm_back(back_normed_attend)
    input_gradient = (back_after_attend + back_tokens).astype(jnp.bfloat16)[None, None]
    back_modulation_row = jnp.concatenate(
        [
            back_shift_attend,
            back_scale_attend,
            back_gate_attend,
            back_shift_feed,
            back_scale_feed,
            back_gate_feed,
        ]
    )
    modulation_terms = own_onehot[:, None] * back_modulation_row[None, :]
    context_terms = own_onehot[:, None, None] * back_context[None]
    modulation_total, context_total = lax.psum((modulation_terms, context_terms), "frame")
    back_modulation_weight = jnp.dot(
        cond_rows.astype(jnp.float32).T, modulation_total, precision=lax.Precision.HIGHEST
    )
    back_modulation_bias = lax.dynamic_slice_in_dim(
        jnp.sum(modulation_total, axis=0), frame_index * bias_width, bias_width, 0
    )
    back_text_projection = jnp.einsum(
        "stk,std->kd",
        text_share,
        context_total.astype(jnp.bfloat16),
        preferred_element_type=jnp.float32,
    )
    part_sin, part_sout, part_cq, part_cmem, part_cout, part_exp, part_red, part_tin, part_tout = (
        back_spatial_input,
        back_spatial_output,
        back_cross_query,
        back_cross_memory,
        back_cross_output,
        back_expand,
        back_reduce,
        back_temporal,
        back_temporal_out,
    )
    shares = (
        lax.psum_scatter(part_sin, "frame", scatter_dimension=0, tiled=True),
        lax.psum_scatter(part_sout, "frame", scatter_dimension=0, tiled=True),
        lax.psum_scatter(part_cq, "frame", scatter_dimension=0, tiled=True),
        lax.psum_scatter(part_cmem, "frame", scatter_dimension=0, tiled=True),
        lax.psum_scatter(part_cout, "frame", scatter_dimension=0, tiled=True),
        lax.psum_scatter(part_exp, "frame", scatter_dimension=0, tiled=True),
        lax.psum_scatter(part_red, "frame", scatter_dimension=0, tiled=True),
        lax.psum_scatter(part_tin, "frame", scatter_dimension=0, tiled=True),
        lax.psum_scatter(part_tout, "frame", scatter_dimension=0, tiled=True),
        lax.psum_scatter(back_spatial_bias, "frame", scatter_dimension=0, tiled=True),
        lax.psum_scatter(back_cross_bias, "frame", scatter_dimension=0, tiled=True),
        lax.psum_scatter(back_expand_bias, "frame", scatter_dimension=0, tiled=True),
        lax.psum_scatter(back_reduce_bias, "frame", scatter_dimension=0, tiled=True),
        lax.psum_scatter(back_gain, "frame", scatter_dimension=0, tiled=True),
        lax.psum_scatter(back_shift, "frame", scatter_dimension=0, tiled=True),
        lax.psum_scatter(back_temporal_bias, "frame", scatter_dimension=0, tiled=True),
        lax.psum_scatter(back_gate, "frame", scatter_dimension=0, tiled=True),
    )
    matrix_totals = (
        lax.psum(shares[0].astype(jnp.bfloat16), "clip").astype(jnp.float32),
        lax.psum(shares[1].astype(jnp.bfloat16), "clip").astype(jnp.float32),
        lax.psum(shares[2].astype(jnp.bfloat16), "clip").astype(jnp.float32),
        lax.psum(shares[3].astype(jnp.bfloat16), "clip").astype(jnp.float32),
        lax.psum(shares[4].astype(jnp.bfloat16), "clip").astype(jnp.float32),
        lax.psum(shares[5].astype(jnp.bfloat16), "clip").astype(jnp.float32),
        lax.psum(shares[6].astype(jnp.bfloat16), "clip").astype(jnp.float32),
        lax.psum(shares[7].astype(jnp.bfloat16), "clip").astype(jnp.float32),
        lax.psum(shares[8].astype(jnp.bfloat16), "clip").astype(jnp.float32),
    )
    others = (
        lax.psum(back_modulation_weight.astype(jnp.bfloat16), "clip").astype(jnp.float32),
        lax.psum(back_modulation_bias.astype(jnp.bfloat16), "clip").astype(jnp.float32),
        lax.psum(back_text_projection.astype(jnp.bfloat16), "clip").astype(jnp.float32),
        lax.psum(shares[9].astype(jnp.bfloat16), "clip").astype(jnp.float32),
        lax.psum(shares[10].astype(jnp.bfloat16), "clip").astype(jnp.float32),
        lax.psum(shares[11].astype(jnp.bfloat16), "clip").astype(jnp.float32),
        lax.psum(shares[12].astype(jnp.bfloat16), "clip").astype(jnp.float32),
        lax.psum(shares[13].astype(jnp.bfloat16), "clip").astype(jnp.float32),
        lax.psum(shares[14].astype(jnp.bfloat16), "clip").astype(jnp.float32),
        lax.psum(shares[15].astype(jnp.bfloat16), "clip").astype(jnp.float32),
        lax.psum(shares[16].astype(jnp.bfloat16), "clip").astype(jnp.float32),
    )
    return (
        block_output,
        input_gradient,
        others[0],
        others[1],
        matrix_totals[0],
        matrix_totals[1],
        others[3],
        others[2],
        matrix_totals[2],
        matrix_totals[3],
        matrix_totals[4],
        others[4],
        matrix_totals[5],
        others[5],
        matrix_totals[6],
        others[6],
        others[7],
        others[8],
        matrix_totals[7],
        matrix_totals[8],
        others[9],
        others[10],
    )


def solution(mesh):
    placed = (
        P("clip", "frame", None, None),
        P("clip", "frame", None, None),
        P("clip", None, None, None),
        P("clip", None),
        P("clip", None),
        P("clip", None),
        P("clip", None),
        P("frame", None),
        P("frame"),
        P("frame", None),
        P("frame", None),
        P("frame"),
        P("frame", None),
        P("frame", None),
        P("frame", None),
        P("frame", None),
        P("frame"),
        P("frame", None),
        P("frame"),
        P("frame", None),
        P("frame"),
        P("frame"),
        P("frame"),
        P("frame", None),
        P("frame", None),
        P("frame"),
        P("frame"),
    )
    return jax.shard_map(
        on_device,
        mesh=mesh,
        in_specs=placed,
        out_specs=(
            P("clip", "frame", None, None),
            P("clip", "frame", None, None),
            P("frame", None),
            P("frame"),
            P("frame", None),
            P("frame", None),
            P("frame"),
            P("frame", None),
            P("frame", None),
            P("frame", None),
            P("frame", None),
            P("frame"),
            P("frame", None),
            P("frame"),
            P("frame", None),
            P("frame"),
            P("frame"),
            P("frame"),
            P("frame", None),
            P("frame", None),
            P("frame"),
            P("frame"),
        ),
        check_vma=False,
    )
```

profile of v0, /device:TPU:27, one launch (start us, length us, event | category | flops | bytes accessed | tf_op | source)
XLA Modules:
  0.0 2419.0 jit_solution(8869729926439001009)
XLA Ops:
  27.7 26.9 %all-reduce.17 = (bf16[1152]{0:T(1024)(128)(2,1)S(1)}, bf16[1152]{0:T(1024)(128)(2,1)S(1)}, bf16[1152]{0:T(1024)(128)(2,1)S(1)}, bf16[4608]{0:T(1024)(128)(2,1)S...) all-reduce(bf16[1152]{0:T(1024)(128)(2,1)S(1)} %dynamic-update-slic, ...), channel_id=1, replica_groups=mesh['clip'=4,'frame'=8] {'frame'}, use_global_device_ids=true, to_apply=%add | all-reduce | flops 12672 | bytes 50688
  82.7 85.8 %all-gather.11.cloned.1.call-done = bf16[1152,3456]{1,0:T(8,128)(2,1)} async-done(((bf16[144,3456]{1,0:T(8,128)(2,1)}), bf16[1152,3456]{1,0:T(8,128)(2,1)}) %all-gather.11.cloned.1.call-update) | async-done | bytes 7962640 | tf_op jit(solution)/shard_map/all_gather | solution.py:192
  218.2 20.0 all-gather.19.cloned.1.call-done
  245.2 83.8 %all-gather.15.cloned.1.call-done = bf16[4096,1152]{1,0:T(8,128)(2,1)} async-done(((bf16[512,1152]{1,0:T(8,128)(2,1)}), bf16[4096,1152]{1,0:T(8,128)(2,1)}) %all-gather.15.cloned.1.call-update) | async-done | bytes 9437200 | tf_op jit(solution)/shard_map/all_gather | solution.py:167
  334.5 51.4 %all-gather.17.cloned.1.call-done = bf16[1152,2304]{1,0:T(8,128)(2,1)} async-done(((bf16[144,2304]{1,0:T(8,128)(2,1)}), bf16[1152,2304]{1,0:T(8,128)(2,1)}) %all-gather.17.cloned.1.call-update) | async-done | bytes 5308432 | tf_op jit(solution)/shard_map/all_gather | solution.py:196
  395.7 25.2 %all-gather.21.cloned.1.call-done = bf16[1152,1152]{1,0:T(8,128)(2,1)} async-done(((bf16[144,1152]{1,0:T(8,128)(2,1)}), bf16[1152,1152]{1,0:T(8,128)(2,1)}) %all-gather.21.cloned.1.call-update) | async-done | bytes 2654224 | tf_op jit(solution)/shard_map/all_gather | solution.py:197
  427.3 94.1 %all-gather.23.cloned.1.call-done = bf16[1152,4608]{1,0:T(8,128)(2,1)} async-done(((bf16[144,4608]{1,0:T(8,128)(2,1)}), bf16[1152,4608]{1,0:T(8,128)(2,1)}) %all-gather.23.cloned.1.call-update) | async-done | bytes 10616848 | tf_op jit(solution)/shard_map/all_gather | solution.py:199
  521.5 12.2 fusion.115
  533.7 88.4 %all-gather.25.cloned.1.call-done = bf16[4608,1152]{1,0:T(8,128)(2,1)} async-done(((bf16[576,1152]{1,0:T(8,128)(2,1)}), bf16[4608,1152]{1,0:T(8,128)(2,1)}) %all-gather.25.cloned.1.call-update) | async-done | bytes 10616848 | tf_op jit(solution)/shard_map/all_gather | solution.py:201
  622.1 13.2 convolution_add_fusion.1
  675.6 32.5 %all-to-all-done = bf16[8,2,36864]{2,1,0:T(2,128)(2,1)S(1)} async-done(((bf16[8,2,36864]{2,1,0:T(2,128)(2,1)}), bf16[8,2,36864]{2,1,0:T(2,128)(2,1)S(1)}, u32[]{:S(2)}, u32[]{:S(2)}) %all-to-all-start) | async-done | bytes 1179680 | tf_op jit(solution)/shard_map/all_to_all | solution.py:256
  714.8 34.8 %all-gather.27.cloned.1.call-done = bf16[1152,3456]{1,0:T(8,128)(2,1)} async-done(((bf16[144,3456]{1,0:T(8,128)(2,1)}), bf16[1152,3456]{1,0:T(8,128)(2,1)}) %all-gather.27.cloned.1.call-update) | async-done | bytes 7962640 | tf_op jit(solution)/shard_map/all_gather | solution.py:205
  759.6 14.0 reshape.752
  826.3 10.8 convert_element_type.521
  856.4 26.2 %all-to-all-done.3 = bf16[8,64,1152]{2,1,0:T(8,128)(2,1)} async-done(((bf16[8,64,1152]{2,1,0:T(8,128)(2,1)}), bf16[8,64,1152]{2,1,0:T(8,128)(2,1)}, u32[]{:S(2)}, u32[]{:S(2)}) %all-to-all-start.3) | async-done | bytes 1179680 | tf_op jit(solution)/shard_map/all_to_all | solution.py:321
  888.5 18.6 convert_reduce_fusion
  907.1 11.6 multiply_reduce_fusion.6
  953.8 11.3 multiply_reduce_fusion
  965.1 12.1 multiply_convert_fusion
  1044.0 10.4 fusion.57
  1055.7 14.2 fusion.116
  1070.7 12.8 fusion.114
  1093.4 91.4 %all-reduce.30 = (bf16[1152]{0:T(1024)(128)(2,1)S(1)}, bf16[4,120,1152]{2,1,0:T(8,128)(2,1)S(1)}, bf16[1152]{0:T(1024)(128)(2,1)S(1)}, bf16[4608]{0:T(1024)(128)...) all-reduce(f32[1152]{0:T(1024)S(1)} %copy-done.82, ...), channel_id=4, replica_groups=mesh['clip'=4,'frame'=8] {'frame'}, use_global_device_ids=true, to_apply=%region_45.46.clone | all-reduce | flops 565632 | bytes 3393792
  1193.8 12.6 reduce-scatter.18.cloned.1.call-done
  1208.2 58.7 %reduce-scatter.14.cloned.1.call-done = f32[144,1152]{1,0:T(8,128)} async-done(((f32[1152,1152]{1,0:T(8,128)}), f32[144,1152]{1,0:T(8,128)}) %reduce-scatter.14.cloned.1.call-update) | async-done | bytes 663568 | tf_op jit(solution)/shard_map/reduce_scatter | solution.py:452
  1268.7 59.2 %reduce-scatter.12.cloned.1.call-done = f32[144,1152]{1,0:T(8,128)} async-done(((f32[1152,1152]{1,0:T(8,128)}), f32[144,1152]{1,0:T(8,128)}) %reduce-scatter.12.cloned.1.call-update) | async-done | bytes 663568 | tf_op jit(solution)/shard_map/reduce_scatter | solution.py:451
  1329.8 109.3 %reduce-scatter.16.cloned.1.call-done = f32[144,2304]{1,0:T(8,128)} async-done(((f32[1152,2304]{1,0:T(8,128)}), f32[144,2304]{1,0:T(8,128)}) %reduce-scatter.16.cloned.1.call-update) | async-done | bytes 1327120 | tf_op jit(solution)/shard_map/reduce_scatter | solution.py:453
  1441.3 159.2 %reduce-scatter.24.cloned.1.call-done = f32[144,3456]{1,0:T(8,128)} async-done(((f32[1152,3456]{1,0:T(8,128)}), f32[144,3456]{1,0:T(8,128)}) %reduce-scatter.24.cloned.1.call-update) | async-done | bytes 1990672 | tf_op jit(solution)/shard_map/reduce_scatter | solution.py:457
  1603.2 158.9 %reduce-scatter.10.cloned.1.call-done = f32[144,3456]{1,0:T(8,128)} async-done(((f32[1152,3456]{1,0:T(8,128)}), f32[144,3456]{1,0:T(8,128)}) %reduce-scatter.10.cloned.1.call-update) | async-done | bytes 1990672 | tf_op jit(solution)/shard_map/reduce_scatter | solution.py:450
  1764.7 208.3 %reduce-scatter.22.cloned.1.call-done = f32[576,1152]{1,0:T(8,128)} async-done(((f32[4608,1152]{1,0:T(8,128)}), f32[576,1152]{1,0:T(8,128)}) %reduce-scatter.22.cloned.1.call-update) | async-done | bytes 2654224 | tf_op jit(solution)/shard_map/reduce_scatter | solution.py:456
  1975.9 208.0 %reduce-scatter.20.cloned.1.call-done = f32[144,4608]{1,0:T(8,128)} async-done(((f32[1152,4608]{1,0:T(8,128)}), f32[144,4608]{1,0:T(8,128)}) %reduce-scatter.20.cloned.1.call-update) | async-done | bytes 2654224 | tf_op jit(solution)/shard_map/reduce_scatter | solution.py:455
  2200.4 193.2 %all-reduce.29.cloned.1.call-done = (bf16[144,6912]{1,0:T(8,128)(2,1)}, bf16[144,3456]{1,0:T(8,128)(2,1)}, bf16[144,1152]{1,0:T(8,128)(2,1)}, bf16[512,1152]{1,0...) async-done(((bf16[144,6912]{1,0:T(8,128)(2,1)}, ...) | async-done | bytes 9805840 | tf_op jit(solution)/shard_map/psum | solution.py:480
  (461 shorter events, 427.9 us)
Async XLA Ops:
  7.2 74.5 %all-reduce.25.cloned.1.call-start = ((), (), s32[]{:S(2)}) async-start(), calls=%async_computation.13 | async-start | bytes 221184 | tf_op jit(solution)/shard_map/psum | solution.py:166
  10.2 158.3 %all-gather.11.cloned.1.call-start = ((), (), s32[]{:S(2)}) async-start(), calls=%async_computation.14 | async-start | bytes 8957952 | tf_op jit(solution)/shard_map/all_gather | solution.py:192
  11.0 201.1 %all-gather.13.cloned.1.call-start = ((), (), s32[]{:S(2)}) async-start(), calls=%async_computation.15 | async-start | bytes 2985984 | tf_op jit(solution)/shard_map/all_gather | solution.py:193
  11.7 226.5 %all-gather.19.cloned.1.call-start = ((), (), s32[]{:S(2)}) async-start(), calls=%async_computation.18 | async-start | bytes 2985984 | tf_op jit(solution)/shard_map/all_gather | solution.py:195
  12.4 316.5 %all-gather.15.cloned.1.call-start = ((), (), s32[]{:S(2)}) async-start(), calls=%async_computation.16 | async-start | bytes 10616832 | tf_op jit(solution)/shard_map/all_gather | solution.py:167
  13.0 372.9 %all-gather.17.cloned.1.call-start = ((), (), s32[]{:S(2)}) async-start(), calls=%async_computation.17 | async-start | bytes 5971968 | tf_op jit(solution)/shard_map/all_gather | solution.py:196
  13.6 407.3 %all-gather.21.cloned.1.call-start = ((), (), s32[]{:S(2)}) async-start(), calls=%async_computation.19 | async-start | bytes 2985984 | tf_op jit(solution)/shard_map/all_gather | solution.py:197
  14.3 507.1 %all-gather.23.cloned.1.call-start = ((), (), s32[]{:S(2)}) async-start(), calls=%async_computation.20 | async-start | bytes 11943936 | tf_op jit(solution)/shard_map/all_gather | solution.py:199
  15.1 607.0 %all-gather.25.cloned.1.call-start = ((), (), s32[]{:S(2)}) async-start(), calls=%async_computation.21 | async-start | bytes 11943936 | tf_op jit(solution)/shard_map/all_gather | solution.py:201
  15.8 648.8 %all-gather.29.cloned.1.call-start = ((), (), s32[]{:S(2)}) async-start(), calls=%async_computation.23 | async-start | bytes 2985984 | tf_op jit(solution)/shard_map/all_gather | solution.py:206
  68.6 581.4 %all-to-all-start.2 = ((bf16[8,2,36864]{2,1,0:T(2,128)(2,1)}), bf16[8,2,36864]{2,1,0:T(2,128)(2,1)}, u32[]{:S(2)}, u32[]{:S(2)}) async-start(bf16[8,2,36864]{2,1,0:T(2,128)(2,1)} %reshape.822), calls=%async_computation.2 | async-start | bytes 2359296 | tf_op jit(solution)/shard_map/all_to_all | solution.py:285
  76.3 673.3 %all-gather.27.cloned.1.call-start = ((), (), s32[]{:S(2)}) async-start(), calls=%async_computation.22 | async-start | bytes 8957952 | tf_op jit(solution)/shard_map/all_gather | solution.py:205
  80.2 313.3 %copy-start.79 = (pred[120]{0:T(512)(128)(4,1)}, pred[120]{0:T(512)(128)(4,1)S(1)}, u32[]{:S(2)}) copy-start(pred[120]{0:T(512)(128)(4,1)S(1)} %iota_compare_fusion.1) | copy-start | bytes 364
  82.7 338.2 %copy-start.45 = (f32[1152]{0:T(1024)}, f32[1152]{0:T(1024)S(1)}, u32[]{:S(2)}) copy-start(f32[1152]{0:T(1024)S(1)} %get-tuple-element.38) | copy-start | bytes 13828
  82.7 438.8 %copy-start.86 = (f32[1152]{0:T(1024)}, f32[1152]{0:T(1024)S(1)}, u32[]{:S(2)}) copy-start(f32[1152]{0:T(1024)S(1)} %get-tuple-element.39) | copy-start | bytes 13828
  82.7 836.0 %copy-start.63 = (f32[1152]{0:T(1024)}, f32[1152]{0:T(1024)S(1)}, u32[]{:S(2)}) copy-start(f32[1152]{0:T(1024)S(1)} %get-tuple-element.35) | copy-start | bytes 13828
  425.6 493.1 %copy-start.73 = (f32[512]{0:T(512)}, f32[512]{0:T(512)S(1)}, u32[]{:S(2)}) copy-start(f32[512]{0:T(512)S(1)} %broadcast_multiply_fusion.4) | copy-start | bytes 6148
  427.3 491.4 %copy-start.84 = (f32[512]{0:T(512)}, f32[512]{0:T(512)S(1)}, u32[]{:S(2)}) copy-start(f32[512]{0:T(512)S(1)} %fusion.90) | copy-start | bytes 6148
  650.0 58.1 %all-to-all-start = ((bf16[8,2,36864]{2,1,0:T(2,128)(2,1)}), bf16[8,2,36864]{2,1,0:T(2,128)(2,1)S(1)}, u32[]{:S(2)}, u32[]{:S(2)}) async-start(bf16[8,2,36864]{2,1,0:T(2,128)(2,1)} %reshape.820), calls=%async_computation | async-start | bytes 2359296 | tf_op jit(solution)/shard_map/all_to_all | solution.py:256
  811.4 39.0 %all-to-all-start.1 = ((bf16[8,64,1152]{2,1,0:T(8,128)(2,1)}), bf16[8,64,1152]{2,1,0:T(8,128)(2,1)}, u32[]{:S(2)}, u32[]{:S(2)}) async-start(bf16[8,64,1152]{2,1,0:T(8,128)(2,1)} %fusion.19), calls=%async_computation.1 | async-start | bytes 2359296 | tf_op jit(solution)/shard_map/all_to_all | solution.py:278
  850.5 32.1 %all-to-all-start.3 = ((bf16[8,64,1152]{2,1,0:T(8,128)(2,1)}), bf16[8,64,1152]{2,1,0:T(8,128)(2,1)}, u32[]{:S(2)}, u32[]{:S(2)}) async-start(bf16[8,64,1152]{2,1,0:T(8,128)(2,1)} %add_convert_fusion.2), calls=%async_computation.3 | async-start | bytes 2359296 | tf_op jit(solution)/shard_map/all_to_all | solution.py:321
  855.7 332.1 %all-reduce.27.cloned.1.call-start = ((), (), s32[]{:S(2)}) async-start(), calls=%async_computation.24 | async-start | bytes 221184 | tf_op jit(solution)/shard_map/psum | solution.py:425
  996.4 195.5 %reduce-scatter.26.cloned.1.call-start = ((), (), s32[]{:S(2)}) async-start(), calls=%async_computation.33 | async-start | bytes 5971968 | tf_op jit(solution)/shard_map/reduce_scatter | solution.py:458
  1002.1 204.3 %reduce-scatter.18.cloned.1.call-start = ((), (), s32[]{:S(2)}) async-start(), calls=%async_computation.29 | async-start | bytes 5971968 | tf_op jit(solution)/shard_map/reduce_scatter | solution.py:454
  1008.6 258.2 %reduce-scatter.14.cloned.1.call-start = ((), (), s32[]{:S(2)}) async-start(), calls=%async_computation.27 | async-start | bytes 5971968 | tf_op jit(solution)/shard_map/reduce_scatter | solution.py:452
  1014.5 313.4 %reduce-scatter.12.cloned.1.call-start = ((), (), s32[]{:S(2)}) async-start(), calls=%async_computation.26 | async-start | bytes 5971968 | tf_op jit(solution)/shard_map/reduce_scatter | solution.py:451
  1020.2 418.9 %reduce-scatter.16.cloned.1.call-start = ((), (), s32[]{:S(2)}) async-start(), calls=%async_computation.28 | async-start | bytes 11943936 | tf_op jit(solution)/shard_map/reduce_scatter | solution.py:453
  1032.2 568.4 %reduce-scatter.24.cloned.1.call-start = ((), (), s32[]{:S(2)}) async-start(), calls=%async_computation.32 | async-start | bytes 17915904 | tf_op jit(solution)/shard_map/reduce_scatter | solution.py:457
  1043.3 718.7 %reduce-scatter.10.cloned.1.call-start = ((), (), s32[]{:S(2)}) async-start(), calls=%async_computation.25 | async-start | bytes 17915904 | tf_op jit(solution)/shard_map/reduce_scatter | solution.py:450
  1054.5 918.5 %reduce-scatter.22.cloned.1.call-start = ((), (), s32[]{:S(2)}) async-start(), calls=%async_computation.31 | async-start | bytes 23887872 | tf_op jit(solution)/shard_map/reduce_scatter | solution.py:456
  1070.0 1113.9 %reduce-scatter.20.cloned.1.call-start = ((), (), s32[]{:S(2)}) async-start(), calls=%async_computation.30 | async-start | bytes 23887872 | tf_op jit(solution)/shard_map/reduce_scatter | solution.py:455
  1083.6 1310.1 %all-reduce.29.cloned.1.call-start = ((), (), s32[]{:S(2)}) async-start(), calls=%async_computation.34 | async-start | bytes 19611648 | tf_op jit(solution)/shard_map/psum | solution.py:480
  (98 other events, 1513.9 us)
Sparse Core Ops, SparseCore 0:
  10.9 52.6 all-reduce.24
  65.4 103.1 all-gather.10
  170.3 33.0 all-gather.12
  205.0 33.1 all-gather.18
  239.8 89.0 all-gather.14
  330.5 55.3 all-gather.16
  387.6 33.2 all-gather.20
  422.6 98.7 all-gather.22
  523.2 98.8 all-gather.24
  623.7 33.2 all-gather.28
  658.7 90.8 all-gather.26
  996.5 52.1 all-reduce.26
  1051.0 68.8 reduce-scatter.25
  1122.0 84.2 reduce-scatter.17
  1208.5 58.3 reduce-scatter.13
  1269.0 58.8 reduce-scatter.11
  1330.1 108.9 reduce-scatter.15
  1441.4 159.0 reduce-scatter.23
  1602.9 159.0 reduce-scatter.9
  1764.4 208.5 reduce-scatter.21
  1975.3 208.5 reduce-scatter.19
  2192.3 201.3 all-reduce.28
where the time goes:
time: 2430 us; the launch traced here: 2420 us
  waiting for transfers between devices  1720 us (71%)
  matrix products  303 us (12%)
  other arithmetic  132 us (5%)
  blocking collectives  125 us (5%)
  local copies, waits for them, and re-layouts  93.5 us (4%)
  starting transfers between devices  28.3 us (1%)
    reduce_scatter x1, waiting for transfers between devices, on_device(): lax.psum_scatter(part_red, 'frame', scatter_dimension=0, tiled=True)  208 us
    reduce_scatter x1, waiting for transfers between devices, on_device(): lax.psum_scatter(part_exp, 'frame', scatter_dimension=0, tiled=True)  208 us
    psum x1, waiting for transfers between devices, on_device(): lax.psum(back_modulation_weight.astype(jnp.bfloat16), 'clip')  193 us
    reduce_scatter x1, waiting for transfers between devices, on_device(): lax.psum_scatter(part_tin, 'frame', scatter_dimension=0, tiled=True)  159 us
    reduce_scatter x1, waiting for transfers between devices, on_device(): lax.psum_scatter(part_sin, 'frame', scatter_dimension=0, tiled=True)  159 us
    unnamed x2, blocking collectives  118 us
    reduce_scatter x1, waiting for transfers between devices, on_device(): lax.psum_scatter(part_cmem, 'frame', scatter_dimension=0, tiled=True)  109 us
    all_gather x1, waiting for transfers between devices, on_device(): lax.all_gather(expand_weight, 'frame', axis=0, tiled=True)  94.1 us
  transfers between devices with their start and end apart: 26, of which 19 were waited for; matrix products, arithmetic and copies ran while one was open for 13% of the time, Pallas kernels for 0%

commit v1 on v0

--- a/solution.py
+++ b/solution.py
@@ -1,8 +1,11 @@
+import functools
 import math
 
 import jax
 import jax.numpy as jnp
 from jax import lax
+from jax.experimental import pallas as pl
+from jax.experimental.pallas import tpu as pltpu
 from jax.sharding import PartitionSpec as P
 
 HEADS = 16
@@ -100,6 +103,501 @@
         * att_scale
     )
     return (back_queries, back_keys, back_values)
+
+
+MESH_ID = pl.DeviceIdType.MESH
+LANES = 128
+PIECE_SLOTS = 4
+
+
+def neighbours():
+    column = lax.axis_index("clip")
+    frame = lax.axis_index("frame")
+    depth = frame // 2
+    core = frame % 2
+    across_x = column + 1 - 2 * (column % 2)
+    across_y = column + 2 - 4 * (column // 2)
+    sibling = frame + 1 - 2 * core
+    return column, frame, depth, core, across_x, across_y, sibling
+
+
+def greet(peers):
+    barrier = pltpu.get_barrier_semaphore()
+    for peer in peers:
+        pl.semaphore_signal(barrier, inc=1, device_id=peer, device_id_type=MESH_ID)
+    pl.semaphore_wait(barrier, len(peers))
+
+
+class Copies:
+    def __init__(self, send_sems, recv_sems):
+        self.send_sems, self.recv_sems, self.count, self.started = send_sems, recv_sems, 0, []
+
+    def start(self, source, target, device):
+        copy = pltpu.make_async_remote_copy(
+            src_ref=source,
+            dst_ref=target,
+            send_sem=self.send_sems.at[self.count],
+            recv_sem=self.recv_sems.at[self.count],
+            device_id=device,
+            device_id_type=MESH_ID,
+        )
+        self.count += 1
+        copy.start()
+        self.started.append(copy)
+        return copy
+
+    def finish(self):
+        for copy in self.started:
+            copy.wait_send()
+
+
+def rows_at(ref, start, size, step):
+    return ref.at[pl.ds(pl.multiple_of(start, step), size), :]
+
+
+def whole_unit(ref, tall, unit, frame):
+    if tall:
+        height = ref.shape[0] // 32
+        return rows_at(ref, frame * (4 * height) + unit * height, height, height)
+    height, width = ref.shape[0] // 8, ref.shape[1] // 4
+    return ref.at[
+        pl.ds(pl.multiple_of(frame * height, height), height),
+        pl.ds(pl.multiple_of(unit * width, LANES), width),
+    ]
+
+
+def whole_share(ref, tall, frame):
+    height = ref.shape[0] // 8
+    return rows_at(ref, frame * height, height, height)
+
+
+def share_unit(ref, tall, unit):
+    if tall:
+        height = ref.shape[0] // 4
+        return rows_at(ref, unit * height, height, height)
+    width = ref.shape[1] // 4
+    return ref.at[:, pl.ds(pl.multiple_of(unit * width, LANES), width)]
+
+
+def gather_kernel(talls, *refs):
+    count = len(talls)
+    shares, (vec_in, mod_in, cot_in) = refs[:count], refs[count : count + 3]
+    wholes, (vec_out, mod_out, cot_out) = (
+        refs[count + 3 : 2 * count + 3],
+        refs[2 * count + 3 : 2 * count + 6],
+    )
+    send_sems, recv_sems, local_sems = refs[2 * count + 6 :]
+    column, frame, depth, core, across_x, across_y, sibling = neighbours()
+    frame_peers = [(column, (frame + shift) % 8) for shift in range(1, 8)]
+    greet(frame_peers + [(across_x, frame), (across_y, frame)])
+    copies = Copies(send_sems, recv_sems)
+    locals_started = []
+
+    def local(source, target):
+        copy = pltpu.make_async_copy(source, target, local_sems.at[len(locals_started)])
+        copy.start()
+        locals_started.append(copy)
+
+    arrivals = []
+    local(vec_in, vec_out.at[frame])
+    local(mod_in.at[frame], mod_out.at[frame])
+    for peer in frame_peers:
+        arrivals.append(copies.start(vec_in, vec_out.at[frame], peer))
+        arrivals.append(copies.start(mod_in.at[peer[1]], mod_out.at[frame], peer))
+    from_depth = []
+    for share, whole, tall in zip(shares, wholes, talls):
+        own = whole_share(whole, tall, frame)
+        local(share, own)
+        from_depth.append(
+            [
+                copies.start(
+                    share_unit(share, tall, column),
+                    whole_unit(whole, tall, column, frame),
+                    (column, ((depth + shift) % 4) * 2 + core),
+                )
+                for shift in range(1, 4)
+            ]
+        )
+        arrivals.append(copies.start(share, own, (column, sibling)))
+    local(cot_in.at[frame], cot_out.at[frame])
+    for peer in frame_peers:
+        arrivals.append(copies.start(cot_in.at[peer[1]], cot_out.at[frame], peer))
+
+    from_x, from_y, from_far = {}, {}, {}
+
+    def pass_on(index, shift, unit, device):
+        source = ((depth + 4 - shift) % 4) * 2 + core
+        piece = whole_unit(wholes[index], talls[index], unit, source)
+        return copies.start(piece, piece, device)
+
+    def first(index):
+        for shift in range(1, 4):
+            from_depth[index][shift - 1].wait_recv()
+            from_x[index, shift] = pass_on(index, shift, column, (across_x, frame))
+            from_y[index, shift] = pass_on(index, shift, column, (across_y, frame))
+            arrivals.append(pass_on(index, shift, column, (column, sibling)))
+
+    def second(index):
+        for shift in range(1, 4):
+            x_first = (index + shift) % 2 == 0
+            from_x[index, shift].wait_recv()
+            if x_first:
+                from_far[index, shift] = pass_on(index, shift, across_x, (across_y, frame))
+            arrivals.append(pass_on(index, shift, across_x, (column, sibling)))
+            from_y[index, shift].wait_recv()
+            if not x_first:
+                from_far[index, shift] = pass_on(index, shift, across_y, (across_x, frame))
+            arrivals.append(pass_on(index, shift, across_y, (column, sibling)))
+
+    def third(index):
+        for shift in range(1, 4):
+            from_far[index, shift].wait_recv()
+            arrivals.append(pass_on(index, shift, 3 - column, (column, sibling)))
+
+    for step in range(count + 2):
+        if step < count:
+            first(step)
+        if 0 <= step - 1 < count:
+            second(step - 1)
+        if 0 <= step - 2:
+            third(step - 2)
+    for copy in arrivals:
+        copy.wait_recv()
+    copies.finish()
+    for copy in locals_started:
+        copy.wait()
+
+
+def gather_all(shares, talls, vec, mod_rows, cot_rows):
+    if lax.axis_size("clip") != 4 or lax.axis_size("frame") != 8:
+        wholes = [lax.all_gather(share, "frame", axis=0, tiled=True) for share in shares]
+        vecs = lax.all_gather(vec, "frame", axis=0)
+        mods = lax.all_to_all(mod_rows, "frame", split_axis=0, concat_axis=0, tiled=True)
+        cots = lax.all_to_all(cot_rows, "frame", split_axis=0, concat_axis=0, tiled=True)
+        return wholes, vecs, mods, cots
+    count = len(shares)
+    anywhere = pl.BlockSpec(memory_space=pl.ANY)
+    out_shape = [
+        jax.ShapeDtypeStruct((8 * share.shape[0], share.shape[1]), share.dtype) for share in shares
+    ]
+    out_shape.append(jax.ShapeDtypeStruct((8,) + vec.shape, vec.dtype))
+    out_shape.append(jax.ShapeDtypeStruct(mod_rows.shape, mod_rows.dtype))
+    out_shape.append(jax.ShapeDtypeStruct(cot_rows.shape, cot_rows.dtype))
+    remote = 21 + count * 25
+    outs = pl.pallas_call(
+        functools.partial(gather_kernel, tuple(talls)),
+        out_shape=out_shape,
+        in_specs=[anywhere] * (count + 3),
+        out_specs=[anywhere] * (count + 3),
+        scratch_shapes=[
+            pltpu.SemaphoreType.DMA((remote,)),
+            pltpu.SemaphoreType.DMA((remote,)),
+            pltpu.SemaphoreType.DMA((count + 3,)),
+        ],
+        compiler_params=pltpu.CompilerParams(collective_id=0, has_side_effects=True),
+        name="gather_all",
+    )(*shares, vec, mod_rows, cot_rows)
+    return outs[:count], outs[count], outs[count + 1], outs[count + 2]
+
+
+def add_stream(count, left_at, right_at, out_at, left_buf, right_buf, out_buf, sems):
+    def loads(index):
+        slot = index % PIECE_SLOTS
+        return (
+            pltpu.make_async_copy(left_at(index), left_buf.at[slot], sems.at[0, slot]),
+            pltpu.make_async_copy(right_at(index), right_buf.at[slot], sems.at[1, slot]),
+        )
+
+    def store(index):
+        slot = index % PIECE_SLOTS
+        return pltpu.make_async_copy(out_buf.at[slot], out_at(index), sems.at[2, slot])
+
+    ahead = min(PIECE_SLOTS - 1, count)
+    for index in range(ahead):
+        for copy in loads(index):
+            copy.start()
+
+    def step(index, carry):
+        @pl.when(index + PIECE_SLOTS - 1 < count)
+        def _():
+            for copy in loads(index + PIECE_SLOTS - 1):
+                copy.start()
+
+        for copy in loads(index):
+            copy.wait()
+
+        @pl.when(index >= PIECE_SLOTS)
+        def _():
+            store(index - PIECE_SLOTS).wait()
+
+        slot = index % PIECE_SLOTS
+        out_buf[slot] = left_buf[slot] + right_buf[slot]
+        store(index).start()
+        return carry
+
+    lax.fori_loop(0, count, step, 0)
+    for index in range(max(0, count - PIECE_SLOTS), count):
+        store(index).wait()
+
+
+def reduce_kernel(plan, *refs):
+    bundles = len(plan)
+    refs = list(refs)
+    take = lambda number: [refs.pop(0) for _ in range(number)]
+    parts = [take(0 if tall else len(widths)) if not tall else take(1) for tall, widths in plan]
+    text_in, vec_in, mod_in = take(3)
+    outs = take(bundles)
+    text_out, vec_out, mod_out = take(3)
+    paired, halved, quartered, lined = take(bundles), take(bundles), take(bundles), take(bundles)
+    text_got, vec_got = take(2)
+    (
+        send_sems,
+        recv_sems,
+        local_sems,
+        stream_sems,
+        left_buf,
+        right_buf,
+        out_buf,
+        four_buf,
+        vec_buf,
+        vec_sum,
+    ) = refs
+    column, frame, depth, core, across_x, across_y, sibling = neighbours()
+    far = 3 - column
+    frame_peers = [(column, (frame + shift) % 8) for shift in range(1, 8)]
+    plane_peers = [(across_x, frame), (across_y, frame), (far, frame)]
+    greet(frame_peers + plane_peers)
+    copies = Copies(send_sems, recv_sems)
+
+    mod_own = pltpu.make_async_copy(mod_in, mod_out.at[column, frame], local_sems.at[0])
+    mod_own.start()
+    vec_own = pltpu.make_async_copy(vec_in.at[frame], vec_got.at[frame], local_sems.at[1])
+    vec_own.start()
+    vec_copies = [copies.start(vec_in.at[peer[1]], vec_got.at[frame], peer) for peer in frame_peers]
+    mod_copies = [copies.start(mod_in, mod_out.at[column, frame], peer) for peer in frame_peers]
+    text_rows = text_in.shape[0] // 4
+    text_copies = [
+        copies.start(
+            rows_at(text_in, peer[0] * text_rows, text_rows, text_rows), text_got.at[slot], peer
+        )
+        for slot, peer in enumerate(plane_peers)
+    ]
+
+    def part_piece(index, unit, owner):
+        tall, widths = plan[index]
+        if tall:
+            return whole_unit(parts[index][0], True, unit, owner)
+        height, width = parts[index][0].shape[0] // 8, paired[index].shape[-1]
+        for ref, units in zip(parts[index], widths):
+            if unit < units:
+                return ref.at[
+                    pl.ds(pl.multiple_of(owner * height, height), height),
+                    pl.ds(unit * width, width),
+                ]
+            unit -= units
+
+    from_core = {}
+    for index in range(bundles):
+        for slot in range(4):
+            owner = slot * 2 + 1 - core
+            for unit in range(4):
+                from_core[index, slot, unit] = copies.start(
+                    part_piece(index, unit, owner), paired[index].at[unit, slot], (column, sibling)
+                )
+
+    def stream(count, left_at, right_at, out_at):
+        add_stream(count, left_at, right_at, out_at, left_buf, right_buf, out_buf, stream_sems)
+
+    from_half, from_quarter, from_line, ends = {}, {}, {}, []
+
+    def pair(index):
+        for slot in range(4):
+            for unit in range(4):
+                from_core[index, slot, unit].wait_recv()
+        for unit in range(4):
+            stream(
+                4,
+                lambda slot: part_piece(index, unit, slot * 2 + core),
+                lambda slot: paired[index].at[unit, slot],
+                lambda slot: paired[index].at[unit, slot],
+            )
+        for slot in range(4):
+            near = across_x if slot < 2 else across_y
+            for which, unit in enumerate((near, far)):
+                from_half[index, slot, which] = copies.start(
+                    paired[index].at[unit, slot], halved[index].at[slot, which], (near, frame)
+                )
+
+    def half(index):
+        for slot in range(4):
+            for which in range(2):
+                from_half[index, slot, which].wait_recv()
+
+        def source(step):
+            slot, which = step // 2, step % 2
+            late = slot // 2
+            unit = column + which * (
+                (1 - late) * (across_y - column) + late * (across_x - column)
+            )
+            return paired[index].at[unit, slot]
+
+        place = lambda step: halved[index].at[step // 2, step % 2]
+        stream(8, source, place, place)
+        for slot in range(4):
+            near = across_y if slot < 2 else across_x
+            from_quarter[index, slot] = copies.start(
+                halved[index].at[slot, 1], quartered[index].at[slot], (near, frame)
+            )
+
+    def quarter(index):
+        for slot in range(4):
+            from_quarter[index, slot].wait_recv()
+        place = lambda slot: quartered[index].at[slot]
+        stream(4, lambda slot: halved[index].at[slot, 0], place, place)
+        for shift in range(1, 4):
+            other = (depth + shift) % 4
+            from_line[index, shift] = copies.start(
+                quartered[index].at[other], lined[index].at[shift - 1], (column, other * 2 + core)
+            )
+
+    def total_of_four(own, others, target, height):
+        loads = [
+            pltpu.make_async_copy(
+                source, four_buf.at[slot, pl.ds(0, height)], stream_sems.at[0, slot]
+            )
+            for slot, source in enumerate([own] + others)
+        ]
+        for copy in loads:
+            copy.start()
+        for copy in loads:
+            copy.wait()
+        total = four_buf[0, 0:height].astype(jnp.float32)
+        for slot in range(1, 4):
+            total = total + four_buf[slot, 0:height].astype(jnp.float32)
+        out_buf[0, 0:height] = total.astype(jnp.bfloat16)
+        copy = pltpu.make_async_copy(out_buf.at[0, pl.ds(0, height)], target, stream_sems.at[2, 0])
+        copy.start()
+        copy.wait()
+        for peer in plane_peers:
+            ends.append(copies.start(target, target, peer))
+
+    def line(index):
+        for shift in range(1, 4):
+            from_line[index, shift].wait_recv()
+        total_of_four(
+            quartered[index].at[depth],
+            [lined[index].at[slot] for slot in range(3)],
+            share_unit(outs[index], plan[index][0], column),
+            lined[index].shape[1],
+        )
+
+    def small():
+        for copy in vec_copies + mod_copies + text_copies:
+            copy.wait_recv()
+        mod_own.wait()
+        vec_own.wait()
+        for peer in plane_peers:
+            ends.append(copies.start(mod_out.at[column], mod_out.at[column], peer))
+        load = pltpu.make_async_copy(vec_got, vec_buf, local_sems.at[0])
+        load.start()
+        load.wait()
+        vec_sum[...] = jnp.sum(vec_buf[...], axis=0)
+        keep = pltpu.make_async_copy(vec_sum, vec_out.at[column], local_sems.at[1])
+        keep.start()
+        keep.wait()
+        for peer in plane_peers:
+            ends.append(copies.start(vec_out.at[column], vec_out.at[column], peer))
+        total_of_four(
+            rows_at(text_in, column * text_rows, text_rows, text_rows),
+            [text_got.at[slot] for slot in range(3)],
+            rows_at(text_out, column * text_rows, text_rows, text_rows),
+            text_rows,
+        )
+
+    for step in range(bundles + 3):
+        if step < bundles:
+            pair(step)
+        if 0 <= step - 1 < bundles:
+            half(step - 1)
+        if 0 <= step - 2 < bundles:
+            quarter(step - 2)
+        if 0 <= step - 3:
+            line(step - 3)
+        if step == 1:
+            small()
+    for copy in ends:
+        copy.wait_recv()
+    copies.finish()
+
+
+def reduce_all(parts, talls, text_part, vec_parts, mod_row):
+    if lax.axis_size("clip") != 4 or lax.axis_size("frame") != 8:
+
+        def total(part):
+            share = lax.psum_scatter(part, "frame", scatter_dimension=0, tiled=True)
+            return lax.psum(share, "clip")
+
+        outs = [
+            jnp.concatenate([total(part) for part in group], axis=1) for group in parts
+        ]
+        text = lax.psum(text_part, "clip")
+        vec = lax.psum_scatter(vec_parts, "frame", scatter_dimension=0, tiled=True)
+        vec = lax.all_gather(vec[0], "clip", axis=0)
+        mods = lax.all_gather(lax.all_gather(mod_row, "frame", axis=0), "clip", axis=0)
+        return outs, text, vec, mods
+    anywhere = pl.BlockSpec(memory_space=pl.ANY)
+    plan, out_shape, landing = [], [], [[], [], [], []]
+    height = width = 0
+    for group, tall in zip(parts, talls):
+        rows = group[0].shape[0]
+        wide = sum(part.shape[1] for part in group)
+        height, width = (rows // 32, wide) if tall else (rows // 8, wide // 4)
+        plan.append((tall, tuple(part.shape[1] // width for part in group)))
+        out_shape.append(jax.ShapeDtypeStruct((rows // 8, wide), jnp.bfloat16))
+        for place, lead in zip(landing, ((4, 4), (4, 2), (4,), (3,))):
+            place.append(jax.ShapeDtypeStruct(lead + (height, width), jnp.bfloat16))
+    out_shape.append(jax.ShapeDtypeStruct(text_part.shape, jnp.bfloat16))
+    out_shape.append(jax.ShapeDtypeStruct((4,) + vec_parts.shape[1:], jnp.float32))
+    out_shape.append(jax.ShapeDtypeStruct((4, 8) + mod_row.shape, jnp.float32))
+    for place in landing:
+        out_shape.extend(place)
+    out_shape.append(
+        jax.ShapeDtypeStruct((3, text_part.shape[0] // 4, text_part.shape[1]), jnp.bfloat16)
+    )
+    out_shape.append(jax.ShapeDtypeStruct(vec_parts.shape, jnp.float32))
+    operands = [part for group in parts for part in group] + [text_part, vec_parts, mod_row]
+    bundles = len(plan)
+    remote = bundles * (16 + 8 + 4 + 3 + 3) + 7 + 7 + 3 + 3 + 3 + 3
+    piece = (PIECE_SLOTS, height, width)
+    outs = pl.pallas_call(
+        functools.partial(reduce_kernel, tuple(plan)),
+        out_shape=out_shape,
+        in_specs=[anywhere] * len(operands),
+        out_specs=[anywhere] * len(out_shape),
+        scratch_shapes=[
+            pltpu.SemaphoreType.DMA((remote,)),
+            pltpu.SemaphoreType.DMA((remote,)),
+            pltpu.SemaphoreType.DMA((2,)),
+            pltpu.SemaphoreType.DMA((3, PIECE_SLOTS)),
+            pltpu.VMEM(piece, jnp.bfloat16),
+            pltpu.VMEM(piece, jnp.bfloat16),
+            pltpu.VMEM(piece, jnp.bfloat16),
+            pltpu.VMEM((4, height, width), jnp.bfloat16),
+            pltpu.VMEM(vec_parts.shape, jnp.float32),
+            pltpu.VMEM(vec_parts.shape[1:], jnp.float32),
+        ],
+        compiler_params=pltpu.CompilerParams(
+            collective_id=1, has_side_effects=True, vmem_limit_bytes=32 * 1024 * 1024
+        ),
+        name="reduce_all",
+    )(*operands)
+    return outs[:bundles], outs[bundles], outs[bundles + 1], outs[bundles + 2]
+
+
+def pack_rows(parts, rows):
+    flat = jnp.concatenate(parts, axis=-1)
+    flat = jnp.pad(flat, [(0, 0)] * (flat.ndim - 1) + [(0, rows * LANES - flat.shape[-1])])
+    return flat.reshape(flat.shape[:-1] + (rows, LANES))
 
 
 def on_device(
@@ -161,52 +659,64 @@
         + bias_placed[None, :]
     )
     share_rows = text_projection.shape[0]
-    text_share = lax.dynamic_slice_in_dim(text_tokens[0], frame_index * share_rows, share_rows, 2)
+    text_share = lax.dynamic_slice_in_dim(
+        text_tokens[0], frame_index * text_projection.shape[0], text_projection.shape[0], 2
+    )
     own_text = lax.dynamic_index_in_dim(text_tokens[0], own_clip, 0, keepdims=False)
-    modulation = lax.psum(modulation_part, "frame")
-    projection = lax.all_gather(text_projection, "frame", axis=0, tiled=True)
+    vectors = (
+        spatial_bias,
+        cross_bias,
+        expand_bias,
+        reduce_bias,
+        temporal_gain,
+        temporal_shift,
+        temporal_bias,
+        temporal_gate,
+    )
+    vector_sizes = [vector.shape[0] for vector in vectors]
+    vector_rows = -(-sum(vector_sizes) // (8 * LANES)) * 8
+    packed_vectors = pack_rows([vector.astype(jnp.float32) for vector in vectors], vector_rows)
+    mod_rows_high = -(-(6 * model_width) // (8 * LANES)) * 8
+    frame_onehot = (clip_ids[:, None] == slot_ids[None, :]).astype(jnp.float32)
+    frame_modulation = jnp.sum(frame_onehot[:, :, None] * modulation_part[None], axis=1)
+    talls = (True, False, False, False, True, False)
+    wholes, vecs, mods, cot_columns = gather_all(
+        (
+            text_projection,
+            jnp.concatenate([spatial_input, spatial_output], axis=1),
+            jnp.concatenate([cross_query, cross_memory, cross_output], axis=1),
+            expand_weight,
+            reduce_weight,
+            jnp.concatenate([temporal_input, temporal_output], axis=1),
+        ),
+        talls,
+        packed_vectors,
+        pack_rows([frame_modulation], mod_rows_high),
+        cotangent[0, 0].reshape(frame_count, patch_count // frame_count, model_width),
+    )
+    projection, whole_spatial, whole_text, whole_expand, whole_reduce, whole_time = wholes
     context = jnp.dot(own_text, projection, preferred_element_type=jnp.float32)
-    own_modulation = lax.dynamic_index_in_dim(modulation, own_clip, 0, keepdims=False)
+    own_modulation = jnp.sum(mods, axis=0).reshape(-1)[: 6 * model_width]
     shift_attend, scale_attend, gate_attend, shift_feed, scale_feed, gate_feed = jnp.split(
         own_modulation, 6
     )
+    vecs = vecs.reshape(frame_count, -1)[:, : sum(vector_sizes)]
+    vector_ends = [sum(vector_sizes[: index + 1]) for index in range(len(vector_sizes) - 1)]
     (
-        whole_input,
-        whole_output,
         whole_bias,
-        whole_query,
-        whole_memory,
-        whole_cross,
         whole_cross_bias,
-        whole_expand,
         whole_expand_bias,
-        whole_reduce,
         whole_reduce_bias,
         whole_gain,
         whole_shift,
-        whole_temporal,
-        whole_temporal_out,
         whole_temporal_bias,
         whole_gate,
-    ) = (
-        lax.all_gather(spatial_input, "frame", axis=0, tiled=True),
-        lax.all_gather(spatial_output, "frame", axis=0, tiled=True),
-        lax.all_gather(spatial_bias, "frame", axis=0, tiled=True),
-        lax.all_gather(cross_query, "frame", axis=0, tiled=True),
-        lax.all_gather(cross_memory, "frame", axis=0, tiled=True),
-        lax.all_gather(cross_output, "frame", axis=0, tiled=True),
-        lax.all_gather(cross_bias, "frame", axis=0, tiled=True),
-        lax.all_gather(expand_weight, "frame", axis=0, tiled=True),
-        lax.all_gather(expand_bias, "frame", axis=0, tiled=True),
-        lax.all_gather(reduce_weight, "frame", axis=0, tiled=True),
-        lax.all_gather(reduce_bias, "frame", axis=0, tiled=True),
-        lax.all_gather(temporal_gain, "frame", axis=0, tiled=True),
-        lax.all_gather(temporal_shift, "frame", axis=0, tiled=True),
-        lax.all_gather(temporal_input, "frame", axis=0, tiled=True),
-        lax.all_gather(temporal_output, "frame", axis=0, tiled=True),
-        lax.all_gather(temporal_bias, "frame", axis=0, tiled=True),
-        lax.all_gather(temporal_gate, "frame", axis=0, tiled=True),
-    )
+    ) = [part.reshape(-1) for part in jnp.split(vecs, vector_ends, axis=1)]
+    whole_input, whole_output = whole_spatial[:, : 3 * model_width], whole_spatial[:, 3 * model_width :]
+    whole_query = whole_text[:, :model_width]
+    whole_memory = whole_text[:, model_width : 3 * model_width]
+    whole_cross = whole_text[:, 3 * model_width :]
+    whole_temporal, whole_temporal_out = whole_time[:, : 3 * model_width], whole_time[:, 3 * model_width :]
     tokens = latents[0, 0].astype(jnp.float32)
     normed_attend = modulate(tokens, shift_attend, scale_attend).astype(jnp.bfloat16)
     spatial_heads = jnp.dot(normed_attend, whole_input, preferred_element_type=jnp.float32).astype(
@@ -275,14 +785,12 @@
     result = result + whole_temporal_bias.astype(jnp.float32)
     result_low = result.astype(jnp.bfloat16)
     kept_state = (normed_time, time_heads, time_low, time_logsum)
-    returned = lax.all_to_all(result_low, "frame", split_axis=0, concat_axis=1, tiled=True)
-    temporal_value = returned[0].astype(jnp.float32)
     gate_keep = whole_gate.astype(jnp.float32) * own_keep
-    block_output = (after_feed + gate_keep * temporal_value).astype(jnp.bfloat16)[None, None]
     upstream = cotangent[0, 0].astype(jnp.float32)
-    back_gate = jnp.sum(upstream * temporal_value, axis=0) * own_keep
-    back_sent = (upstream * gate_keep).astype(jnp.bfloat16)
-    back_columns = lax.all_to_all(back_sent[None], "frame", split_axis=1, concat_axis=0, tiled=True)
+    keep_frames = 1.0 - jnp.sum(frame_onehot * motion_free[0].astype(jnp.float32)[None, :], axis=1)
+    back_columns = (
+        cot_columns.astype(jnp.float32) * (keep_frames[:, None, None] * whole_gate[None, None, :])
+    ).astype(jnp.bfloat16)
     normed_time, time_heads, time_low, time_logsum = kept_state
     frames_here, positions = (columns.shape[0], columns.shape[1])
     back_temporal_bias = jnp.sum(back_columns.astype(jnp.float32), axis=(0, 1))
@@ -318,9 +826,20 @@
         affine_norm, columns.astype(jnp.float32), gain_float, shift_float
     )
     back_inputs, back_gain, back_shift = norm_back(back_normed)
-    back_return = lax.all_to_all(
-        back_inputs.astype(jnp.bfloat16), "frame", split_axis=0, concat_axis=1, tiled=True
-    )
+    returned, back_return = jnp.split(
+        lax.all_to_all(
+            jnp.concatenate([result_low, back_inputs.astype(jnp.bfloat16)], axis=2),
+            "frame",
+            split_axis=0,
+            concat_axis=1,
+            tiled=True,
+        ),
+        2,
+        axis=2,
+    )
+    temporal_value = returned[0].astype(jnp.float32)
+    block_output = (after_feed + gate_keep * temporal_value).astype(jnp.bfloat16)[None, None]
+    back_gate = jnp.sum(upstream * temporal_value, axis=0) * own_keep
     back_feed_total = upstream + back_return[0].astype(jnp.float32)
     back_gate_feed = jnp.sum(back_feed_total * branch_feed, axis=0)
     back_branch_feed = (back_feed_total * gate_feed).astype(jnp.bfloat16)
@@ -420,75 +939,71 @@
             back_gate_feed,
         ]
     )
-    modulation_terms = own_onehot[:, None] * back_modulation_row[None, :]
-    context_terms = own_onehot[:, None, None] * back_context[None]
-    modulation_total, context_total = lax.psum((modulation_terms, context_terms), "frame")
-    back_modulation_weight = jnp.dot(
-        cond_rows.astype(jnp.float32).T, modulation_total, precision=lax.Precision.HIGHEST
-    )
-    back_modulation_bias = lax.dynamic_slice_in_dim(
-        jnp.sum(modulation_total, axis=0), frame_index * bias_width, bias_width, 0
-    )
+    own_conditioning = jnp.sum(own_onehot[:, None] * conditioning.astype(jnp.float32), axis=0)
+    all_context = lax.all_gather(back_context.astype(jnp.bfloat16), "frame", axis=0)
+    context_total = jnp.einsum("fs,ftd->std", frame_onehot, all_context.astype(jnp.float32))
     back_text_projection = jnp.einsum(
         "stk,std->kd",
         text_share,
         context_total.astype(jnp.bfloat16),
         preferred_element_type=jnp.float32,
     )
-    part_sin, part_sout, part_cq, part_cmem, part_cout, part_exp, part_red, part_tin, part_tout = (
-        back_spatial_input,
-        back_spatial_output,
-        back_cross_query,
-        back_cross_memory,
-        back_cross_output,
-        back_expand,
-        back_reduce,
-        back_temporal,
-        back_temporal_out,
-    )
-    shares = (
-        lax.psum_scatter(part_sin, "frame", scatter_dimension=0, tiled=True),
-        lax.psum_scatter(part_sout, "frame", scatter_dimension=0, tiled=True),
-        lax.psum_scatter(part_cq, "frame", scatter_dimension=0, tiled=True),
-        lax.psum_scatter(part_cmem, "frame", scatter_dimension=0, tiled=True),
-        lax.psum_scatter(part_cout, "frame", scatter_dimension=0, tiled=True),
-        lax.psum_scatter(part_exp, "frame", scatter_dimension=0, tiled=True),
-        lax.psum_scatter(part_red, "frame", scatter_dimension=0, tiled=True),
-        lax.psum_scatter(part_tin, "frame", scatter_dimension=0, tiled=True),
-        lax.psum_scatter(part_tout, "frame", scatter_dimension=0, tiled=True),
-        lax.psum_scatter(back_spatial_bias, "frame", scatter_dimension=0, tiled=True),
-        lax.psum_scatter(back_cross_bias, "frame", scatter_dimension=0, tiled=True),
-        lax.psum_scatter(back_expand_bias, "frame", scatter_dimension=0, tiled=True),
-        lax.psum_scatter(back_reduce_bias, "frame", scatter_dimension=0, tiled=True),
-        lax.psum_scatter(back_gain, "frame", scatter_dimension=0, tiled=True),
-        lax.psum_scatter(back_shift, "frame", scatter_dimension=0, tiled=True),
-        lax.psum_scatter(back_temporal_bias, "frame", scatter_dimension=0, tiled=True),
-        lax.psum_scatter(back_gate, "frame", scatter_dimension=0, tiled=True),
+    back_vectors = (
+        back_spatial_bias,
+        back_cross_bias,
+        back_expand_bias,
+        back_reduce_bias,
+        back_gain,
+        back_shift,
+        back_temporal_bias,
+        back_gate,
+    )
+    vector_parts = pack_rows(
+        [vector.reshape(frame_count, -1) for vector in back_vectors], vector_rows
+    )
+    row_high = -(-(7 * model_width) // (8 * LANES)) * 8
+    row_parts = pack_rows([back_modulation_row, own_conditioning], row_high)
+    low = lambda part: part.astype(jnp.bfloat16)
+    totals, text_total, vec_totals, rows_all = reduce_all(
+        (
+            (low(back_temporal), low(back_temporal_out)),
+            (low(back_reduce),),
+            (low(back_expand),),
+            (low(back_cross_query), low(back_cross_memory), low(back_cross_output)),
+            (low(back_spatial_input), low(back_spatial_output)),
+        ),
+        (False, True, False, False, False),
+        low(back_text_projection),
+        vector_parts,
+        row_parts,
+    )
+    high = lambda part: part.astype(jnp.float32)
+    total_time, total_reduce, total_expand, total_text, total_spatial = totals
+    vec_total = jnp.sum(vec_totals, axis=0).reshape(-1)
+    vec_total = jnp.split(vec_total[: sum(vector_sizes)], vector_ends)
+    rows_all = rows_all.reshape(-1, row_high * LANES)
+    rows_gradient = rows_all[:, : 6 * model_width]
+    rows_condition = lax.dynamic_slice_in_dim(
+        rows_all, 6 * model_width + frame_index * row_count, row_count, 1
+    )
+    back_modulation_weight = jnp.einsum(
+        "nd,ne->de", rows_condition, rows_gradient, precision=lax.Precision.HIGHEST
+    )
+    back_modulation_bias = jnp.sum(
+        lax.dynamic_slice_in_dim(rows_gradient, frame_index * bias_width, bias_width, 1), axis=0
     )
     matrix_totals = (
-        lax.psum(shares[0].astype(jnp.bfloat16), "clip").astype(jnp.float32),
-        lax.psum(shares[1].astype(jnp.bfloat16), "clip").astype(jnp.float32),
-        lax.psum(shares[2].astype(jnp.bfloat16), "clip").astype(jnp.float32),
-        lax.psum(shares[3].astype(jnp.bfloat16), "clip").astype(jnp.float32),
-        lax.psum(shares[4].astype(jnp.bfloat16), "clip").astype(jnp.float32),
-        lax.psum(shares[5].astype(jnp.bfloat16), "clip").astype(jnp.float32),
-        lax.psum(shares[6].astype(jnp.bfloat16), "clip").astype(jnp.float32),
-        lax.psum(shares[7].astype(jnp.bfloat16), "clip").astype(jnp.float32),
-        lax.psum(shares[8].astype(jnp.bfloat16), "clip").astype(jnp.float32),
-    )
-    others = (
-        lax.psum(back_modulation_weight.astype(jnp.bfloat16), "clip").astype(jnp.float32),
-        lax.psum(back_modulation_bias.astype(jnp.bfloat16), "clip").astype(jnp.float32),
-        lax.psum(back_text_projection.astype(jnp.bfloat16), "clip").astype(jnp.float32),
-        lax.psum(shares[9].astype(jnp.bfloat16), "clip").astype(jnp.float32),
-        lax.psum(shares[10].astype(jnp.bfloat16), "clip").astype(jnp.float32),
-        lax.psum(shares[11].astype(jnp.bfloat16), "clip").astype(jnp.float32),
-        lax.psum(shares[12].astype(jnp.bfloat16), "clip").astype(jnp.float32),
-        lax.psum(shares[13].astype(jnp.bfloat16), "clip").astype(jnp.float32),
-        lax.psum(shares[14].astype(jnp.bfloat16), "clip").astype(jnp.float32),
-        lax.psum(shares[15].astype(jnp.bfloat16), "clip").astype(jnp.float32),
-        lax.psum(shares[16].astype(jnp.bfloat16), "clip").astype(jnp.float32),
-    )
+        high(total_spatial[:, : 3 * model_width]),
+        high(total_spatial[:, 3 * model_width :]),
+        high(total_text[:, :model_width]),
+        high(total_text[:, model_width : 3 * model_width]),
+        high(total_text[:, 3 * model_width :]),
+        high(total_expand),
+        high(total_reduce),
+        high(total_time[:, : 3 * model_width]),
+        high(total_time[:, 3 * model_width :]),
+    )
+    others = (back_modulation_weight, back_modulation_bias, high(text_total)) + tuple(vec_total)
     return (
         block_output,
         input_gradient,

time: 2430 us -> 1180 us (0.49)
  waiting for transfers between devices: 1720 us -> 54.6 us
  Pallas kernels: 0 us -> 613 us
  blocking collectives: 125 us -> 0 us
  other arithmetic: 132 us -> 90.8 us
  matrix products: 303 us -> 272 us
    reduce_scatter x9 -> x0, waiting for transfers between devices: 974 us -> none  [the longest x1 208 us: on_device(): lax.psum_scatter(part_red, 'frame', scatter_dimension=0, tiled=True)]
    pallas_call x0 -> x2, Pallas kernels: none -> 613 us  [the longest x1 343 us: reduce_all(): pl.pallas_call(functools.partial(reduce_kernel, tuple(plan)), out_shape=o...]
    all_gather x10 -> x1, waiting for transfers between devices: 484 us -> 1.16 us  [on_device(): lax.all_gather(back_context.astype(jnp.bfloat16), 'frame', axis=0)]
    psum x3 -> x0, waiting for transfers between devices: 193 us -> none  [the longest x1 193 us: on_device(): lax.psum(back_modulation_weight.astype(jnp.bfloat16), 'clip')]
    unnamed x2 -> x0, blocking collectives: 118 us -> none
    convert_element_type x37 -> x10, other arithmetic: 44 us -> 12.3 us  [the longest x9 12.2 us: on_device(): high = lambda part: part.astype(jnp.float32)]
  transfers between devices with their start and end apart: 26 -> 3, of which waited for: 19 -> 3; matrix products, arithmetic and copies ran while one was open for 13% -> 4% of each run, Pallas kernels for 0% -> 0%
where the time goes in v1:
time: 1180 us; the launch traced here: 1160 us
  Pallas kernels  613 us (52%)
  matrix products  272 us (23%)
  other arithmetic  90.8 us (8%)
  local copies, waits for them, and re-layouts  88.3 us (7%)
  waiting for transfers between devices  54.6 us (5%)
  starting transfers between devices  24.5 us (2%)
  between operations  19.1 us (2%)
    pallas_call x1, Pallas kernels, reduce_all(): pl.pallas_call(functools.partial(reduce_kernel, tuple(plan)), out_shape=o...  343 us
    pallas_call x1, Pallas kernels, gather_all(): pl.pallas_call(functools.partial(gather_kernel, tuple(talls)), out_shape=...  270 us
    all_to_all x1, waiting for transfers between devices, on_device(): lax.all_to_all(jnp.concatenate([result_low, back_inputs.astype(jnp.bfloat...  36.6 us
  transfers between devices with their start and end apart: 3, of which 3 were waited for; matrix products, arithmetic and copies ran while one was open for 4% of the time, Pallas kernels for 0%

profile of v1, /device:TPU:27, one launch (start us, length us, event | category | flops | bytes accessed | tf_op | source)
XLA Modules:
  0.0 1162.0 jit_solution(12152462529752914651)
XLA Ops:
  16.1 5.4 concatenate.34
  28.7 269.9 %gather_all.1 = (bf16[4096,1152]{1,0:T(8,128)(2,1)}, bf16[1152,4608]{1,0:T(8,128)(2,1)}, bf16[1152,4608]{1,0:T(8,128)(2,1)}, bf16[1152,4608]{1,0:T(8,128)(2,1)},...) custom-call(bf16[512,1152]{1,0:T(8,128)(2,1)} %refs_0_.1, ...), custom_call_target="tpu_custom_call" | custom-call | tf_op jit(solution)/shard_map/gather_all/pallas_call | solution.py:287
  301.1 5.7 convolution_convert_fusion.12
  312.4 9.9 fusion.20
  322.4 6.2 copy.134
  328.6 9.7 multiply_reduce_fusion.1
  338.3 8.5 exponential_reduce_fusion
  346.9 9.1 convolution_convert_fusion.14
  356.0 5.6 fusion.78
  379.0 10.3 fusion.145
  389.3 14.8 %convolution_add_fusion.1 = f32[512,1152]{1,0:T(8,128)S(1)} fusion(bf16[4608,1152]{1,0:T(8,128)(2,1)} %get-tuple-element.45, f32[1152]{0:T(1024)S(1)} %add.354, f32[512,4608]{1,0:T(8,128)S(1)} %fusion.145, f32[4608]{0:T(1024)S(1)} %add.349), kind=kOutput, calls=%fused_computation.66 | convolution fusion | flops 5460000768 | bytes 22436352 | tf_op jit(solution)/shard_map/dot_general | solution.py:758
  409.2 9.2 reduce.16
  419.6 17.6 %all-to-all-start = ((bf16[8,2,36864]{2,1,0:T(2,128)(2,1)}), bf16[8,2,36864]{2,1,0:T(2,128)(2,1)S(1)}, u32[]{:S(2)}, u32[]{:S(2)}) async-start(bf16[8,2,36864]{2,1,0:T(2,128)(2,1)} %reshape.865), calls=%async_computation | async-start | bytes 2359296 | tf_op jit(solution)/shard_map/all_to_all | solution.py:766
  447.2 16.8 %all-to-all-done = bf16[8,2,36864]{2,1,0:T(2,128)(2,1)S(1)} async-done(((bf16[8,2,36864]{2,1,0:T(2,128)(2,1)}), bf16[8,2,36864]{2,1,0:T(2,128)(2,1)S(1)}, u32[]{:S(2)}, u32[]{:S(2)}) %all-to-all-start) | async-done | bytes 1179680 | tf_op jit(solution)/shard_map/all_to_all | solution.py:766
  470.1 10.0 fusion.23
  480.1 13.8 %reshape.837 = bf16[8,64,3,16,72]{4,3,2,1,0:T(8,128)(2,1)} reshape(bf16[8,64,3456]{2,1,0:T(8,128)(2,1)} %fusion.23) | data formatting | bytes 7077888 | tf_op jit(solution)/shard_map/reshape | solution.py:775
  524.1 10.8 convert_element_type.435
  534.8 9.3 fusion.146
  558.8 6.9 all-to-all-start.1
  574.7 6.6 fusion.refs_0_
  581.3 36.6 %all-to-all-done.1 = bf16[8,64,2304]{2,1,0:T(8,128)(2,1)} async-done(((bf16[8,64,2304]{2,1,0:T(8,128)(2,1)}), bf16[8,64,2304]{2,1,0:T(8,128)(2,1)}, u32[]{:S(2)}, u32[]{:S(2)}) %all-to-all-start.1) | async-done | bytes 2359328 | tf_op jit(solution)/shard_map/all_to_all | solution.py:830
  623.3 17.3 %convert_reduce_fusion = (f32[4608]{0:T(1024)S(1)}, bf16[512,4608]{1,0:T(8,128)(2,1)}) fusion(f32[512,4608]{1,0:T(8,128)} %copy-done.97, f32[4608]{0:T(1024)S(1)} %add.349, bf16[512,1152]{1,0:T(8,128)(2,1)S(1)} %get-tuple-element.89, bf16[4608,1152]{1,0:T(8,128)(2,1)} %get-tuple-element.45), kind=kOutput, calls=%fused_computation.22 | convolution fusion | flops 5490077184 | bytes 25989120 | tf_op jit(solution)/shard_map/pd,fd->pf/dot_general | solution.py:850
  640.6 12.0 %multiply_reduce_fusion.5 = (f32[1152]{0:T(1024)S(1)}, f32[512]{0:T(512)S(1)}, f32[1152]{0:T(1024)S(1)}, f32[512,1152]{1,0:T(8,128)S(1)}) fusion(f32[512,1152]{1,0:T(8,128)S(1)} %copy-done.14, f32[512]{0:T(512)S(1)} %copy-done.85, f32[512]{0:T(512)S(1)} %copy-done.73, f32[1152]{0:T(1024)S(1)} %copy-done.64, bf16[512,4608]{1,0:T(8,128)(2,1)} %get-tuple-element.73, ...), kind=kOutput, calls=%fused_computation.111 | convolution fusion | flops 5440534016 | bytes 20073984 | tf_op jit(solution)/shard_map/pf,df->pd/dot_general | solution.py:857
  671.0 5.9 convert_reduce_fusion.5
  684.2 7.6 convolution_bitcast_fusion.4
  691.9 11.5 multiply_reduce_fusion
  703.4 11.8 %multiply_convert_fusion = bf16[16,512,512]{1,2,0:T(8,128)(2,1)S(1)} fusion(f32[16,512,512]{1,2,0:T(8,128)} %get-tuple-element.136, f32[16,512,512]{1,2,0:T(8,128)} %get-tuple-element.119, f32[16,512]{1,0:T(8,128)S(1)} %get-tuple-element.135, f32[16,512]{1,0:T(8,128)S(1)} %copy-done.52), kind=kLoop, calls=%fused_computation.3 | loop fusion | flops 20971520 | bytes 42008576 | tf_op jit(solution)/shard_map/convert_element_type | solution.py:96
  719.5 10.8 convolution_convert_fusion.refs_3_
  744.3 10.4 fusion.58
  768.3 7.9 convolution_convert_fusion.2.refs_7_
  776.2 10.3 convolution_convert_fusion.1.refs_2_
  791.9 342.7 %reduce_all.1 = (bf16[144,4608]{1,0:T(8,128)(2,1)S(1)}, bf16[576,1152]{1,0:T(8,128)(2,1)S(1)}, bf16[144,4608]{1,0:T(8,128)(2,1)S(1)}, bf16[144,4608]{1,0:T(8,128...) custom-call(bf16[1152,3456]{1,0:T(8,128)(2,1)} %fusion.refs_0_, ...), custom_call_target="tpu_custom_call" | custom-call | tf_op jit(solution)/shard_map/reduce_all/pallas_call | solution.py:572
  (382 shorter events, 202.0 us)
Async XLA Ops:
  7.2 17.2 %copy-start = (bf16[144,6912]{1,0:T(8,128)(2,1)S(1)}, bf16[144,6912]{1,0:T(8,128)(2,1)}, u32[]{:S(2)}) copy-start(bf16[144,6912]{1,0:T(8,128)(2,1)} %param.34) | copy-start | bytes 5971972
  7.2 18.6 %copy-start.56 = (bf16[144,1152]{1,0:T(8,128)(2,1)S(1)}, bf16[144,1152]{1,0:T(8,128)(2,1)}, u32[]{:S(2)}) copy-start(bf16[144,1152]{1,0:T(8,128)(2,1)} %param.51) | copy-start | bytes 995332
  7.2 18.6 %copy-start.49 = (bf16[144,3456]{1,0:T(8,128)(2,1)S(1)}, bf16[144,3456]{1,0:T(8,128)(2,1)}, u32[]{:S(2)}) copy-start(bf16[144,3456]{1,0:T(8,128)(2,1)} %param.50) | copy-start | bytes 2985988
  14.7 432.4 %copy-start.82 = (s32[8]{0:T(128)}, s32[8]{0:T(128)S(1)}, u32[]{:S(2)}) copy-start(s32[8]{0:T(128)S(1)} %get-tuple-element.83) | copy-start | bytes 100
  309.5 61.5 %copy-start.27 = (bf16[120,2304]{0,1:T(8,128)(2,1)}, bf16[120,2304]{0,1:T(8,128)(2,1)S(1)}, u32[]{:S(2)}) copy-start(bf16[120,2304]{0,1:T(8,128)(2,1)S(1)} %copy.136) | copy-start | bytes 1658884
  311.5 59.5 %copy-start.80 = (pred[120]{0:T(512)(128)(4,1)}, pred[120]{0:T(512)(128)(4,1)S(1)}, u32[]{:S(2)}) copy-start(pred[120]{0:T(512)(128)(4,1)S(1)} %iota_compare_fusion.2) | copy-start | bytes 364
  311.5 10.8 copy-start.61
  311.6 10.8 copy-start.86
  311.6 60.6 %copy-start.90 = (f32[1152]{0:T(1024)}, f32[1152]{0:T(1024)S(1)}, u32[]{:S(2)}) copy-start(f32[1152]{0:T(1024)S(1)} %get-tuple-element.106) | copy-start | bytes 13828
  311.6 67.4 %copy-start.63 = (f32[1152]{0:T(1024)}, f32[1152]{0:T(1024)S(1)}, u32[]{:S(2)}) copy-start(f32[1152]{0:T(1024)S(1)} %get-tuple-element.103) | copy-start | bytes 13828
  311.6 67.4 %copy-start.88 = (f32[1152]{0:T(1024)}, f32[1152]{0:T(1024)S(1)}, u32[]{:S(2)}) copy-start(f32[1152]{0:T(1024)S(1)} %get-tuple-element.102) | copy-start | bytes 13828
  377.1 12.2 %copy-start.72 = (f32[512]{0:T(512)}, f32[512]{0:T(512)S(1)}, u32[]{:S(2)}) copy-start(f32[512]{0:T(512)S(1)} %broadcast_multiply_fusion.4) | copy-start | bytes 6148
  389.3 14.8 %copy-start.97 = (f32[512,4608]{1,0:T(8,128)}, f32[512,4608]{1,0:T(8,128)S(1)}, u32[]{:S(2)}) copy-start(f32[512,4608]{1,0:T(8,128)S(1)} %fusion.145) | copy-start | bytes 28311556
  389.3 14.8 %copy-start.13 = (f32[512,1152]{1,0:T(8,128)S(1)}, f32[512,1152]{1,0:T(8,128)}, u32[]{:S(2)}) copy-start(f32[512,1152]{1,0:T(8,128)} %copy-done.12) | copy-start | bytes 7077892
  419.6 44.4 %all-to-all-start = ((bf16[8,2,36864]{2,1,0:T(2,128)(2,1)}), bf16[8,2,36864]{2,1,0:T(2,128)(2,1)S(1)}, u32[]{:S(2)}, u32[]{:S(2)}) async-start(bf16[8,2,36864]{2,1,0:T(2,128)(2,1)} %reshape.865), calls=%async_computation | async-start | bytes 2359296 | tf_op jit(solution)/shard_map/all_to_all | solution.py:766
  558.8 59.0 %all-to-all-start.1 = ((bf16[8,64,2304]{2,1,0:T(8,128)(2,1)}), bf16[8,64,2304]{2,1,0:T(8,128)(2,1)}, u32[]{:S(2)}, u32[]{:S(2)}) async-start(bf16[8,64,2304]{2,1,0:T(8,128)(2,1)} %pad_maximum_fusion), calls=%async_computation.1 | async-start | bytes 4718592 | tf_op jit(solution)/shard_map/all_to_all | solution.py:830
  565.8 221.9 %all-gather.3.cloned.1.call-start = ((), (), s32[]{:S(2)}) async-start(), calls=%async_computation.2 | async-start | bytes 2488320 | tf_op jit(solution)/shard_map/all_gather | solution.py:943
  574.7 43.2 %copy-start.19 = (bf16[1,1,512,1152]{3,2,1,0:T(8,128)(2,1)S(1)}, bf16[1,1,512,1152]{3,2,1,0:T(8,128)(2,1)}, u32[]{:S(2)}) copy-start(bf16[1,1,512,1152]{3,2,1,0:T(8,128)(2,1)} %param.28) | copy-start | bytes 3538948
  623.3 17.3 %copy-start.40 = (bf16[512,1152]{1,0:T(8,128)(2,1)}, bf16[512,1152]{1,0:T(8,128)(2,1)S(1)}, u32[]{:S(2)}) copy-start(bf16[512,1152]{1,0:T(8,128)(2,1)S(1)} %get-tuple-element.89) | copy-start | bytes 3538948
  623.3 17.3 %copy-start.14 = (f32[512,1152]{1,0:T(8,128)S(1)}, f32[512,1152]{1,0:T(8,128)}, u32[]{:S(2)}) copy-start(f32[512,1152]{1,0:T(8,128)} %copy-done.12) | copy-start | bytes 7077892
  623.3 17.3 %copy-start.64 = (f32[1152]{0:T(1024)S(1)}, f32[1152]{0:T(1024)}, u32[]{:S(2)}) copy-start(f32[1152]{0:T(1024)} %copy-done.63) | copy-start | bytes 13828
  623.3 17.3 %copy-start.73 = (f32[512]{0:T(512)S(1)}, f32[512]{0:T(512)}, u32[]{:S(2)}) copy-start(f32[512]{0:T(512)} %copy-done.72) | copy-start | bytes 6148
  623.3 17.3 %copy-start.85 = (f32[512]{0:T(512)S(1)}, f32[512]{0:T(512)}, u32[]{:S(2)}) copy-start(f32[512]{0:T(512)} %copy-done.84) | copy-start | bytes 6148
  640.6 12.0 %copy-start.77 = (f32[512]{0:T(512)S(1)}, f32[512]{0:T(512)}, u32[]{:S(2)}) copy-start(f32[512]{0:T(512)} %copy-done.76) | copy-start | bytes 6148
  719.5 10.8 copy-start.44
  719.5 10.8 copy-start.99
  743.0 13.1 %slice-start = ((s8[10616832]{0:T(1024)(128)(4,1)}), s8[4194304]{0:T(1024)(128)(4,1)S(1)}, s32[]{:S(2)}) async-start(s8[10616832]{0:T(1024)(128)(4,1)} %bitcast.393), calls=%async_computation.3 | async-start | bytes 8388608
  743.7 11.0 copy-start.32
  744.3 11.8 %slice-start.1 = ((s8[10616832]{0:T(1024)(128)(4,1)}), s8[4194304]{0:T(1024)(128)(4,1)S(1)}, s32[]{:S(2)}) async-start(s8[10616832]{0:T(1024)(128)(4,1)} %bitcast.393), calls=%async_computation.4 | async-start | bytes 8388608
  744.3 11.8 %slice-start.2 = ((s8[10616832]{0:T(1024)(128)(4,1)}), s8[2228224]{0:T(1024)(128)(4,1)S(1)}, s32[]{:S(2)}) async-start(s8[10616832]{0:T(1024)(128)(4,1)} %bitcast.393), calls=%async_computation.5 | async-start | bytes 4456448
  764.0 12.2 %slice-start.3 = ((s8[9437184]{0:T(1024)(128)(4,1)}), s8[4194304]{0:T(1024)(128)(4,1)S(1)}, s32[]{:S(2)}) async-start(s8[9437184]{0:T(1024)(128)(4,1)} %bitcast.396), calls=%async_computation.6 | async-start | bytes 8388608
  776.2 11.5 copy-start.83
  (77 other events, 290.1 us)
Sparse Core Ops, SparseCore 0:
  758.8 28.7 all-gather.2

commit v2 on v1

v2 whole, which is shorter than its diff:
```python
import functools
import math
import types

import jax
import jax.numpy as jnp
from jax import lax
from jax.experimental import pallas as pl
from jax.experimental.pallas import tpu as pltpu
from jax.sharding import PartitionSpec as P

HEADS = 16


eps_norm = 1e-06
big_negative = -1e30


def assign_clips(frame_counts, frame_count):
    slot_count = frame_counts.shape[0]
    slot_ids = jnp.arange(slot_count, dtype=jnp.int32)
    longest = jnp.max(frame_counts)
    long_slot = jnp.min(jnp.where(frame_counts == longest, slot_ids, slot_count))
    frame_ids = jnp.arange(frame_count, dtype=jnp.int32)
    long_gaps = jnp.maximum(longest - 1, 1)
    frame_gaps = frame_count - 1
    step_index = (frame_ids * long_gaps + frame_gaps - 1) // frame_gaps
    on_long = step_index * frame_gaps // long_gaps == frame_ids
    long_marks = on_long.astype(jnp.int32)
    before_count = jnp.cumsum(long_marks) - long_marks
    order_rank = frame_ids - before_count
    rest_counts = jnp.where(slot_ids == long_slot, 0, frame_counts)
    rest_ends = jnp.cumsum(rest_counts)
    rest_ids = jnp.sum((rest_ends[None, :] <= order_rank[:, None]).astype(jnp.int32), axis=1)
    return jnp.where(on_long, long_slot, rest_ids)


def normalize(values):
    average = jnp.mean(values, axis=-1, keepdims=True)
    centred = values - average
    spread = jnp.mean(centred * centred, axis=-1, keepdims=True)
    return centred * lax.rsqrt(spread + eps_norm)


def normal_parts(values):
    average = jnp.mean(values, axis=-1, keepdims=True)
    centred = values - average
    rate = lax.rsqrt(jnp.mean(centred * centred, axis=-1, keepdims=True) + eps_norm)
    return centred * rate, rate


def modulate(values, offset, scaling):
    return normalize(values) * (1.0 + scaling) + offset


def affine_norm(values, norm_gain, offset):
    return normalize(values) * norm_gain + offset


def smooth_gelu(values):
    return jax.nn.gelu(values, approximate=True)


def slope_gelu(values):
    inner = math.sqrt(2.0 / math.pi)
    bent = jnp.tanh(inner * (values + 0.044715 * values * values * values))
    steep = inner * (1.0 + 3.0 * 0.044715 * values * values)
    return 0.5 * (1.0 + bent) + 0.5 * values * (1.0 - bent * bent) * steep


def embed_time(time_steps, model_width):
    half_width = model_width // 2
    frequency = jnp.exp(-math.log(10000.0) * jnp.arange(half_width, dtype=jnp.float32) / half_width)
    angles = time_steps.astype(jnp.float32)[:, None] * frequency[None, :]
    return jax.nn.silu(jnp.concatenate([jnp.cos(angles), jnp.sin(angles)], axis=1))


def attend(queries, key_rows, values, valid_mask, att_scale):
    scores = (
        jnp.einsum("qbhd,kbhd->bhqk", queries, key_rows, preferred_element_type=jnp.float32)
        * att_scale
    )
    if valid_mask is not None:
        scores = jnp.where(valid_mask, scores, big_negative)
    largest = jnp.max(scores, axis=-1, keepdims=True)
    summed = jnp.sum(jnp.exp(scores - largest), axis=-1, keepdims=True)
    logsum = largest + jnp.log(summed)
    weights = jnp.exp(scores - logsum).astype(jnp.bfloat16)
    output = jnp.einsum("bhqk,kbhd->qbhd", weights, values, preferred_element_type=jnp.float32)
    return (output, logsum)


def attend_back(queries, key_rows, values, valid_mask, att_scale, logsum, upstream):
    scores = (
        jnp.einsum("qbhd,kbhd->bhqk", queries, key_rows, preferred_element_type=jnp.float32)
        * att_scale
    )
    if valid_mask is not None:
        scores = jnp.where(valid_mask, scores, big_negative)
    weights = jnp.exp(scores - logsum)
    back_weights = jnp.einsum(
        "qbhd,kbhd->bhqk", upstream, values, preferred_element_type=jnp.float32
    )
    back_values = jnp.einsum(
        "bhqk,qbhd->kbhd",
        weights.astype(jnp.bfloat16),
        upstream,
        preferred_element_type=jnp.float32,
    )
    inner_sum = jnp.sum(back_weights * weights, axis=-1, keepdims=True)
    back_scores = (weights * (back_weights - inner_sum)).astype(jnp.bfloat16)
    back_queries = (
        jnp.einsum("bhqk,kbhd->qbhd", back_scores, key_rows, preferred_element_type=jnp.float32)
        * att_scale
    )
    back_keys = (
        jnp.einsum("bhqk,qbhd->kbhd", back_scores, queries, preferred_element_type=jnp.float32)
        * att_scale
    )
    return (back_queries, back_keys, back_values)


MESH_ID = pl.DeviceIdType.MESH
LANES = 128
PIECE_SLOTS = 4


def neighbours():
    column = lax.axis_index("clip")
    frame = lax.axis_index("frame")
    depth = frame // 2
    core = frame % 2
    across_x = column + 1 - 2 * (column % 2)
    across_y = column + 2 - 4 * (column // 2)
    sibling = frame + 1 - 2 * core
    return column, frame, depth, core, across_x, across_y, sibling


def greet(peers):
    barrier = pltpu.get_barrier_semaphore()
    for peer in peers:
        pl.semaphore_signal(barrier, inc=1, device_id=peer, device_id_type=MESH_ID)
    pl.semaphore_wait(barrier, len(peers))


class Copies:
    def __init__(self, send_sems, recv_sems):
        self.send_sems, self.recv_sems, self.count, self.started = send_sems, recv_sems, 0, []
        self.maybe = []

    def start(self, source, target, device):
        copy = pltpu.make_async_remote_copy(
            src_ref=source,
            dst_ref=target,
            send_sem=self.send_sems.at[self.count],
            recv_sem=self.recv_sems.at[self.count],
            device_id=device,
            device_id_type=MESH_ID,
        )
        self.count += 1
        assert self.count <= self.send_sems.shape[0]
        copy.start()
        self.started.append(copy)
        return copy

    def start_if(self, condition, source, target, device, recv_sem):
        copy = pltpu.make_async_remote_copy(
            src_ref=source,
            dst_ref=target,
            send_sem=self.send_sems.at[self.count],
            recv_sem=recv_sem,
            device_id=device,
            device_id_type=MESH_ID,
        )
        self.count += 1
        assert self.count <= self.send_sems.shape[0]
        pl.when(condition)(copy.start)
        self.maybe.append((condition, copy))

    def finish(self):
        for copy in self.started:
            copy.wait_send()
        for condition, copy in self.maybe:
            pl.when(condition)(copy.wait_send)


def rows_at(ref, start, size, step):
    return ref.at[pl.ds(pl.multiple_of(start, step), size), :]


def whole_unit(ref, tall, unit, frame):
    if tall:
        height = ref.shape[0] // 32
        return rows_at(ref, frame * (4 * height) + unit * height, height, height)
    height, width = ref.shape[0] // 8, ref.shape[1] // 4
    return ref.at[
        pl.ds(pl.multiple_of(frame * height, height), height),
        pl.ds(pl.multiple_of(unit * width, LANES), width),
    ]


def whole_share(ref, tall, frame):
    height = ref.shape[0] // 8
    return rows_at(ref, frame * height, height, height)


def share_unit(ref, tall, unit):
    if tall:
        height = ref.shape[0] // 4
        return rows_at(ref, unit * height, height, height)
    width = ref.shape[1] // 4
    return ref.at[:, pl.ds(pl.multiple_of(unit * width, LANES), width)]


def gather_all(shares, vec, mod_rows):
    wholes = [lax.all_gather(share, "frame", axis=0, tiled=True) for share in shares]
    vecs = lax.all_gather(vec, "frame", axis=0)
    mods = lax.all_to_all(mod_rows, "frame", split_axis=0, concat_axis=0, tiled=True)
    return wholes, vecs, mods


def add_stream(count, left_at, right_at, out_at, left_buf, right_buf, out_buf, sems):
    def loads(index):
        slot = index % PIECE_SLOTS
        return (
            pltpu.make_async_copy(left_at(index), left_buf.at[slot], sems.at[0, slot]),
            pltpu.make_async_copy(right_at(index), right_buf.at[slot], sems.at[1, slot]),
        )

    def store(index):
        slot = index % PIECE_SLOTS
        return pltpu.make_async_copy(out_buf.at[slot], out_at(index), sems.at[2, slot])

    ahead = min(PIECE_SLOTS - 1, count)
    for index in range(ahead):
        for copy in loads(index):
            copy.start()

    def step(index, carry):
        @pl.when(index + PIECE_SLOTS - 1 < count)
        def _():
            for copy in loads(index + PIECE_SLOTS - 1):
                copy.start()

        for copy in loads(index):
            copy.wait()

        @pl.when(index >= PIECE_SLOTS)
        def _():
            store(index - PIECE_SLOTS).wait()

        slot = index % PIECE_SLOTS
        out_buf[slot] = left_buf[slot] + right_buf[slot]
        store(index).start()
        return carry

    lax.fori_loop(0, count, step, 0)
    for index in range(max(0, count - PIECE_SLOTS), count):
        store(index).wait()


ROW_TILE = 64
HEAD_LANES = 128
MOD_ROWS = 6


def dot_rows(left, right):
    return lax.dot_general(
        left, right, (((1,), (1,)), ((), ())), preferred_element_type=jnp.float32
    )


def dot_plain(left, right):
    return jnp.dot(left, right, preferred_element_type=jnp.float32)


def run_tiles(body, count, ins, outs):
    pltpu.emit_pipeline(
        body,
        grid=(count,),
        in_specs=[pl.BlockSpec(block, index) for _, block, index in ins],
        out_specs=[pl.BlockSpec(block, index) for _, block, index in outs],
    )(*[ref for ref, _, _ in ins], *[ref for ref, _, _ in outs])


def by_rows(ref, size):
    if len(ref.shape) == 4:
        return (ref, (1,) + ref.shape[1:], lambda step: (step, 0, 0, 0))
    return (ref, (size, ref.shape[1]), lambda step: (step, 0))


def by_columns(ref, size):
    return (ref, (ref.shape[0], size), lambda step: (0, step))


def tile_rows(step, size):
    return pl.ds(pl.multiple_of(step * size, size), size)


def add_row(rows, which, values):
    rows[which : which + 1, :] += jnp.sum(values, axis=0, keepdims=True)


def split_heads(source, first, heads, width, count):
    height = source.shape[0]
    tile = min(height, ROW_TILE)

    def step(index, carry):
        rows = tile_rows(index, tile)
        for head in range(count):
            start = first + head * width
            heads[head, rows, 0:width] = source[rows, start : start + width]
        return carry

    lax.fori_loop(0, height // tile, step, 0)


def merge_heads(heads, target, first, width, count):
    height = target.shape[0]
    tile = min(height, ROW_TILE)

    def step(index, carry):
        rows = tile_rows(index, tile)
        joined = jnp.concatenate([heads[head, rows, 0:width] for head in range(count)], axis=1)
        target[rows, first : first + width * count] = joined
        return carry

    lax.fori_loop(0, height // tile, step, 0)


def attention_back(att_scale, queries, keys, values, mask, logsum, upstream, outs):
    out_queries, out_keys, out_values = outs
    count = queries.shape[0]

    def body(query, key, value):
        head = pl.program_id(0)
        query, key, value, given = query[0], key[0], value[0], upstream[head]
        scores = dot_rows(key, query) * att_scale
        if mask is not None:
            scores = scores + mask[:, 0:1]
        weights = jnp.exp(scores - logsum[head, 0:1, :])
        back_weights = dot_rows(value, given)
        inner = jnp.sum(back_weights * weights, axis=0, keepdims=True)
        back_scores = (weights * (back_weights - inner)).astype(jnp.bfloat16)
        out_values[head] = dot_plain(weights.astype(jnp.bfloat16), given).astype(jnp.bfloat16)
        out_keys[head] = (dot_plain(back_scores, query) * att_scale).astype(jnp.bfloat16)
        turned = lax.dot_general(
            key, back_scores, (((0,), (0,)), ((), ())), preferred_element_type=jnp.float32
        )
        out_queries[head] = (turned * att_scale).T.astype(jnp.bfloat16)

    per_head = lambda ref: (ref, (1,) + ref.shape[1:], lambda step: (step, 0, 0))
    run_tiles(body, count, [per_head(queries), per_head(keys), per_head(values)], [])


ROW = types.SimpleNamespace(
    shift_a=0, scale_a=1, gate_a=2, shift_m=3, scale_m=4, gate_m=5, condition=6, gate_t=7,
    spatial=8, cross=9, reduce=10, gain=11, shift=12, temporal=13, expand=14, high=24,
)


def back_stages(r, att_scale):
    width = r.running.shape[1]
    head_size = width // HEADS
    third = width // 3
    plain = jnp.float32

    def clear():
        r.row_sums[...] = jnp.zeros_like(r.row_sums)
        for heads in (r.head_in, r.head_query, r.head_key, r.head_value):
            heads[...] = jnp.zeros_like(heads)

    def feed_first():
        def body(cot, sent, branch):
            rows = tile_rows(pl.program_id(0), ROW_TILE)
            total = cot[...].astype(plain) + sent[...].reshape(cot.shape).astype(plain)
            r.running[rows, :] = total
            add_row(r.row_sums, ROW.gate_m, total * branch[...].astype(plain))
            down = (total * r.mods[5:6, :]).astype(jnp.bfloat16)
            r.low[rows, :] = down
            add_row(r.row_sums, ROW.reduce, down.astype(plain))

        ins = [by_rows(ref, ROW_TILE) for ref in (r.cotangent, r.back_sent, r.branch_feed)]
        run_tiles(body, r.low.shape[0] // ROW_TILE, ins, [])

    def part_by_rows(turned, right, target, size, place=0):
        def body(left, out):
            out[...] = dot_plain(left[...], right()).astype(jnp.bfloat16)

        run_tiles(
            body,
            turned.shape[0] // size,
            [by_rows(turned, size)],
            [(target, (size, width), lambda step: (step, place))],
        )

    def part_by_columns(turned, right, target, size, first=0, count=None):
        def body(left, out):
            columns = tile_rows(pl.program_id(0) + first, size)
            out[...] = dot_plain(left[...], right[:, columns]).astype(jnp.bfloat16)

        whole = (turned, turned.shape, lambda step: (0, 0))
        run_tiles(
            body,
            target.shape[1] // size if count is None else count,
            [whole],
            [(target, (target.shape[0], size), lambda step: (0, step + first))],
        )

    def reduce_part():
        part_by_rows(r.hidden_turned, lambda: r.low[...], r.part_reduce, 512)

    def feed_hidden():
        def body(weight, slope):
            columns = tile_rows(pl.program_id(0), 512)
            back = dot_rows(r.low[...], weight[...]) * slope[...].astype(plain)
            down = back.astype(jnp.bfloat16)
            r.broad[:, columns] = down

        run_tiles(
            body,
            r.broad.shape[1] // 512,
            [by_rows(r.whole_reduce, 512), by_columns(r.gelu_slope, 512)],
            [],
        )
        for unit in range(4):
            piece = r.broad[:, unit * width : (unit + 1) * width].astype(plain)
            add_row(r.row_sums, ROW.expand + unit, piece)

    def expand_part():
        part_by_columns(r.feed_turned, r.broad, r.part_expand, 512)

    def back_through(weight, block, place, source, target):
        def body(rows):
            columns = tile_rows(pl.program_id(0), third)
            target(columns, dot_rows(source(), rows[...]))

        run_tiles(body, 3, [(weight, (third, block), lambda step: (step, place))], [])

    def set_wide(columns, value):
        r.wide[:, columns] = value

    def add_running(columns, value):
        r.running[:, columns] += value

    def set_broad(columns, value):
        r.broad[:, columns] = value.astype(jnp.bfloat16)

    def back_three(weight):
        def body(*blocks):
            columns = tile_rows(pl.program_id(0), third)
            total = dot_rows(r.broad[:, 0:width], blocks[0][...])
            for place in (1, 2):
                total += dot_rows(
                    r.broad[:, place * width : (place + 1) * width], blocks[place][...]
                )
            r.wide[:, columns] = total

        block = lambda place: (weight, (third, width), lambda step: (step, place))
        run_tiles(body, 3, [block(0), block(1), block(2)], [])

    def feed_normed():
        back_through(r.whole_expand, 4 * width, 0, lambda: r.broad[...], set_wide)

    def norm_back(rows, normal, rate, shift_row, scale_row):
        back = r.wide[rows, :]
        normal = normal.astype(plain)
        add_row(r.row_sums, shift_row, back)
        add_row(r.row_sums, scale_row, back * normal)
        back = back * (1.0 + r.mods[scale_row : scale_row + 1, :])
        mean = jnp.mean(back, axis=1, keepdims=True)
        inner = jnp.mean(back * normal, axis=1, keepdims=True)
        return (back - mean - normal * inner) * rate[rows, 0:1]

    def feed_last():
        def body(normal):
            rows = tile_rows(pl.program_id(0), ROW_TILE)
            total = r.running[rows, :] + norm_back(rows, normal[...], r.feed_rate, 3, 4)
            r.running[rows, :] = total
            down = total.astype(jnp.bfloat16)
            r.low[rows, :] = down
            add_row(r.row_sums, ROW.cross, down.astype(plain))

        run_tiles(body, r.low.shape[0] // ROW_TILE, [by_rows(r.feed_normal, ROW_TILE)], [])

    def cross_part():
        part_by_rows(r.cross_turned, lambda: r.low[...], r.part_text.at[:, pl.ds(0, 4 * width)], third, 3)

    def cross_given():
        back_through(r.whole_text, width, 3, lambda: r.low[...], set_broad)
        split_heads(r.broad, 0, r.head_in, head_size, HEADS)

    def cross_attention():
        attention_back(
            att_scale,
            r.cross_queries,
            r.cross_keys,
            r.cross_values,
            r.text_mask,
            r.cross_logsum,
            r.head_in,
            (r.head_query, r.cross_key, r.cross_value),
        )
        merge_heads(r.head_query, r.broad, 0, head_size, HEADS)
        merge_heads(r.cross_key, r.memory, 0, head_size, HEADS)
        merge_heads(r.cross_value, r.memory, width, head_size, HEADS)

    def query_part():
        part_by_rows(r.after_turned, lambda: r.broad[:, 0:width], r.part_text.at[:, pl.ds(0, 4 * width)], third, 0)

    def memory_part():
        for place in range(2):
            part_by_rows(
                r.context_turned,
                lambda: r.memory[:, place * width : (place + 1) * width],
                r.part_text.at[:, pl.ds(0, 4 * width)],
                third,
                place + 1,
            )

    def context_back():
        def body(keys, values, out):
            back = dot_rows(r.memory[:, 0:width], keys[...])
            back = back + dot_rows(r.memory[:, width : 2 * width], values[...])
            out[...] = back.astype(jnp.bfloat16)

        run_tiles(
            body,
            3,
            [
                (r.whole_text, (third, width), lambda step: (step, 1)),
                (r.whole_text, (third, width), lambda step: (step, 2)),
            ],
            [by_columns(r.back_context, third)],
        )

    def query_back():
        back_through(r.whole_text, width, 0, lambda: r.broad[:, 0:width], add_running)

    def spatial_first():
        def body(branch):
            rows = tile_rows(pl.program_id(0), ROW_TILE)
            total = r.running[rows, :]
            add_row(r.row_sums, ROW.gate_a, total * branch[...].astype(plain))
            down = (total * r.mods[2:3, :]).astype(jnp.bfloat16)
            r.low[rows, :] = down
            add_row(r.row_sums, ROW.spatial, down.astype(plain))

        run_tiles(body, r.low.shape[0] // ROW_TILE, [by_rows(r.branch_attend, ROW_TILE)], [])

    def output_part():
        def body(left, out):
            out[:, 0:width] = dot_plain(left[...], r.low[...]).astype(jnp.bfloat16)
            out[:, width:] = jnp.zeros_like(out[:, width:])

        run_tiles(
            body,
            3,
            [by_rows(r.spatial_turned, third)],
            [(r.part_text, (third, width + third), lambda step: (step, 3))],
        )

    def spatial_given():
        back_through(r.whole_spatial, width, 3, lambda: r.low[...], set_broad)
        split_heads(r.broad, 0, r.head_in, head_size, HEADS)

    def spatial_attention():
        attention_back(
            att_scale,
            r.queries,
            r.keys,
            r.values,
            None,
            r.spatial_logsum,
            r.head_in,
            (r.head_query, r.head_key, r.head_value),
        )
        merge_heads(r.head_query, r.broad, 0, head_size, HEADS)
        merge_heads(r.head_key, r.broad, width, head_size, HEADS)
        merge_heads(r.head_value, r.broad, 2 * width, head_size, HEADS)

    def input_part(first=0, count=7):
        part_by_columns(r.attend_turned, r.broad, r.part_input, 512, first, count)

    def attend_normed():
        back_three(r.whole_spatial)

    def attend_last():
        def body(normal, out):
            rows = tile_rows(pl.program_id(0), ROW_TILE)
            total = r.running[rows, :] + norm_back(rows, normal[...], r.attend_rate, 0, 1)
            out[...] = total.astype(jnp.bfloat16)

        run_tiles(
            body,
            r.low.shape[0] // ROW_TILE,
            [by_rows(r.attend_normal, ROW_TILE)],
            [by_rows(r.tokens_out, ROW_TILE)],
        )

    tile = r.low.shape[0] // 4
    quads = [pl.ds(index * tile, tile) for index in range(4)]

    def by_blocks(ref):
        return (ref, (1,) + ref.shape[1:], lambda step: (step, 0, 0, 0))

    def turn(source, target):
        def step(index, carry):
            rows = tile_rows(index, tile)
            target[:, rows] = source[rows, :].astype(plain).T.astype(jnp.bfloat16)
            return carry

        lax.fori_loop(0, 4, step, 0)

    def time_first():
        def body(cols):
            rows = tile_rows(pl.program_id(0), tile)
            values = cols[...].reshape(tile, width).astype(plain)
            values = values - jnp.mean(values, axis=1, keepdims=True)
            rate = lax.rsqrt(jnp.mean(values * values, axis=1, keepdims=True) + eps_norm)
            normal = values * rate
            r.time_normal[rows, :] = normal.astype(jnp.bfloat16)
            r.time_rate[rows, :] = jnp.broadcast_to(rate, (tile, LANES))
            r.low[rows, :] = (normal * r.vectors[0:1, :] + r.vectors[1:2, :]).astype(jnp.bfloat16)

        run_tiles(body, 4, [by_blocks(r.time_cols)], [])
        turn(r.low, r.time_turned)

    def time_heads():
        def body(weight):
            columns = tile_rows(pl.program_id(0), third)
            r.broad[:, columns] = dot_plain(r.low[...], weight[...]).astype(jnp.bfloat16)

        run_tiles(body, 9, [by_columns(r.whole_time, third)], [])
        for place, heads in enumerate((r.head_query, r.head_key, r.head_value)):
            split_heads(r.broad, place * width, heads, head_size, HEADS)

    def time_attention():
        def step(pair, carry):
            spots = [(pair * 2 + index, rows) for index in range(2) for rows in quads]
            keys = [r.head_key[spot] for spot in spots]
            values = [r.head_value[spot] for spot in spots]
            scores = [
                dot_rows(key, r.head_query[spot]) * att_scale + r.time_mask[...]
                for key, spot in zip(keys, spots)
            ]
            largest = [jnp.max(score, axis=0, keepdims=True) for score in scores]
            logsums = [
                top + jnp.log(jnp.sum(jnp.exp(score - top), axis=0, keepdims=True))
                for score, top in zip(scores, largest)
            ]
            weights = [
                jnp.exp(score - logs).astype(jnp.bfloat16) for score, logs in zip(scores, logsums)
            ]
            turned = [
                lax.dot_general(
                    value, weight, (((0,), (0,)), ((), ())), preferred_element_type=plain
                )
                for value, weight in zip(values, weights)
            ]
            turned = [value.T.astype(jnp.bfloat16) for value in turned]
            for (head, rows), logs, value in zip(spots, logsums, turned):
                r.time_logsum[head, 0:1, rows] = logs
                r.head_in[head, rows, :] = value
            return carry

        lax.fori_loop(0, HEADS // 2, step, 0)
        merge_heads(r.head_in, r.middle, 0, head_size, HEADS)
        turn(r.middle, r.middle_turned)

    def time_result():
        def body(weight, out):
            columns = tile_rows(pl.program_id(0), third)
            value = dot_plain(r.middle[...], weight[...]) + r.vectors[2:3, columns]
            out[...] = value.astype(jnp.bfloat16).reshape(out.shape)

        shape = r.time_result.shape
        run_tiles(
            body,
            3,
            [(r.whole_time, (width, third), lambda step: (0, 9 + step))],
            [(r.time_result, shape[:3] + (third,), lambda step: (0, 0, 0, step))],
        )

    def time_given():
        def body(cols):
            rows = tile_rows(pl.program_id(0), tile)
            values = cols[...].reshape(tile, width).astype(plain)
            down = (values * (r.time_keep[rows, 0:1] * r.vectors[3:4, :])).astype(jnp.bfloat16)
            r.low[rows, :] = down
            add_row(r.row_sums, ROW.temporal, down.astype(plain))

        run_tiles(body, 4, [by_blocks(r.cot_cols)], [])
        back_through(r.whole_time, width, 3, lambda: r.low[...], set_broad)
        split_heads(r.broad, 0, r.head_in, head_size, HEADS)

    def time_out_part():
        def body(out):
            rows = tile_rows(pl.program_id(0), third)
            out[...] = dot_plain(r.middle_turned[rows, :], r.low[...]).astype(jnp.bfloat16)

        run_tiles(body, 3, [], [(r.part_time, (third, width), lambda step: (step, 3))])

    def time_attention_back():
        def step(pair, carry):
            spots = [(pair * 2 + index, rows) for index in range(2) for rows in quads]
            queries = [r.head_query[spot] for spot in spots]
            keys = [r.head_key[spot] for spot in spots]
            values = [r.head_value[spot] for spot in spots]
            givens = [r.head_in[spot] for spot in spots]
            weights = [
                jnp.exp(
                    dot_rows(key, query) * att_scale
                    + r.time_mask[...]
                    - r.time_logsum[head, 0:1, rows]
                )
                for key, query, (head, rows) in zip(keys, queries, spots)
            ]
            backs = [dot_rows(value, given) for value, given in zip(values, givens)]
            inner = [
                jnp.sum(back * weight, axis=0, keepdims=True)
                for back, weight in zip(backs, weights)
            ]
            backs = [
                (weight * (back - total)).astype(jnp.bfloat16)
                for weight, back, total in zip(weights, backs, inner)
            ]
            back_values = [
                dot_plain(weight.astype(jnp.bfloat16), given).astype(jnp.bfloat16)
                for weight, given in zip(weights, givens)
            ]
            back_keys = [
                (dot_plain(back, query) * att_scale).astype(jnp.bfloat16)
                for back, query in zip(backs, queries)
            ]
            turned = [
                lax.dot_general(key, back, (((0,), (0,)), ((), ())), preferred_element_type=plain)
                for key, back in zip(keys, backs)
            ]
            turned = [(value * att_scale).T.astype(jnp.bfloat16) for value in turned]
            for (head, rows), *outs in zip(spots, turned, back_keys, back_values):
                r.head_query[head, rows, :] = outs[0]
                r.head_key[head, rows, :] = outs[1]
                r.head_value[head, rows, :] = outs[2]
            return carry

        lax.fori_loop(0, HEADS // 2, step, 0)
        for place, heads in enumerate((r.head_query, r.head_key, r.head_value)):
            merge_heads(heads, r.broad, place * width, head_size, HEADS)

    def time_normed():
        back_three(r.whole_time)

    def time_last():
        def body(out):
            rows = tile_rows(pl.program_id(0), tile)
            back = r.wide[rows, :]
            normal = r.time_normal[rows, :].astype(plain)
            add_row(r.row_sums, ROW.shift, back)
            add_row(r.row_sums, ROW.gain, back * normal)
            back = back * r.vectors[0:1, :]
            mean = jnp.mean(back, axis=1, keepdims=True)
            inner = jnp.mean(back * normal, axis=1, keepdims=True)
            back = (back - mean - normal * inner) * r.time_rate[rows, 0:1]
            out[...] = back.astype(jnp.bfloat16).reshape(out.shape)

        run_tiles(body, 4, [], [by_blocks(r.time_back)])

    def time_in_part():
        def body(out):
            columns = tile_rows(pl.program_id(0), third)
            out[...] = dot_plain(r.time_turned[...], r.broad[:, columns]).astype(jnp.bfloat16)

        run_tiles(body, 9, [], [by_columns(r.part_time, third)])

    def block_last():
        def body(after, result, cot, out):
            value = result[...].reshape(cot.shape).astype(plain)
            add_row(r.row_sums, ROW.gate_t, cot[...].astype(plain) * value * r.vectors[5:6, :])
            out[...] = (after[...] + r.vectors[4:5, :] * value).astype(jnp.bfloat16)

        ins = [by_rows(ref, ROW_TILE) for ref in (r.after_feed, r.returned, r.cotangent)]
        run_tiles(body, r.low.shape[0] // ROW_TILE, ins, [by_rows(r.block_out, ROW_TILE)])

    return types.SimpleNamespace(**locals())


def back_kernel(together, att_scale, names, *refs):
    r = types.SimpleNamespace(**dict(zip(names, refs)))
    if together:
        r.back_sent, r.returned = r.back_sent_cols, r.returned_cols
    do = back_stages(r, att_scale)
    if not together:
        do.clear()
        do.feed_first()
        do.reduce_part()
        do.feed_hidden()
        do.expand_part()
        do.feed_normed()
        do.feed_last()
        do.cross_part()
        do.cross_given()
        do.cross_attention()
        do.query_part()
        do.memory_part()
        do.context_back()
        do.query_back()
        do.spatial_first()
        do.output_part()
        do.spatial_given()
        do.spatial_attention()
        do.input_part()
        do.attend_normed()
        do.attend_last()
        return
    column, frame, depth, core, across_x, across_y, sibling = neighbours()
    far = 3 - column
    frame_peers = [(column, (frame + shift) % 8) for shift in range(1, 8)]
    line_peers = [(column, ((depth + shift) % 4) * 2 + core) for shift in range(1, 4)]
    plane_peers = [(across_x, frame), (across_y, frame), (far, frame)]
    greet(frame_peers + plane_peers)
    copies = Copies(r.send_sems, r.recv_sems)
    talls, bundles = PART_TALLS, len(PART_TALLS)
    cut = lambda ref, *span: ref.at[:, pl.ds(*span)]
    parts = [
        r.part_time,
        r.part_reduce,
        cut(r.part_expand, 0, 3584),
        cut(r.part_expand, 3584, 1024),
        r.part_text,
        cut(r.part_input, 0, 2048),
        cut(r.part_input, 2048, 1536),
    ]
    many = lambda name: [vars(r)[f"{name}_{index}"] for index in range(bundles)]
    paired, halved, quartered, lined = (many(name) for name in LANDING)
    summed, crossed = halved, quartered
    outs = [
        r.share_time,
        r.share_reduce,
        cut(r.share_expand, 0, 3584),
        cut(r.share_expand, 3584, 1024),
        r.share_text,
        cut(r.share_input, 0, 2048),
        cut(r.share_input, 2048, 1536),
    ]

    def part_piece(index, unit, owner):
        return whole_unit(parts[index], talls[index], unit, owner)

    from_core = {}

    def send(index, units=range(4)):
        for slot in range(4):
            owner = slot * 2 + 1 - core
            for unit in units:
                from_core[index, slot, unit] = copies.start(
                    part_piece(index, unit, owner), paired[index].at[unit, slot], (column, sibling)
                )

    def stream(index, count, left_at, right_at, out_at):
        wide = pl.ds(0, paired[index].shape[-1])
        buffers = [ref.at[:, :, wide] for ref in (r.left_buf, r.right_buf, r.out_buf)]
        add_stream(count, left_at, right_at, out_at, *buffers, r.stream_sems)

    from_half, from_quarter, from_line, ends = {}, {}, {}, []

    def pair(index):
        for slot in range(4):
            for unit in range(4):
                from_core[index, slot, unit].wait_recv()
        place = lambda step: paired[index].at[step // 4, step % 4]
        stream(
            index, 16, lambda step: part_piece(index, step // 4, (step % 4) * 2 + core), place, place
        )
        if index == LINE_FIRST:
            for shift in range(1, 4):
                other = (depth + shift) % 4
                for unit in range(4):
                    from_line[index, shift, unit] = copies.start(
                        paired[index].at[unit, other],
                        lined[index].at[shift - 1, unit],
                        (column, other * 2 + core),
                    )
            return
        for slot in range(4):
            near = across_x if slot < 2 else across_y
            for which, unit in enumerate((near, far)):
                from_half[index, slot, which] = copies.start(
                    paired[index].at[unit, slot], halved[index].at[slot, which], (near, frame)
                )

    def half(index):
        for slot in range(4):
            for which in range(2):
                from_half[index, slot, which].wait_recv()

        def source(step):
            slot, which = step // 2, step % 2
            late = slot // 2
            unit = column + which * (
                (1 - late) * (across_y - column) + late * (across_x - column)
            )
            return paired[index].at[unit, slot]

        place = lambda step: halved[index].at[step // 2, step % 2]
        stream(index, 8, source, place, place)
        for slot in range(4):
            near = across_y if slot < 2 else across_x
            from_quarter[index, slot] = copies.start(
                halved[index].at[slot, 1], quartered[index].at[slot], (near, frame)
            )

    def quarter(index):
        for slot in range(4):
            from_quarter[index, slot].wait_recv()
        place = lambda slot: quartered[index].at[slot]
        stream(index, 4, lambda slot: halved[index].at[slot, 0], place, place)
        for shift in range(1, 4):
            other = (depth + shift) % 4
            from_line[index, shift] = copies.start(
                quartered[index].at[other], lined[index].at[shift - 1], (column, other * 2 + core)
            )

    def total_of_four(own, others, target, height, width):
        loads = [
            pltpu.make_async_copy(
                source,
                r.four_buf.at[slot, pl.ds(0, height), pl.ds(0, width)],
                r.stream_sems.at[0, slot],
            )
            for slot, source in enumerate([own] + others)
        ]
        for copy in loads:
            copy.start()
        for copy in loads:
            copy.wait()
        total = r.four_buf[0, 0:height, 0:width].astype(jnp.float32)
        for slot in range(1, 4):
            total = total + r.four_buf[slot, 0:height, 0:width].astype(jnp.float32)
        r.out_buf[0, 0:height, 0:width] = total.astype(jnp.bfloat16)
        copy = pltpu.make_async_copy(
            r.out_buf.at[0, pl.ds(0, height), pl.ds(0, width)], target, r.stream_sems.at[2, 0]
        )
        copy.start()
        copy.wait()

    spread, relayed = {}, []

    def hand_out(index):
        target = share_unit(outs[index], talls[index], column)
        spread[index] = [copies.start(target, target, peer) for peer in plane_peers[:2]]
        if index >= bundles - 2:
            ends.extend(spread[index])
            ends.append(copies.start(target, target, plane_peers[2]))

    def relay(index):
        x_first = index % 2 == 0
        first, second = spread[index] if x_first else spread[index][::-1]
        first.wait_recv()
        target = share_unit(outs[index], talls[index], across_x if x_first else across_y)
        ends.append(copies.start(target, target, plane_peers[1 if x_first else 0]))
        ends.append(second)

    def line_sums():
        index = LINE_FIRST
        for shift in range(1, 4):
            for unit in range(4):
                from_line[index, shift, unit].wait_recv()
        for unit in range(4):
            total_of_four(
                paired[index].at[unit, depth],
                [lined[index].at[slot, unit] for slot in range(3)],
                summed[index].at[unit],
                *paired[index].shape[2:],
            )
        for slot, peer in enumerate(plane_peers):
            from_half[index, slot] = copies.start(
                summed[index].at[peer[0]], crossed[index].at[slot], peer
            )

    def line_last():
        index = LINE_FIRST
        for slot in range(3):
            from_half[index, slot].wait_recv()
        total_of_four(
            summed[index].at[column],
            [crossed[index].at[slot] for slot in range(3)],
            share_unit(outs[index], talls[index], column),
            *paired[index].shape[2:],
        )
        hand_out(index)

    def line(index):
        for shift in range(1, 4):
            from_line[index, shift].wait_recv()
        total_of_four(
            quartered[index].at[depth],
            [lined[index].at[slot] for slot in range(3)],
            share_unit(outs[index], talls[index], column),
            *lined[index].shape[1:],
        )
        hand_out(index)

    contexts, paired_contexts, texts = [], [], []
    text_rows = r.text_part.shape[0] // 4

    def context_send():
        contexts.extend(
            copies.start(r.back_context, r.context_all.at[frame], peer) for peer in line_peers
        )
        paired_contexts.append(
            copies.start(r.back_context, r.context_all.at[frame], (column, sibling))
        )
        move(r.back_context, r.held_context, r.context_all.at[frame])

    def context_pair():
        for shift, copy in zip(range(1, 4), contexts):
            copy.wait_recv()
            place = r.context_all.at[((depth + 4 - shift) % 4) * 2 + core]
            paired_contexts.append(copies.start(place, place, (column, sibling)))

    def text_part():
        for copy in paired_contexts:
            copy.wait_recv()
        each = r.context_all.shape[1]

        def body(text, context, out):
            total = dot_plain(text[:, 0:each], context[0])
            for index in range(1, 8):
                total = total + dot_plain(text[:, index * each : (index + 1) * each], context[index])
            out[...] = total.astype(jnp.bfloat16)

        run_tiles(
            body,
            4,
            [
                by_rows(r.text_turned, text_rows),
                (r.context_all, r.context_all.shape, lambda step: (0, 0, 0)),
            ],
            [by_rows(r.text_part, text_rows)],
        )
        for slot, peer in enumerate(plane_peers):
            texts.append(
                copies.start(
                    rows_at(r.text_part, peer[0] * text_rows, text_rows, text_rows),
                    r.text_got.at[slot],
                    peer,
                )
            )

    def text_line():
        for copy in texts:
            copy.wait_recv()
        total_of_four(
            rows_at(r.text_part, column * text_rows, text_rows, text_rows),
            [r.text_got.at[slot] for slot in range(3)],
            rows_at(r.text_out, column * text_rows, text_rows, text_rows),
            *r.text_got.shape[1:],
        )
        target = rows_at(r.text_out, column * text_rows, text_rows, text_rows)
        for peer in plane_peers:
            ends.append(copies.start(target, target, peer))

    cots_got, back_got, result_got, rows_got, rows_paired = [], [], [], [], []
    here = r.local_sems

    def move(source, held, target):
        load = pltpu.make_async_copy(source, held, here.at[0])
        load.start()
        load.wait()
        store = pltpu.make_async_copy(held, target, here.at[0])
        store.start()
        store.wait()

    def cols_send(source, target, got):
        for peer in frame_peers:
            got.append(copies.start(source.at[peer[1]], target.at[:, frame], peer))
        move(source.at[frame], r.held_cols, target.at[:, frame])

    def return_send(source, target, got):
        for peer in frame_peers:
            got.append(copies.start(source.at[:, peer[1]], target.at[frame], peer))
        move(source.at[:, frame], r.held_cols, target.at[frame])

    def arrive(got):
        for copy in got:
            copy.wait_recv()

    def rows_send():
        for peer in line_peers:
            rows_got.append(copies.start(r.row_sums, r.rows_all.at[frame], peer))
        rows_paired.append(copies.start(r.row_sums, r.rows_all.at[frame], (column, sibling)))
        r.rows_all[frame] = r.row_sums[...]

    def rows_pair():
        for shift, copy in zip(range(1, 4), rows_got):
            copy.wait_recv()
            place = r.rows_all.at[((depth + 4 - shift) % 4) * 2 + core]
            rows_paired.append(copies.start(place, place, (column, sibling)))

    def rows_plane():
        arrive(rows_paired)
        mods = r.rows_all.at[:, pl.ds(0, 8)]
        own = [pltpu.make_async_copy(mods, r.mods_out.at[column], here.at[0])]
        for peer in plane_peers:
            ends.append(copies.start(mods, r.mods_out.at[column], peer))
        r.sums[...] = jnp.sum(r.rows_all[:, 8:, :], axis=0)
        own.append(pltpu.make_async_copy(r.sums, r.sums_out.at[column], here.at[1]))
        for copy in own:
            copy.start()
        for peer in plane_peers:
            ends.append(copies.start(r.sums, r.sums_out.at[column], peer))
        for copy in own:
            copy.wait()

    cols_send(r.cot_rows, r.cot_cols, cots_got)
    do.clear()
    r.row_sums[ROW.condition : ROW.condition + 1, :] = r.vectors[6:7, :]
    do.time_first()
    do.time_heads()
    do.time_attention()
    arrive(cots_got)
    do.time_given()
    do.time_attention_back()
    do.time_normed()
    do.time_last()
    return_send(r.time_back, r.back_sent_cols, back_got)
    do.time_in_part()
    do.time_out_part()
    send(0)
    do.time_result()
    arrive(back_got)
    return_send(r.time_result, r.returned_cols, result_got)
    do.feed_first()
    pair(0)
    do.reduce_part()
    send(1)
    do.feed_hidden()
    pair(1)
    half(0)
    do.expand_part()
    send(2)
    send(3)
    do.feed_normed()
    pair(2)
    pair(3)
    do.feed_last()
    half(1)
    do.cross_part()
    do.cross_given()
    quarter(0)
    arrive(result_got)
    do.block_last()
    do.cross_attention()
    half(2)
    line_sums()
    line(0)
    quarter(1)
    do.query_part()
    do.memory_part()
    do.context_back()
    context_send()
    do.query_back()
    do.spatial_first()
    do.output_part()
    send(4)
    relay(0)
    line(1)
    line_last()
    quarter(2)
    do.spatial_given()
    pair(4)
    do.spatial_attention()
    context_pair()
    relay(1)
    line(2)
    half(4)
    do.input_part(0, 4)
    send(5)
    do.input_part(4, 3)
    send(6)
    text_part()
    relay(3)
    quarter(4)
    pair(5)
    pair(6)
    do.attend_normed()
    do.attend_last()
    rows_send()
    relay(2)
    half(5)
    half(6)
    rows_pair()
    text_line()
    line(4)
    quarter(5)
    quarter(6)
    rows_plane()
    relay(4)
    line(5)
    line(6)
    for copy in ends:
        copy.wait_recv()
    copies.finish()


LANDING = ("paired", "halved", "quartered", "lined")
PART_TALLS = (False, True, False, False, False, False, False)
LINE_FIRST = 3


def backward(att_scale, together, o, text_turned):
    anywhere = pl.BlockSpec(memory_space=pl.ANY)
    inside = pl.BlockSpec(memory_space=pltpu.VMEM)
    tokens, width = o.cotangent.shape
    hidden = o.gelu_slope.shape[1]
    text_count = o.cross_keys.shape[1]
    low, full = jnp.bfloat16, jnp.float32
    shape = jax.ShapeDtypeStruct
    third = width // 3
    hbm_out = dict(
        part_reduce=shape((hidden, width), low),
        part_expand=shape((width, hidden), low),
        part_text=shape((width, 5 * width + third), low),
        part_input=shape((width, 3 * width + LANES), low),
        back_context=shape((text_count, width), low),
        tokens_out=shape((tokens, width), low),
    )
    scratch = dict(
        running=pltpu.VMEM((tokens, width), full),
        wide=pltpu.VMEM((tokens, width), full),
        low=pltpu.VMEM((tokens, width), low),
        broad=pltpu.VMEM((tokens, hidden), low),
        head_in=pltpu.VMEM((HEADS, tokens, HEAD_LANES), low),
        head_query=pltpu.VMEM((HEADS, tokens, HEAD_LANES), low),
        head_key=pltpu.VMEM((HEADS, tokens, HEAD_LANES), low),
        head_value=pltpu.VMEM((HEADS, tokens, HEAD_LANES), low),
        cross_key=pltpu.VMEM((HEADS, text_count, HEAD_LANES), low),
        cross_value=pltpu.VMEM((HEADS, text_count, HEAD_LANES), low),
        memory=pltpu.VMEM((text_count, 2 * width), low),
    )
    hbm_in = dict(
        whole_spatial=o.whole_spatial,
        whole_text=o.whole_text,
        whole_expand=o.whole_expand,
        whole_reduce=o.whole_reduce,
        cotangent=o.cotangent,
        branch_feed=o.branch_feed,
        hidden_turned=o.hidden_turned,
        gelu_slope=o.gelu_slope,
        feed_turned=o.feed_turned,
        feed_normal=o.feed_normal,
        cross_turned=o.cross_turned,
        cross_queries=o.cross_queries,
        cross_keys=o.cross_keys,
        cross_values=o.cross_values,
        after_turned=o.after_turned,
        context_turned=o.context_turned,
        branch_attend=o.branch_attend,
        spatial_turned=o.spatial_turned,
        queries=o.queries,
        keys=o.keys,
        values=o.values,
        attend_turned=o.attend_turned,
        attend_normal=o.attend_normal,
    )
    vmem_in = dict(
        mods=o.mods,
        feed_rate=o.feed_rate,
        attend_rate=o.attend_rate,
        cross_logsum=o.cross_logsum,
        spatial_logsum=o.spatial_logsum,
        text_mask=o.text_mask,
    )
    if not together:
        hbm_in.update(back_sent=o.back_sent)
    vmem_out = dict(row_sums=shape((ROW.high, width), full))
    if together:
        hbm_in.update(
            time_cols=o.time_cols,
            cot_rows=o.cot_rows,
            whole_time=o.whole_time,
            after_feed=o.after_feed,
            text_turned=text_turned,
        )
        vmem_in.update(vectors=o.vectors, time_keep=o.time_keep, time_mask=o.time_mask)
        rows = o.cot_rows.shape
        cols = (rows[1], rows[0]) + rows[2:]
        hbm_out.update(cot_cols=shape(cols, low))
        hbm_out.update(part_time=shape((width, 4 * width), low))
        hbm_out.update(time_result=shape(cols, low))
        hbm_out.update(time_back=shape(cols, low))
        hbm_out.update(back_sent_cols=shape(rows, low))
        hbm_out.update(returned_cols=shape(rows, low))
        hbm_out.update(block_out=shape((tokens, width), low))
        hbm_out.update(mods_out=shape((4, 8, 8, width), full))
        hbm_out.update(sums_out=shape((4, ROW.high - 8, width), full))
        high = width // 8
        wides = (width, width, 896, 256, width + third, 512, 384)
        high = width // 8
        for index, wide in enumerate(wides):
            piece = (high, wide)
            first = index == LINE_FIRST
            landing = [(4, 4), (4,) if first else (4, 2), (4,), (3, 4) if first else (3,)]
            for name, lead in zip(LANDING, landing):
                hbm_out[f"{name}_{index}"] = shape(lead + piece, low)
        hbm_out.update(
            share_time=shape((high, 4 * width), low),
            share_reduce=shape((4 * high, width), low),
            share_expand=shape((high, 4 * width), low),
            share_text=shape((high, 5 * width + third), low),
            share_input=shape((high, 3 * width + LANES), low),
        )
        text_shape = (text_turned.shape[0], width)
        hbm_out.update(context_all=shape((8, text_count, width), low))
        hbm_out.update(text_part=shape(text_shape, low))
        hbm_out.update(text_got=shape((3, text_shape[0] // 4, width), low))
        hbm_out.update(text_out=shape(text_shape, low))
        remote = len(PART_TALLS) * (16 + 8 + 4 + 3 + 3) + 7 + 3 + 3 + 4 * 7 + 6
        piece = (high, width + third)
        scratch.update(
            send_sems=pltpu.SemaphoreType.DMA((remote,)),
            recv_sems=pltpu.SemaphoreType.DMA((remote,)),
            stream_sems=pltpu.SemaphoreType.DMA((3, PIECE_SLOTS)),
            local_sems=pltpu.SemaphoreType.DMA((2,)),
            left_buf=pltpu.VMEM((PIECE_SLOTS,) + piece, low),
            right_buf=pltpu.VMEM((PIECE_SLOTS,) + piece, low),
            out_buf=pltpu.VMEM((PIECE_SLOTS,) + piece, low),
            four_buf=pltpu.VMEM((4,) + piece, low),
            rows_all=pltpu.VMEM((8, ROW.high, width), full),
            sums=pltpu.VMEM((ROW.high - 8, width), full),
            time_normal=pltpu.VMEM((tokens, width), low),
            time_rate=pltpu.VMEM((tokens, LANES), full),
            time_turned=pltpu.VMEM((width, tokens), low),
            time_logsum=pltpu.VMEM((HEADS, 8, tokens), full),
            held_cols=pltpu.VMEM((cols[0],) + cols[2:], low),
            held_context=pltpu.VMEM((text_count, width), low),
            middle=pltpu.VMEM((tokens, width), low),
            middle_turned=pltpu.VMEM((width, tokens), low),
        )
    names = list(hbm_in) + list(vmem_in) + list(hbm_out) + list(vmem_out) + list(scratch)
    results = pl.pallas_call(
        functools.partial(back_kernel, together, att_scale, names),
        out_shape=list(hbm_out.values()) + list(vmem_out.values()),
        in_specs=[anywhere] * len(hbm_in) + [inside] * len(vmem_in),
        out_specs=[anywhere] * len(hbm_out) + [inside] * len(vmem_out),
        scratch_shapes=list(scratch.values()),
        compiler_params=pltpu.CompilerParams(
            collective_id=1 if together else None,
            has_side_effects=True,
            vmem_limit_bytes=60 * 1024 * 1024,
        ),
        name="backward",
    )(*hbm_in.values(), *vmem_in.values())
    return types.SimpleNamespace(**dict(zip(list(hbm_out) + list(vmem_out), results)))


def one_slice():
    return lax.axis_size("clip") == 4 and lax.axis_size("frame") == 8


def sum_shares(group):
    def total(part):
        return lax.psum(lax.psum_scatter(part, "frame", scatter_dimension=0, tiled=True), "clip")

    return jnp.concatenate([total(part) for part in group], axis=1)


FORWARD_TALLS = (False, True, False, False, True, False)
VEC = types.SimpleNamespace(
    spatial=0, cross=1, reduce=2, gain=3, shift=4, temporal=5, gate=6, expand=7, high=16
)


def forward_stages(r, att_scale):
    tokens, width = r.low.shape
    head_size = width // HEADS
    third = width // 3
    tile = tokens // 4
    plain = jnp.float32
    row = lambda which: r.rows_low[which : which + 1, :]

    def clear():
        for heads in (r.head_query, r.head_key, r.head_value, r.cross_key, r.cross_value):
            heads[...] = jnp.zeros_like(heads)

    def sum_mods():
        r.mods[...] = jnp.sum(r.mods_got[...], axis=0)

    def sum_rows():
        r.rows_low[...] = jnp.sum(r.rows_got[...].astype(plain), axis=0)
        for unit in range(4):
            r.rows_expand[0:1, unit * width : (unit + 1) * width] = row(VEC.expand + unit)

    def turn_out(source, target):
        height = source.shape[0] // target.shape[1] * LANES

        def body(out):
            rows = tile_rows(pl.program_id(0), LANES)
            out[...] = source[rows, :].astype(plain).T.astype(jnp.bfloat16)

        run_tiles(body, target.shape[1] // LANES, [], [by_columns(target, LANES)])

    def normed(values, rate_out, rows, shift, scale):
        values = values - jnp.mean(values, axis=1, keepdims=True)
        rate = lax.rsqrt(jnp.mean(values * values, axis=1, keepdims=True) + eps_norm)
        normal = values * rate
        rate_out[rows, :] = jnp.broadcast_to(rate, (tile, LANES))
        shift, scale = (r.mods[which : which + 1, :] for which in (shift, scale))
        r.low[rows, :] = (normal * (1.0 + scale) + shift).astype(jnp.bfloat16)
        return normal.astype(jnp.bfloat16)

    def attend_first():
        def body(latents, out):
            rows = tile_rows(pl.program_id(0), tile)
            values = latents[...].astype(plain)
            out[...] = normed(values, r.attend_rate, rows, ROW.shift_a, ROW.scale_a)

        run_tiles(body, 4, [by_rows(r.latents, tile)], [by_rows(r.attend_normal, tile)])
        turn_out(r.low, r.attend_turned)

    def through(weight, place, count, left, target, size=third):
        def body(block):
            columns = tile_rows(pl.program_id(0), size)
            target(columns, dot_plain(left(), block[...]))

        high = weight.shape[0]
        run_tiles(body, count, [(weight, (high, size), lambda step: (0, place + step))], [])

    def set_broad(columns, value):
        r.broad[:, columns] = value.astype(jnp.bfloat16)

    def set_memory(columns, value):
        r.memory[:, columns] = value.astype(jnp.bfloat16)

    def attend_heads():
        through(r.whole_spatial, 0, 9, lambda: r.low[...], set_broad)
        for place, heads in enumerate((r.head_query, r.head_key, r.head_value)):
            split_heads(r.broad, place * width, heads, head_size, HEADS)

    def attention(queries, keys, values, mask, logsum, outs, first=0, last=HEADS):
        def step(head, carry):
            query, key, value = queries[head], keys[head], values[head]
            scores = dot_rows(key, query) * att_scale
            if mask is not None:
                scores = scores + mask[:, 0:1]
            largest = jnp.max(scores, axis=0, keepdims=True)
            total = jnp.sum(jnp.exp(scores - largest), axis=0, keepdims=True)
            logs = largest + jnp.log(total)
            logsum[head, 0:1, :] = logs
            weights = jnp.exp(scores - logs).astype(jnp.bfloat16)
            turned = lax.dot_general(
                value, weights, (((0,), (0,)), ((), ())), preferred_element_type=plain
            )
            outs[head] = turned.T.astype(jnp.bfloat16)
            return carry

        lax.fori_loop(first, last, step, 0)

    def attend_attention(half):
        attention(
            r.head_query,
            r.head_key,
            r.head_value,
            None,
            r.spatial_logsum,
            r.head_out,
            half * HEADS // 2,
            (half + 1) * HEADS // 2,
        )

    def attend_merge():
        merge_heads(r.head_out, r.middle, 0, head_size, HEADS)
        turn_out(r.middle, r.spatial_turned)

    def attend_last():
        def body(weight, latents, branch):
            columns = tile_rows(pl.program_id(0), third)
            value = dot_plain(r.middle[...], weight[...])
            value = value + r.rows_low[VEC.spatial : VEC.spatial + 1, columns]
            branch[...] = value.astype(jnp.bfloat16)
            after = latents[...].astype(plain)
            after = after + r.mods[ROW.gate_a : ROW.gate_a + 1, columns] * value
            r.running[:, columns] = after
            r.low[:, columns] = after.astype(jnp.bfloat16)

        run_tiles(
            body,
            3,
            [
                (r.whole_spatial, (width, third), lambda step: (0, 9 + step)),
                by_columns(r.latents, third),
            ],
            [by_columns(r.branch_attend, third)],
        )
        turn_out(r.low, r.after_turned)

    def context():
        def body(weight):
            columns = tile_rows(pl.program_id(0), third)
            r.context[:, columns] = dot_plain(r.own_text[...], weight[...]).astype(jnp.bfloat16)

        run_tiles(body, 3, [by_columns(r.whole_context, third)], [])
        turn_out(r.context, r.context_turned)

    def cross_heads():
        through(r.whole_text, 3, 6, lambda: r.context[...], set_memory)
        split_heads(r.memory, 0, r.cross_key, head_size, HEADS)
        split_heads(r.memory, width, r.cross_value, head_size, HEADS)
        through(r.whole_text, 0, 3, lambda: r.low[...], set_broad)
        split_heads(r.broad, 0, r.cross_query, head_size, HEADS)

    def cross_attention():
        attention(
            r.cross_query, r.cross_key, r.cross_value, r.text_mask, r.cross_logsum, r.head_out
        )
        merge_heads(r.head_out, r.middle, 0, head_size, HEADS)
        turn_out(r.middle, r.cross_turned)

    def add_cross(columns, value):
        r.running[:, columns] += value + r.rows_low[VEC.cross : VEC.cross + 1, columns]

    def cross_last():
        through(r.whole_text, 9, 3, lambda: r.middle[...], add_cross)

    def feed_first():
        def body(out):
            rows = tile_rows(pl.program_id(0), tile)
            out[...] = normed(r.running[rows, :], r.feed_rate, rows, ROW.shift_m, ROW.scale_m)

        run_tiles(body, 4, [], [by_rows(r.feed_normal, tile)])
        turn_out(r.low, r.feed_turned)

    def feed_hidden():
        size = 512

        def body(weight, slope, turned):
            columns = tile_rows(pl.program_id(0), size)
            values = dot_plain(r.low[...], weight[...]) + r.rows_expand[0:1, columns]
            inner = math.sqrt(2.0 / math.pi)
            square = values * values
            bent = jnp.tanh(inner * values * (1.0 + 0.044715 * square))
            half = 0.5 * (1.0 + bent)
            hidden = values * half
            steep = inner * (1.0 + 3.0 * 0.044715 * square)
            slope[...] = (half + 0.5 * values * (1.0 - bent * bent) * steep).astype(jnp.bfloat16)
            r.broad[:, columns] = hidden.astype(jnp.bfloat16)
            turned[...] = hidden.T.astype(jnp.bfloat16)

        run_tiles(
            body,
            r.broad.shape[1] // size,
            [by_columns(r.whole_expand, size)],
            [by_columns(r.gelu_slope, size), by_rows(r.hidden_turned, size)],
        )

    def feed_last():
        def body(weight, branch, after, sent):
            columns = tile_rows(pl.program_id(0), third)
            value = dot_plain(r.broad[...], weight[...])
            value = value + r.rows_low[VEC.reduce : VEC.reduce + 1, columns]
            branch[...] = value.astype(jnp.bfloat16)
            value = r.running[:, columns] + r.mods[ROW.gate_m : ROW.gate_m + 1, columns] * value
            after[...] = value
            sent[...] = value.astype(jnp.bfloat16).reshape(sent.shape)

        shape = r.sent.shape
        run_tiles(
            body,
            3,
            [by_columns(r.whole_reduce, third)],
            [
                by_columns(r.branch_feed, third),
                by_columns(r.after_feed, third),
                (r.sent, shape[:3] + (third,), lambda step: (0, 0, 0, step)),
            ],
        )

    return types.SimpleNamespace(**locals())


def forward_kernel(att_scale, names, *refs):
    r = types.SimpleNamespace(**dict(zip(names, refs)))
    r.held = [
        r.held_spatial, r.held_context, r.held_text, r.held_expand, r.held_reduce, r.held_time
    ]
    do = forward_stages(r, att_scale)
    shares = [
        r.share_spatial, r.share_context, r.share_text, r.share_expand, r.share_reduce, r.share_time
    ]
    wholes = [
        r.whole_spatial, r.whole_context, r.whole_text, r.whole_expand, r.whole_reduce, r.whole_time
    ]
    talls, count = FORWARD_TALLS, len(FORWARD_TALLS)
    column, frame, depth, core, across_x, across_y, sibling = neighbours()
    frame_peers = [(column, (frame + shift) % 8) for shift in range(1, 8)]
    greet(frame_peers + [(across_x, frame), (across_y, frame)])
    copies = Copies(r.send_sems, r.recv_sems)
    locals_started = []

    def local(source, target):
        copy = pltpu.make_async_copy(source, target, r.local_sems.at[len(locals_started)])
        copy.start()
        locals_started.append(copy)
        return copy

    mods, rows, arrivals = [], [], {index: [] for index in range(count)}
    from_x, from_y, from_far, own_place = {}, {}, {}, {}

    def send_mods():
        own = local(r.mod_parts.at[frame], r.mods_got.at[frame])
        for peer in frame_peers:
            mods.append(copies.start(r.mod_parts.at[peer[1]], r.mods_got.at[frame], peer))
        own.wait()

    def send_rows():
        own = local(r.row_parts, r.rows_got.at[frame])
        for peer in frame_peers:
            rows.append(copies.start(r.row_parts, r.rows_got.at[frame], peer))
        own.wait()

    def send(index):
        share, whole, tall = shares[index], wholes[index], talls[index]
        own = whole_share(whole, tall, frame)
        held = r.held[index]
        load = local(share, held)
        arrivals[index].append(copies.start(share, own, (column, sibling)))
        own_place[index] = (load, held, own)

    def place(index):
        load, held, own = own_place[index]
        load.wait()
        own_place[index] = local(held, own)

    order = (
        jnp.where(depth == 0, 3, 1),
        jnp.where((depth == 0) | (depth == 3), 2, 3),
        jnp.where(depth == 0, 1, jnp.where(depth == 3, 3, 2)),
    )

    def next_frame(step):
        return jnp.clip(depth + step, 0, 3) * 2 + core

    def send_depth(index):
        share, whole, tall = shares[index], wholes[index], talls[index]
        source = share_unit(share, tall, column)
        target = whole_unit(whole, tall, column, frame)
        for step, shift in ((1, 1), (-1, 3)):
            copies.start_if(
                (depth < 3) if step == 1 else (depth > 0),
                source,
                target,
                (column, next_frame(step)),
                r.depth_sems.at[index, shift],
            )

    def pass_depth(index, shift):
        source = ((depth + 4 - shift) % 4) * 2 + core
        piece = whole_unit(wholes[index], talls[index], column, source)
        copies.start_if(
            (depth >= shift) & (depth < 3),
            piece,
            piece,
            (column, next_frame(1)),
            r.depth_sems.at[index, (shift + 1) % 4],
        )
        copies.start_if(
            (depth < shift) & (depth > 0),
            piece,
            piece,
            (column, next_frame(-1)),
            r.depth_sems.at[index, shift - 1],
        )

    def wait_depth(index, shift):
        source = ((depth + 4 - shift) % 4) * 2 + core
        piece = whole_unit(wholes[index], talls[index], column, source)
        pltpu.make_async_remote_copy(
            src_ref=piece,
            dst_ref=piece,
            send_sem=r.send_sems.at[0],
            recv_sem=r.depth_sems.at[index, shift],
            device_id=(column, sibling),
            device_id_type=MESH_ID,
        ).wait_recv()

    def pass_on(index, turn, unit, device):
        source = ((depth + 4 - order[turn]) % 4) * 2 + core
        piece = whole_unit(wholes[index], talls[index], unit, source)
        return copies.start(piece, piece, device)

    def first(index, turns=(0, 1, 2)):
        for turn in turns:
            wait_depth(index, order[turn])
            pass_depth(index, order[turn])
            from_x[index, turn] = pass_on(index, turn, column, (across_x, frame))
            from_y[index, turn] = pass_on(index, turn, column, (across_y, frame))
            arrivals[index].append(pass_on(index, turn, column, (column, sibling)))
        if index + 2 < count and turns[-1] == 2:
            send(index + 2)
            send_depth(index + 2)

    def second(index):
        for turn in range(3):
            x_first = (index + turn) % 2 == 0
            from_x[index, turn].wait_recv()
            if x_first:
                from_far[index, turn] = pass_on(index, turn, across_x, (across_y, frame))
            arrivals[index].append(pass_on(index, turn, across_x, (column, sibling)))
            from_y[index, turn].wait_recv()
            if not x_first:
                from_far[index, turn] = pass_on(index, turn, across_y, (across_x, frame))
            arrivals[index].append(pass_on(index, turn, across_y, (column, sibling)))

    def third(index):
        for turn in range(3):
            from_far[index, turn].wait_recv()
            arrivals[index].append(pass_on(index, turn, 3 - column, (column, sibling)))

    def ready(index):
        place(index)
        for copy in arrivals[index]:
            copy.wait_recv()
        own_place[index].wait()

    def arrive(got):
        for copy in got:
            copy.wait_recv()

    send_mods()
    for index in (0, 1):
        send(index)
        send_depth(index)
    do.clear()
    arrive(mods)
    do.sum_mods()
    do.attend_first()
    first(0)
    send_rows()
    second(0)
    first(1)
    third(0)
    ready(0)
    do.attend_heads()
    kept = [
        local(r.head_query, r.queries),
        local(r.head_key, r.keys),
        local(r.head_value, r.values),
    ]
    second(1)
    first(2, (0, 1))
    do.attend_attention(0)
    third(1)
    first(2, (2,))
    do.attend_attention(1)
    do.attend_merge()
    first(3, (0, 1))
    second(2)
    arrive(rows)
    do.sum_rows()
    do.attend_last()
    first(3, (2,))
    third(2)
    ready(1)
    do.context()
    second(3)
    ready(2)
    do.cross_heads()
    kept += [
        local(r.cross_query, r.cross_queries),
        local(r.cross_key, r.cross_keys),
        local(r.cross_value, r.cross_values),
    ]
    first(4, (0, 1))
    third(3)
    do.cross_attention()
    first(4, (2,))
    second(4)
    do.cross_last()
    do.feed_first()
    first(5, (0, 1))
    ready(3)
    do.feed_hidden()
    third(4)
    first(5, (2,))
    ready(4)
    do.feed_last()
    cols = []
    own = local(r.sent.at[frame], r.held_cols)
    for peer in frame_peers:
        cols.append(copies.start(r.sent.at[peer[1]], r.time_cols.at[:, frame], peer))
    own.wait()
    own = local(r.held_cols, r.time_cols.at[:, frame])
    second(5)
    third(5)
    ready(5)
    arrive(cols)
    own.wait()
    copies.finish()
    for copy in kept:
        copy.wait()


def forward(att_scale, o):
    anywhere = pl.BlockSpec(memory_space=pl.ANY)
    inside = pl.BlockSpec(memory_space=pltpu.VMEM)
    tokens, width = o.latents.shape
    text_count = o.own_text.shape[0]
    hidden = 4 * width
    low, full = jnp.bfloat16, jnp.float32
    shape = jax.ShapeDtypeStruct
    hbm_in = dict(
        share_spatial=o.share_spatial,
        share_context=o.share_context,
        share_text=o.share_text,
        share_expand=o.share_expand,
        share_reduce=o.share_reduce,
        share_time=o.share_time,
        latents=o.latents,
        mod_parts=o.mod_parts,
        row_parts=o.row_parts,
    )
    vmem_in = dict(own_text=o.own_text, text_mask=o.text_mask)
    heads = (HEADS, tokens, HEAD_LANES)
    text_heads = (HEADS, text_count, HEAD_LANES)
    whole = lambda share: shape((8 * share.shape[0], share.shape[1]), low)
    hbm_out = dict(
        whole_spatial=whole(o.share_spatial),
        whole_context=whole(o.share_context),
        whole_text=whole(o.share_text),
        whole_expand=whole(o.share_expand),
        whole_reduce=whole(o.share_reduce),
        whole_time=whole(o.share_time),
    )
    hbm_out.update(
        attend_normal=shape((tokens, width), low),
        attend_turned=shape((width, tokens), low),
        queries=shape(heads, low),
        keys=shape(heads, low),
        values=shape(heads, low),
        spatial_turned=shape((width, tokens), low),
        branch_attend=shape((tokens, width), low),
        after_turned=shape((width, tokens), low),
        context_turned=shape((width, text_count), low),
        cross_queries=shape(heads, low),
        cross_keys=shape(text_heads, low),
        cross_values=shape(text_heads, low),
        cross_turned=shape((width, tokens), low),
        feed_normal=shape((tokens, width), low),
        feed_turned=shape((width, tokens), low),
        gelu_slope=shape((tokens, hidden), low),
        hidden_turned=shape((hidden, tokens), low),
        branch_feed=shape((tokens, width), low),
        after_feed=shape((tokens, width), full),
        sent=shape((8, tokens // (8 * 16), 16, width), low),
        time_cols=shape((tokens // (8 * 16), 8, 16, width), low),
    )
    vmem_out = dict(
        mods=shape((8, width), full),
        rows_low=shape((VEC.high, width), full),
        attend_rate=shape((tokens, LANES), full),
        feed_rate=shape((tokens, LANES), full),
        spatial_logsum=shape((HEADS, 8, tokens), full),
        cross_logsum=shape((HEADS, 8, tokens), full),
    )
    remote = 21 + len(FORWARD_TALLS) * 30
    held = lambda share: pltpu.VMEM(share.shape, low)
    scratch = dict(
        running=pltpu.VMEM((tokens, width), full),
        low=pltpu.VMEM((tokens, width), low),
        middle=pltpu.VMEM((tokens, width), low),
        broad=pltpu.VMEM((tokens, hidden), low),
        head_query=pltpu.VMEM(heads, low),
        head_key=pltpu.VMEM(heads, low),
        head_value=pltpu.VMEM(heads, low),
        head_out=pltpu.VMEM(heads, low),
        cross_query=pltpu.VMEM(heads, low),
        cross_key=pltpu.VMEM(text_heads, low),
        cross_value=pltpu.VMEM(text_heads, low),
        memory=pltpu.VMEM((text_count, 2 * width), low),
        context=pltpu.VMEM((text_count, width), low),
        rows_expand=pltpu.VMEM((8, hidden), full),
        held_spatial=held(o.share_spatial),
        held_context=held(o.share_context),
        held_text=held(o.share_text),
        held_expand=held(o.share_expand),
        held_reduce=held(o.share_reduce),
        held_time=held(o.share_time),
        held_cols=pltpu.VMEM((tokens // (8 * 16), 16, width), low),
        mods_got=pltpu.VMEM((8, 8, width), full),
        rows_got=pltpu.VMEM((8, VEC.high, width), low),
        send_sems=pltpu.SemaphoreType.DMA((remote,)),
        recv_sems=pltpu.SemaphoreType.DMA((remote,)),
        depth_sems=pltpu.SemaphoreType.DMA((len(FORWARD_TALLS), 4)),
        local_sems=pltpu.SemaphoreType.DMA((4 + 2 * len(FORWARD_TALLS) + 6,)),
    )
    names = list(hbm_in) + list(vmem_in) + list(hbm_out) + list(vmem_out) + list(scratch)
    results = pl.pallas_call(
        functools.partial(forward_kernel, att_scale, names),
        out_shape=list(hbm_out.values()) + list(vmem_out.values()),
        in_specs=[anywhere] * len(hbm_in) + [inside] * len(vmem_in),
        out_specs=[anywhere] * len(hbm_out) + [inside] * len(vmem_out),
        scratch_shapes=list(scratch.values()),
        compiler_params=pltpu.CompilerParams(
            collective_id=0, has_side_effects=True, vmem_limit_bytes=60 * 1024 * 1024
        ),
        name="forward",
    )(*hbm_in.values(), *vmem_in.values())
    return types.SimpleNamespace(**dict(zip(list(hbm_out) + list(vmem_out), results)))


def pack_rows(parts, rows):
    flat = jnp.concatenate(parts, axis=-1)
    flat = jnp.pad(flat, [(0, 0)] * (flat.ndim - 1) + [(0, rows * LANES - flat.shape[-1])])
    return flat.reshape(flat.shape[:-1] + (rows, LANES))


def results(
    block_output, input_gradient, mods, sums, totals, text_total, frame_index, row_count, bias_width
):
    model_width = mods.shape[-1]
    high = lambda part: part.astype(jnp.float32)
    total_time, total_reduce, total_expand, total_text, total_spatial = totals
    rows_gradient = mods[:, :6].reshape(-1, 6 * model_width)
    rows_condition = lax.dynamic_slice_in_dim(
        mods[:, ROW.condition], frame_index * row_count, row_count, 1
    )
    back_modulation_weight = jnp.einsum(
        "nd,ne->de", rows_condition, rows_gradient, precision=lax.Precision.HIGHEST
    )
    back_modulation_bias = jnp.sum(
        lax.dynamic_slice_in_dim(rows_gradient, frame_index * bias_width, bias_width, 1), axis=0
    )
    own_rows = lax.dynamic_slice_in_dim(sums, frame_index * row_count, row_count, 1)
    own_row = lambda which: own_rows[which - 8]
    own_expand = lax.dynamic_slice_in_dim(
        sums[ROW.expand - 8 : ROW.expand - 4].reshape(-1), frame_index * 4 * row_count, 4 * row_count, 0
    )
    own_gate = lax.dynamic_slice_in_dim(
        jnp.sum(mods[:, ROW.gate_t], axis=0), frame_index * row_count, row_count, 0
    )
    vec_total = (
        own_row(ROW.spatial),
        own_row(ROW.cross),
        own_expand,
        own_row(ROW.reduce),
        own_row(ROW.gain),
        own_row(ROW.shift),
        own_row(ROW.temporal),
        own_gate,
    )
    matrix_totals = (
        high(total_spatial[:, : 3 * model_width]),
        high(total_text[:, 4 * model_width : 5 * model_width]),
        high(total_text[:, :model_width]),
        high(total_text[:, model_width : 3 * model_width]),
        high(total_text[:, 3 * model_width : 4 * model_width]),
        high(total_expand),
        high(total_reduce),
        high(total_time[:, : 3 * model_width]),
        high(total_time[:, 3 * model_width :]),
    )
    others = (back_modulation_weight, back_modulation_bias, high(text_total)) + tuple(vec_total)
    return (
        block_output,
        input_gradient,
        others[0],
        others[1],
        matrix_totals[0],
        matrix_totals[1],
        others[3],
        others[2],
        matrix_totals[2],
        matrix_totals[3],
        matrix_totals[4],
        others[4],
        matrix_totals[5],
        others[5],
        matrix_totals[6],
        others[6],
        others[7],
        others[8],
        matrix_totals[7],
        matrix_totals[8],
        others[9],
        others[10],
    )


def on_device(
    latents,
    cotangent,
    text_tokens,
    text_lengths,
    clip_frames,
    timesteps,
    motion_free,
    modulation_weight,
    modulation_bias,
    spatial_input,
    spatial_output,
    spatial_bias,
    text_projection,
    cross_query,
    cross_memory,
    cross_output,
    cross_bias,
    expand_weight,
    expand_bias,
    reduce_weight,
    reduce_bias,
    temporal_gain,
    temporal_shift,
    temporal_input,
    temporal_output,
    temporal_bias,
    temporal_gate,
):
    frame_count = lax.axis_size("frame")
    frame_index = lax.axis_index("frame")
    patch_count = latents.shape[2]
    model_width = latents.shape[3]
    head_size = model_width // HEADS
    att_scale = 1.0 / math.sqrt(head_size)
    slot_count = clip_frames.shape[1]
    text_count = text_tokens.shape[2]
    frame_ids = jnp.arange(frame_count, dtype=jnp.int32)
    clip_ids = assign_clips(clip_frames[0], frame_count)
    slot_ids = jnp.arange(slot_count, dtype=jnp.int32)
    own_clip = jnp.sum(jnp.where(frame_ids == frame_index, clip_ids, 0))
    own_onehot = (slot_ids == own_clip).astype(jnp.float32)
    own_keep = 1.0 - jnp.sum(jnp.where(slot_ids == own_clip, motion_free[0], 0)).astype(jnp.float32)
    own_length = jnp.sum(jnp.where(slot_ids == own_clip, text_lengths[0], 0))
    conditioning = embed_time(timesteps[0], model_width).astype(jnp.bfloat16)
    row_count = modulation_weight.shape[0]
    cond_rows = lax.dynamic_slice_in_dim(conditioning, frame_index * row_count, row_count, 1)
    bias_width = modulation_bias.shape[0]
    bias_placed = lax.dynamic_update_slice_in_dim(
        jnp.zeros((6 * model_width,), jnp.float32),
        modulation_bias.astype(jnp.float32),
        frame_index * bias_width,
        0,
    )
    modulation_part = (
        jnp.dot(cond_rows, modulation_weight, preferred_element_type=jnp.float32)
        + bias_placed[None, :]
    )
    share_rows = text_projection.shape[0]
    if one_slice():
        near = 16
        text_high = -(-text_count // LANES) * LANES
        frame_onehot = (clip_ids[:, None] == slot_ids[None, :]).astype(jnp.float32)
        frame_modulation = jnp.sum(frame_onehot[:, :, None] * modulation_part[None], axis=1)
        frame_modulation = frame_modulation.reshape(frame_count, 6, model_width)
        here = (frame_ids == frame_index).astype(jnp.bfloat16)
        shares = jnp.stack(
            [
                spatial_bias,
                cross_bias,
                reduce_bias,
                temporal_gain,
                temporal_shift,
                temporal_bias,
                temporal_gate,
            ]
        )
        row_parts = jnp.concatenate(
            [
                (shares[:, None] * here[None, :, None]).reshape(-1, model_width),
                (expand_bias[None] * here[:, None]).reshape(-1, model_width),
            ]
        )
        own_text = lax.dynamic_index_in_dim(text_tokens[0], own_clip, 0, keepdims=False)
        text_places = jnp.arange(text_high, dtype=jnp.int32) < own_length
        tokens = latents[0, 0]
        operands = dict(
            share_spatial=jnp.concatenate([spatial_input, spatial_output], axis=1),
            share_context=text_projection,
            share_text=jnp.concatenate([cross_query, cross_memory, cross_output], axis=1),
            share_expand=expand_weight,
            share_reduce=reduce_weight,
            share_time=jnp.concatenate([temporal_input, temporal_output], axis=1),
            latents=tokens,
            mod_parts=jnp.pad(frame_modulation, ((0, 0), (0, 2), (0, 0))),
            row_parts=jnp.pad(row_parts, ((0, VEC.high - row_parts.shape[0]), (0, 0))),
            own_text=jnp.pad(own_text, ((0, text_high - text_count), (0, 0))),
            text_mask=jnp.broadcast_to(
                jnp.where(text_places, 0.0, big_negative)[:, None], (text_high, LANES)
            ),
        )
        operands = types.SimpleNamespace(**operands)
        vars(operands).update(vars(forward(att_scale, operands)))
        keep_frames = 1.0 - jnp.sum(
            frame_onehot * motion_free[0].astype(jnp.float32)[None, :], axis=1
        )
        sequence = jnp.arange(frame_count * near, dtype=jnp.int32)
        same = (sequence[:, None] % near == sequence[None, :] % near) & (
            jnp.repeat(clip_ids, near)[:, None] == jnp.repeat(clip_ids, near)[None, :]
        )
        row_keep = jnp.tile(jnp.repeat(keep_frames, near), patch_count // (frame_count * near))
        rows = operands.rows_low
        own_conditioning = jnp.sum(own_onehot[:, None] * conditioning.astype(jnp.float32), axis=0)
        vars(operands).update(
            cotangent=cotangent[0, 0],
            cot_rows=cotangent[0, 0].reshape(operands.sent.shape),
            vectors=jnp.stack(
                [
                    rows[VEC.gain],
                    rows[VEC.shift],
                    rows[VEC.temporal],
                    rows[VEC.gate],
                    rows[VEC.gate] * own_keep,
                    jnp.full((model_width,), own_keep),
                    own_conditioning,
                    jnp.zeros((model_width,), jnp.float32),
                ]
            ),
            time_keep=jnp.broadcast_to(row_keep[:, None], (patch_count, LANES)),
            time_mask=jnp.where(same, 0.0, big_negative),
        )
        text_share = lax.dynamic_slice_in_dim(
            text_tokens[0], frame_index * text_projection.shape[0], text_projection.shape[0], 2
        )
        frame_text = jnp.pad(text_share, ((0, 0), (0, text_high - text_count), (0, 0)))
        text_turned = jnp.einsum("fs,stk->kft", frame_onehot.astype(jnp.bfloat16), frame_text)
        text_turned = text_turned.reshape(text_projection.shape[0], -1)
        got = backward(att_scale, True, operands, text_turned)
        return results(
            got.block_out[None, None],
            got.tokens_out[None, None],
            got.mods_out.reshape(-1, 8, model_width),
            jnp.sum(got.sums_out, axis=0),
            [got.share_time, got.share_reduce, got.share_expand, got.share_text, got.share_input],
            got.text_out,
            frame_index,
            row_count,
            bias_width,
        )
    text_share = lax.dynamic_slice_in_dim(
        text_tokens[0], frame_index * text_projection.shape[0], text_projection.shape[0], 2
    )
    own_text = lax.dynamic_index_in_dim(text_tokens[0], own_clip, 0, keepdims=False)
    vectors = (
        spatial_bias,
        cross_bias,
        expand_bias,
        reduce_bias,
        temporal_gain,
        temporal_shift,
        temporal_bias,
        temporal_gate,
    )
    vector_sizes = [vector.shape[0] for vector in vectors]
    vector_rows = -(-sum(vector_sizes) // (8 * LANES)) * 8
    packed_vectors = pack_rows([vector.astype(jnp.float32) for vector in vectors], vector_rows)
    mod_rows_high = -(-(6 * model_width) // (8 * LANES)) * 8
    frame_onehot = (clip_ids[:, None] == slot_ids[None, :]).astype(jnp.float32)
    frame_modulation = jnp.sum(frame_onehot[:, :, None] * modulation_part[None], axis=1)
    wholes, vecs, mods = gather_all(
        (
            text_projection,
            jnp.concatenate([spatial_input, spatial_output], axis=1),
            jnp.concatenate([cross_query, cross_memory, cross_output], axis=1),
            expand_weight,
            reduce_weight,
            jnp.concatenate([temporal_input, temporal_output], axis=1),
        ),
        packed_vectors,
        pack_rows([frame_modulation], mod_rows_high),
    )
    projection, whole_spatial, whole_text, whole_expand, whole_reduce, whole_time = wholes
    context = jnp.dot(own_text, projection, preferred_element_type=jnp.float32)
    own_modulation = jnp.sum(mods, axis=0).reshape(-1)[: 6 * model_width]
    shift_attend, scale_attend, gate_attend, shift_feed, scale_feed, gate_feed = jnp.split(
        own_modulation, 6
    )
    vecs = vecs.reshape(frame_count, -1)[:, : sum(vector_sizes)]
    vector_ends = [sum(vector_sizes[: index + 1]) for index in range(len(vector_sizes) - 1)]
    (
        whole_bias,
        whole_cross_bias,
        whole_expand_bias,
        whole_reduce_bias,
        whole_gain,
        whole_shift,
        whole_temporal_bias,
        whole_gate,
    ) = [part.reshape(-1) for part in jnp.split(vecs, vector_ends, axis=1)]
    whole_input, whole_output = whole_spatial[:, : 3 * model_width], whole_spatial[:, 3 * model_width :]
    whole_query = whole_text[:, :model_width]
    whole_memory = whole_text[:, model_width : 3 * model_width]
    whole_cross = whole_text[:, 3 * model_width :]
    whole_temporal, whole_temporal_out = whole_time[:, : 3 * model_width], whole_time[:, 3 * model_width :]
    tokens = latents[0, 0].astype(jnp.float32)
    attend_normal, attend_rate = normal_parts(tokens)
    normed_attend = (attend_normal * (1.0 + scale_attend) + shift_attend).astype(jnp.bfloat16)
    spatial_heads = jnp.dot(normed_attend, whole_input, preferred_element_type=jnp.float32).astype(
        jnp.bfloat16
    )
    spatial_heads = spatial_heads.reshape(patch_count, 1, 3, HEADS, head_size)
    spatial_att, spatial_logsum = attend(
        spatial_heads[:, :, 0], spatial_heads[:, :, 1], spatial_heads[:, :, 2], None, att_scale
    )
    spatial_low = spatial_att.reshape(patch_count, model_width).astype(jnp.bfloat16)
    branch_attend = jnp.dot(
        spatial_low, whole_output, preferred_element_type=jnp.float32
    ) + whole_bias.astype(jnp.float32)
    after_attend = tokens + gate_attend * branch_attend
    after_low = after_attend.astype(jnp.bfloat16)
    cross_heads = jnp.dot(after_low, whole_query, preferred_element_type=jnp.float32).astype(
        jnp.bfloat16
    )
    cross_heads = cross_heads.reshape(patch_count, 1, HEADS, head_size)
    context_low = context.astype(jnp.bfloat16)
    memory_heads = jnp.dot(context_low, whole_memory, preferred_element_type=jnp.float32).astype(
        jnp.bfloat16
    )
    memory_heads = memory_heads.reshape(text_count, 1, 2, HEADS, head_size)
    text_mask = (jnp.arange(text_count, dtype=jnp.int32) < own_length)[None, None, None, :]
    cross_att, cross_logsum = attend(
        cross_heads, memory_heads[:, :, 0], memory_heads[:, :, 1], text_mask, att_scale
    )
    cross_low = cross_att.reshape(patch_count, model_width).astype(jnp.bfloat16)
    branch_cross = jnp.dot(
        cross_low, whole_cross, preferred_element_type=jnp.float32
    ) + whole_cross_bias.astype(jnp.float32)
    after_cross = after_attend + branch_cross
    feed_normal, feed_rate = normal_parts(after_cross)
    normed_feed = (feed_normal * (1.0 + scale_feed) + shift_feed).astype(jnp.bfloat16)
    hidden_pre = jnp.dot(
        normed_feed, whole_expand, preferred_element_type=jnp.float32
    ) + whole_expand_bias.astype(jnp.float32)
    hidden_low = smooth_gelu(hidden_pre).astype(jnp.bfloat16)
    gelu_slope = slope_gelu(hidden_pre).astype(jnp.bfloat16)
    branch_feed = jnp.dot(
        hidden_low, whole_reduce, preferred_element_type=jnp.float32
    ) + whole_reduce_bias.astype(jnp.float32)
    after_feed = after_cross + gate_feed * branch_feed
    sent_low = after_feed.astype(jnp.bfloat16)
    low = lambda part: part.astype(jnp.bfloat16)
    gate_keep = whole_gate.astype(jnp.float32) * own_keep
    upstream = cotangent[0, 0].astype(jnp.float32)
    keep_frames = 1.0 - jnp.sum(frame_onehot * motion_free[0].astype(jnp.float32)[None, :], axis=1)
    time_mask = (clip_ids[:, None] == clip_ids[None, :])[None, None]
    gain_float = whole_gain.astype(jnp.float32)
    shift_float = whole_shift.astype(jnp.float32)
    columns = lax.all_to_all(sent_low[None], "frame", split_axis=1, concat_axis=0, tiled=True)
    frames_here = columns.shape[0]
    positions = columns.shape[1]
    normed_time = affine_norm(columns.astype(jnp.float32), gain_float, shift_float).astype(
        jnp.bfloat16
    )
    time_heads = jnp.einsum(
        "fpd,de->fpe", normed_time, whole_temporal, preferred_element_type=jnp.float32
    )
    time_heads = time_heads.astype(jnp.bfloat16).reshape(
        frames_here, positions, 3, HEADS, head_size
    )
    time_att, time_logsum = attend(
        time_heads[:, :, 0], time_heads[:, :, 1], time_heads[:, :, 2], time_mask, att_scale
    )
    time_low = time_att.reshape(frames_here, positions, model_width).astype(jnp.bfloat16)
    result = jnp.einsum(
        "fpd,de->fpe", time_low, whole_temporal_out, preferred_element_type=jnp.float32
    )
    result = result + whole_temporal_bias.astype(jnp.float32)
    result_low = result.astype(jnp.bfloat16)
    kept_state = (normed_time, time_heads, time_low, time_logsum)
    back_sent = (upstream * gate_keep).astype(jnp.bfloat16)
    back_columns = lax.all_to_all(back_sent[None], "frame", split_axis=1, concat_axis=0, tiled=True)
    normed_time, time_heads, time_low, time_logsum = kept_state
    frames_here, positions = (columns.shape[0], columns.shape[1])
    back_temporal_bias = jnp.sum(back_columns.astype(jnp.float32), axis=(0, 1))
    back_temporal_out = jnp.einsum(
        "fpd,fpe->de", time_low, back_columns, preferred_element_type=jnp.float32
    )
    back_time_att = jnp.einsum(
        "fpe,de->fpd", back_columns, whole_temporal_out, preferred_element_type=jnp.float32
    )
    back_time_att = back_time_att.astype(jnp.bfloat16).reshape(
        frames_here, positions, HEADS, head_size
    )
    back_time_queries, back_time_keys, back_time_values = attend_back(
        time_heads[:, :, 0],
        time_heads[:, :, 1],
        time_heads[:, :, 2],
        time_mask,
        att_scale,
        time_logsum,
        back_time_att,
    )
    back_time_heads = jnp.stack([back_time_queries, back_time_keys, back_time_values], axis=2)
    back_time_heads = back_time_heads.reshape(frames_here, positions, 3 * model_width).astype(
        jnp.bfloat16
    )
    back_temporal = jnp.einsum(
        "fpd,fpe->de", normed_time, back_time_heads, preferred_element_type=jnp.float32
    )
    back_normed = jnp.einsum(
        "fpe,de->fpd", back_time_heads, whole_temporal, preferred_element_type=jnp.float32
    )
    unused_norm, norm_back = jax.vjp(
        affine_norm, columns.astype(jnp.float32), gain_float, shift_float
    )
    back_inputs, back_gain, back_shift = norm_back(back_normed)
    returned, back_return = jnp.split(
        lax.all_to_all(
            jnp.concatenate([result_low, back_inputs.astype(jnp.bfloat16)], axis=2),
            "frame",
            split_axis=0,
            concat_axis=1,
            tiled=True,
        ),
        2,
        axis=2,
    )
    temporal_value = returned[0].astype(jnp.float32)
    block_output = (after_feed + gate_keep * temporal_value).astype(jnp.bfloat16)[None, None]
    back_gate = jnp.sum(upstream * temporal_value, axis=0) * own_keep
    text_high = -(-text_count // LANES) * LANES

    def padded_heads(heads, high):
        heads = jnp.transpose(heads[:, 0], (1, 0, 2))
        return jnp.pad(heads, ((0, 0), (0, high - heads.shape[1]), (0, HEAD_LANES - head_size)))

    padded_context = jnp.pad(context_low, ((0, text_high - text_count), (0, 0)))
    text_places = jnp.arange(text_high, dtype=jnp.int32) < own_length
    operands = dict(
        whole_spatial=whole_spatial,
        whole_text=whole_text,
        whole_expand=whole_expand,
        whole_reduce=whole_reduce,
        cotangent=cotangent[0, 0],
        branch_feed=low(branch_feed),
        hidden_turned=hidden_low.T,
        gelu_slope=gelu_slope,
        feed_turned=normed_feed.T,
        feed_normal=low(feed_normal),
        cross_turned=cross_low.T,
        cross_queries=padded_heads(cross_heads, patch_count),
        cross_keys=padded_heads(memory_heads[:, :, 0], text_high),
        cross_values=padded_heads(memory_heads[:, :, 1], text_high),
        after_turned=after_low.T,
        context_turned=padded_context.T,
        branch_attend=low(branch_attend),
        spatial_turned=spatial_low.T,
        queries=padded_heads(spatial_heads[:, :, 0], patch_count),
        keys=padded_heads(spatial_heads[:, :, 1], patch_count),
        values=padded_heads(spatial_heads[:, :, 2], patch_count),
        attend_turned=normed_attend.T,
        attend_normal=low(attend_normal),
        mods=jnp.pad(own_modulation.reshape(6, model_width), ((0, 2), (0, 0))),
        feed_rate=jnp.broadcast_to(feed_rate, (patch_count, LANES)),
        attend_rate=jnp.broadcast_to(attend_rate, (patch_count, LANES)),
        cross_logsum=jnp.broadcast_to(
            cross_logsum[0, :, None, :, 0], (HEADS, 8, patch_count)
        ),
        spatial_logsum=jnp.broadcast_to(
            spatial_logsum[0, :, None, :, 0], (HEADS, 8, patch_count)
        ),
        text_mask=jnp.broadcast_to(
            jnp.where(text_places, 0.0, big_negative)[:, None], (text_high, LANES)
        ),
    )
    own_conditioning = jnp.sum(own_onehot[:, None] * conditioning.astype(jnp.float32), axis=0)
    operands.update(back_sent=back_return[0])
    got = backward(att_scale, False, types.SimpleNamespace(**operands), None)
    input_gradient = got.tokens_out[None, None]
    rows = got.row_sums
    rows = rows.at[ROW.condition].set(own_conditioning).at[ROW.gate_t].set(back_gate)
    rows = rows.at[ROW.gain].set(back_gain).at[ROW.shift].set(back_shift)
    rows = rows.at[ROW.temporal].set(back_temporal_bias)
    mods = lax.all_gather(rows[:8], ("clip", "frame"), axis=0)
    sums = lax.psum(rows[8:], ("clip", "frame"))
    all_context = lax.all_gather(got.back_context[:text_count], "frame", axis=0)
    context_total = jnp.einsum("fs,ftd->std", frame_onehot, all_context.astype(jnp.float32))
    text_total = lax.psum(
        jnp.einsum(
            "stk,std->kd",
            text_share,
            low(context_total),
            preferred_element_type=jnp.float32,
        ).astype(jnp.bfloat16),
        "clip",
    )
    totals = [
        sum_shares((low(back_temporal), low(back_temporal_out))),
        sum_shares((got.part_reduce,)),
        sum_shares((got.part_expand,)),
        sum_shares((got.part_text,)),
        sum_shares((got.part_input,)),
    ]
    return results(
        block_output,
        input_gradient,
        mods,
        sums,
        totals,
        text_total,
        frame_index,
        row_count,
        bias_width,
    )


def solution(mesh):
    placed = (
        P("clip", "frame", None, None),
        P("clip", "frame", None, None),
        P("clip", None, None, None),
        P("clip", None),
        P("clip", None),
        P("clip", None),
        P("clip", None),
        P("frame", None),
        P("frame"),
        P("frame", None),
        P("frame", None),
        P("frame"),
        P("frame", None),
        P("frame", None),
        P("frame", None),
        P("frame", None),
        P("frame"),
        P("frame", None),
        P("frame"),
        P("frame", None),
        P("frame"),
        P("frame"),
        P("frame"),
        P("frame", None),
        P("frame", None),
        P("frame"),
        P("frame"),
    )
    return jax.shard_map(
        on_device,
        mesh=mesh,
        in_specs=placed,
        out_specs=(
            P("clip", "frame", None, None),
            P("clip", "frame", None, None),
            P("frame", None),
            P("frame"),
            P("frame", None),
            P("frame", None),
            P("frame"),
            P("frame", None),
            P("frame", None),
            P("frame", None),
            P("frame", None),
            P("frame"),
            P("frame", None),
            P("frame"),
            P("frame", None),
            P("frame"),
            P("frame"),
            P("frame"),
            P("frame", None),
            P("frame", None),
            P("frame"),
            P("frame"),
        ),
        check_vma=False,
    )
```

time: 1180 us -> 799 us (0.68)
  matrix products: 272 us -> 6.16 us
  Pallas kernels: 613 us -> 729 us
  local copies, waits for them, and re-layouts: 88.3 us -> 19 us
  other arithmetic: 90.8 us -> 30.6 us
  waiting for transfers between devices: 54.6 us -> 0 us
  starting transfers between devices: 24.5 us -> 0 us
  between operations: 19.1 us -> 4.56 us
    dot_general x49 -> x2, matrix products: 272 us -> 5.73 us  [the longest x1 5.24 us: results(): jnp.einsum('nd,ne->de', rows_condition, rows_gradient, precision=lax.Prec...]
    pallas_call x2, Pallas kernels: 613 us -> 729 us  [the longest x1 474 us: backward(): pl.pallas_call(functools.partial(back_kernel, together, att_scale, names)...]
    all_to_all x2 -> x0, waiting for transfers between devices: 53.4 us -> none  [the longest x1 36.6 us: on_device(): lax.all_to_all(jnp.concatenate([result_low, back_inputs.astype(jnp.bfloat...]
    convert_element_type x9 -> x0, local copies, waits for them, and re-layouts: 32.2 us -> none  [the longest x2 14.4 us: on_device(): back_time_heads.reshape(frames_here, positions, 3 * model_width)]
    reduce_sum x18 -> x3, other arithmetic: 32.8 us -> 2.95 us  [the longest x1 2.23 us: results(): jnp.sum(mods[:, ROW.gate_t], axis=0)]
    all_to_all x2 -> x0, starting transfers between devices: 24.5 us -> none  [the longest x1 17.6 us: on_device(): lax.all_to_all(sent_low[None], 'frame', split_axis=1, concat_axis=0, tile...]
    reshape x11 -> x2, local copies, waits for them, and re-layouts: 20.9 us -> 0.07 us  [the longest x1 0.06 us: on_device(): frame_modulation = frame_modulation.reshape(frame_count, 6, model_width)]
    convert_element_type x16 -> x10, other arithmetic: 31 us -> 11.2 us  [the longest x8 11.2 us: results(): high = lambda part: part.astype(jnp.float32)]
  transfers between devices with their start and end apart: 3 -> 0, of which waited for: 3 -> 0; matrix products, arithmetic and copies ran while one was open for 4% -> 0% of each run, Pallas kernels for 0% -> 0%
where the time goes in v2:
time: 799 us; the launch traced here: 790 us
  Pallas kernels  729 us (91%)
  other arithmetic  30.6 us (4%)
  local copies, waits for them, and re-layouts  19 us (2%)
    pallas_call x1, Pallas kernels, backward(): pl.pallas_call(functools.partial(back_kernel, together, att_scale, names)...  474 us
    pallas_call x1, Pallas kernels, forward(): pl.pallas_call(functools.partial(forward_kernel, att_scale, names), out_s...  255 us

profile of v2, /device:TPU:27, one launch (start us, length us, event | category | flops | bytes accessed | tf_op | source)
XLA Modules:
  0.0 789.8 jit_solution(7190178369417696439)
XLA Ops:
  0.7 1.4 reduce_max.9
  3.2 1.9 fusion.17
  5.2 1.3 fusion.16
  6.8 1.4 fusion.15
  9.8 0.8 convert_dynamic-update-slice_fusion
  14.1 1.4 dynamic-slice_bitcast_fusion
  15.5 1.1 pad.18.refs_9_
  16.6 1.3 fusion.18
  20.7 1.7 pad_maximum_fusion
  22.4 1.2 pad_maximum_fusion.2.refs_5_
  23.6 255.2 %forward.1 = (bf16[1152,4608]{1,0:T(8,128)(2,1)}, bf16[4096,1152]{1,0:T(8,128)(2,1)}, bf16[1152,4608]{1,0:T(8,128)(2,1)}, bf16[1152,4608]{1,0:T(8,128)(2,1)}, bf...) custom-call(bf16[144,4608]{1,0:T(8,128)(2,1)} %get-tuple-element.123, ...), custom_call_target="tpu_custom_call" | custom-call | tf_op jit(solution)/shard_map/forward/pallas_call | solution.py:1898
  279.4 0.8 slice_multiply_fusion
  280.2 0.8 slice.61
  281.7 1.1 constant_dynamic-slice_fusion.2
  283.2 1.3 copy.58
  284.5 1.2 copy.71
  286.0 0.8 broadcast_in_dim.87.refs_35_
  287.8 474.3 %backward.1 = (bf16[4608,1152]{1,0:T(8,128)(2,1)}, bf16[1152,4608]{1,0:T(8,128)(2,1)}, bf16[1152,6144]{1,0:T(8,128)(2,1)}, bf16[1152,3584]{1,0:T(8,128)(2,1)}, b...) custom-call(bf16[1152,4608]{1,0:T(8,128)(2,1)} %get-tuple-element.63, ...), custom_call_target="tpu_custom_call" | custom-call | tf_op jit(solution)/shard_map/backward/pallas_call | solution.py:1342
  762.1 1.4 copy.61
  763.5 2.2 slice_reduce_fusion
  765.9 5.2 fusion.5
  771.1 1.8 convert_element_type.133
  772.9 1.7 convert_element_type.134
  774.6 1.6 convert_element_type.129
  776.2 0.8 copy-done.2
  776.9 1.3 slice_convert_fusion.4
  778.3 1.4 slice_convert_fusion
  779.9 1.4 slice_convert_fusion.1
  781.3 1.2 slice_convert_fusion.2
  783.1 0.9 slice_convert_fusion.3
  786.1 2.5 copy.75
  788.6 1.0 copy.76
  (115 shorter events, 11.8 us)
Async XLA Ops:
  0.7 9.9 %copy-start = (bf16[144,6912]{1,0:T(8,128)(2,1)S(1)}, bf16[144,6912]{1,0:T(8,128)(2,1)}, u32[]{:S(2)}) copy-start(bf16[144,6912]{1,0:T(8,128)(2,1)} %param.34) | copy-start | bytes 5971972
  13.9 2.7 copy-start.18
  13.9 2.7 copy-start.19
  13.9 5.5 copy-start.20
  13.9 5.5 copy-start.21
  14.0 5.5 copy-start.22
  14.0 5.5 copy-start.23
  14.0 5.5 copy-start.24
  14.0 5.5 copy-start.25
  14.0 5.5 copy-start.26
  14.0 5.9 copy-start.17
  14.0 6.6 copy-start.9
  14.0 6.6 copy-start.11
  14.1 6.6 copy-start.12
  14.1 6.6 copy-start.13
  14.1 6.6 copy-start.14
  20.7 1.7 copy-start.8
  20.7 1.7 copy-start.15
  765.9 5.3 copy-start.5
  771.1 1.8 copy-start.4
  772.9 1.7 copy-start.6
  774.6 2.3 copy-start.2
  776.2 2.1 copy-start.3
  778.3 1.6 copy-start.10
  781.3 3.4 copy-start.16
  783.1 5.4 copy-start.7
  786.1 3.5 copy-start.1

commit v3 on v2

--- a/solution.py
+++ b/solution.py
@@ -177,6 +177,10 @@
         pl.when(condition)(copy.start)
         self.maybe.append((condition, copy))
 
+    def release(self, copy):
+        copy.wait_send()
+        self.started = [other for other in self.started if other is not copy]
+
     def finish(self):
         for copy in self.started:
             copy.wait_send()
@@ -259,7 +263,8 @@
         store(index).wait()
 
 
-ROW_TILE = 64
+ROW_TILE = 128
+HEAD_TILE = 64
 HEAD_LANES = 128
 MOD_ROWS = 6
 
@@ -285,7 +290,8 @@
 
 def by_rows(ref, size):
     if len(ref.shape) == 4:
-        return (ref, (1,) + ref.shape[1:], lambda step: (step, 0, 0, 0))
+        many = size // (ref.shape[1] * ref.shape[2])
+        return (ref, (many,) + ref.shape[1:], lambda step: (step, 0, 0, 0))
     return (ref, (size, ref.shape[1]), lambda step: (step, 0))
 
 
@@ -303,7 +309,7 @@
 
 def split_heads(source, first, heads, width, count):
     height = source.shape[0]
-    tile = min(height, ROW_TILE)
+    tile = min(height, HEAD_TILE)
 
     def step(index, carry):
         rows = tile_rows(index, tile)
@@ -317,7 +323,7 @@
 
 def merge_heads(heads, target, first, width, count):
     height = target.shape[0]
-    tile = min(height, ROW_TILE)
+    tile = min(height, HEAD_TILE)
 
     def step(index, carry):
         rows = tile_rows(index, tile)
@@ -328,29 +334,47 @@
     lax.fori_loop(0, height // tile, step, 0)
 
 
-def attention_back(att_scale, queries, keys, values, mask, logsum, upstream, outs):
+def attention_back(att_scale, queries, keys, values, mask, logsum, upstream, outs, group=1):
     out_queries, out_keys, out_values = outs
     count = queries.shape[0]
 
     def body(query, key, value):
-        head = pl.program_id(0)
-        query, key, value, given = query[0], key[0], value[0], upstream[head]
-        scores = dot_rows(key, query) * att_scale
+        heads = [pl.program_id(0) * group + index for index in range(group)]
+        query, key, value = ([ref[index] for index in range(group)] for ref in (query, key, value))
+        given = [upstream[head] for head in heads]
+        scores = [dot_rows(*pair) * att_scale for pair in zip(key, query)]
         if mask is not None:
-            scores = scores + mask[:, 0:1]
-        weights = jnp.exp(scores - logsum[head, 0:1, :])
-        back_weights = dot_rows(value, given)
-        inner = jnp.sum(back_weights * weights, axis=0, keepdims=True)
-        back_scores = (weights * (back_weights - inner)).astype(jnp.bfloat16)
-        out_values[head] = dot_plain(weights.astype(jnp.bfloat16), given).astype(jnp.bfloat16)
-        out_keys[head] = (dot_plain(back_scores, query) * att_scale).astype(jnp.bfloat16)
-        turned = lax.dot_general(
-            key, back_scores, (((0,), (0,)), ((), ())), preferred_element_type=jnp.float32
-        )
-        out_queries[head] = (turned * att_scale).T.astype(jnp.bfloat16)
-
-    per_head = lambda ref: (ref, (1,) + ref.shape[1:], lambda step: (step, 0, 0))
-    run_tiles(body, count, [per_head(queries), per_head(keys), per_head(values)], [])
+            scores = [score + mask[:, 0:1] for score in scores]
+        weights = [
+            jnp.exp(score - logsum[head, 0:1, :]) for score, head in zip(scores, heads)
+        ]
+        backs = [dot_rows(*pair) for pair in zip(value, given)]
+        inner = [
+            jnp.sum(back * weight, axis=0, keepdims=True) for back, weight in zip(backs, weights)
+        ]
+        backs = [
+            (weight * (back - total)).astype(jnp.bfloat16)
+            for weight, back, total in zip(weights, backs, inner)
+        ]
+        back_values = [
+            dot_plain(weight.astype(jnp.bfloat16), one).astype(jnp.bfloat16)
+            for weight, one in zip(weights, given)
+        ]
+        back_keys = [
+            (dot_plain(*pair) * att_scale).astype(jnp.bfloat16) for pair in zip(backs, query)
+        ]
+        turned = [
+            lax.dot_general(*pair, (((0,), (0,)), ((), ())), preferred_element_type=jnp.float32)
+            for pair in zip(key, backs)
+        ]
+        turned = [(one * att_scale).T.astype(jnp.bfloat16) for one in turned]
+        for index, head in enumerate(heads):
+            out_values[head] = back_values[index]
+            out_keys[head] = back_keys[index]
+            out_queries[head] = turned[index]
+
+    per_head = lambda ref: (ref, (group,) + ref.shape[1:], lambda step: (step, 0, 0))
+    run_tiles(body, count // group, [per_head(queries), per_head(keys), per_head(values)], [])
 
 
 ROW = types.SimpleNamespace(
@@ -500,6 +524,7 @@
             r.cross_logsum,
             r.head_in,
             (r.head_query, r.cross_key, r.cross_value),
+            group=4,
         )
         merge_heads(r.head_query, r.broad, 0, head_size, HEADS)
         merge_heads(r.cross_key, r.memory, 0, head_size, HEADS)
@@ -827,57 +852,150 @@
         r.part_reduce,
         cut(r.part_expand, 0, 3584),
         cut(r.part_expand, 3584, 1024),
-        r.part_text,
+        cut(r.part_text, 0, 4 * r.low.shape[1]),
+        cut(r.part_text, 4 * r.low.shape[1], 1536),
         cut(r.part_input, 0, 2048),
         cut(r.part_input, 2048, 1536),
     ]
     many = lambda name: [vars(r)[f"{name}_{index}"] for index in range(bundles)]
-    paired, halved, quartered, lined = (many(name) for name in LANDING)
+    halved, quartered, lined = (many(name) for name in LANDING)
     summed, crossed = halved, quartered
     outs = [
         r.share_time,
         r.share_reduce,
         cut(r.share_expand, 0, 3584),
         cut(r.share_expand, 3584, 1024),
-        r.share_text,
+        cut(r.share_text, 0, 4 * r.low.shape[1]),
+        cut(r.share_text, 4 * r.low.shape[1], 1536),
         cut(r.share_input, 0, 2048),
         cut(r.share_input, 2048, 1536),
     ]
 
-    def part_piece(index, unit, owner):
-        return whole_unit(parts[index], talls[index], unit, owner)
-
-    from_core = {}
-
-    def send(index, units=range(4)):
-        for slot in range(4):
-            owner = slot * 2 + 1 - core
-            for unit in units:
-                from_core[index, slot, unit] = copies.start(
-                    part_piece(index, unit, owner), paired[index].at[unit, slot], (column, sibling)
-                )
+    def part_piece(index, unit, slot):
+        ref = parts[index]
+        if talls[index]:
+            high = ref.shape[0] // 16
+            return rows_at(ref, slot * (4 * high) + unit * high, high, high)
+        high, wide = ref.shape[0] // 4, ref.shape[1] // 4
+        return ref.at[
+            pl.ds(pl.multiple_of(slot * high, high), high),
+            pl.ds(pl.multiple_of(unit * wide, LANES), wide),
+        ]
+
+    left_high = r.left_own.shape[0]
+    piece_high = left_high // 4
+
+    def swap_rows(source, target):
+        high = source.shape[0] // 8
+        return [
+            copies.start(
+                rows_at(source, (slot * 2 + 1 - core) * high, high, high),
+                target.at[pl.ds(slot * high, high)],
+                (column, sibling),
+            )
+            for slot in range(4)
+        ]
+
+    def swap(source, target):
+        return copies.start(source, target, (column, sibling))
+
+    def left_start(source, other, rows_got):
+        arrive(rows_got)
+        deep = pl.ds(0, source.shape[1])
+        started = [
+            pltpu.make_async_copy(
+                rows_at(source, (slot * 2 + core) * piece_high, piece_high, piece_high),
+                r.left_own.at[pl.ds(slot * piece_high, piece_high), deep],
+                r.left_sems.at[slot],
+            )
+            for slot in range(4)
+        ]
+        started.append(pltpu.make_async_copy(other, r.left_other.at[:, deep], r.left_sems.at[4]))
+        for copy in started:
+            copy.start()
+        return started
+
+    def arrive(got):
+        for copy in got:
+            copy.wait_recv()
+
+    def finish_left(started):
+        for copy in started:
+            copy.wait()
+
+    def part(started, right, got, other, target, size, count, place, first=0, deep=None):
+        finish_left(started)
+        if got is not None:
+            got.wait_recv()
+        deep = r.left_own.shape[1] if deep is None else deep
+
+        def body(block, out):
+            columns = tile_rows(pl.program_id(0) + first, size)
+            total = dot_plain(r.left_own[:, 0:deep], right[:, columns])
+            total = total + dot_plain(r.left_other[:, 0:deep], block[...])
+            out[...] = total.astype(jnp.bfloat16)
+
+        run_tiles(
+            body,
+            count,
+            [(other, (other.shape[0], size), lambda step: (0, step + first))],
+            [(target, (left_high, size), lambda step: (0, step + place))],
+        )
+
+    def part_reduce(got):
+        got.wait_recv()
+        arrive(hidden_got)
+        high = r.part_reduce.shape[0] // 4
+
+        def body(own, other, given, out):
+            total = dot_plain(own[...], r.low[...]) + dot_plain(other[...], given[...])
+            out[...] = total.astype(jnp.bfloat16)
+
+        own = r.hidden_turned.at[pl.ds(pl.multiple_of(core * high, high), 7 * high)]
+        run_tiles(
+            body,
+            4,
+            [
+                (own, (high, own.shape[1]), lambda step: (2 * step, 0)),
+                by_rows(r.other_hidden, high),
+                (r.given_feed, r.given_feed.shape, lambda step: (0, 0)),
+            ],
+            [by_rows(r.part_reduce, high)],
+        )
+
+    def part_output(started, got):
+        finish_left(started)
+        got.wait_recv()
+        width = r.low.shape[1]
+
+        def body(given, out):
+            total = dot_plain(r.left_own[...], r.low[...])
+            total = total + dot_plain(r.left_other[...], given[...])
+            out[:, 0:width] = total.astype(jnp.bfloat16)
+            out[:, width:] = jnp.zeros_like(out[:, width:])
+
+        wide = r.part_text.shape[1] // 4
+        run_tiles(
+            body,
+            1,
+            [(r.given_output, r.given_output.shape, lambda step: (0, 0))],
+            [(r.part_text, (left_high, wide), lambda step: (0, 3))],
+        )
 
     def stream(index, count, left_at, right_at, out_at):
-        wide = pl.ds(0, paired[index].shape[-1])
+        wide = pl.ds(0, halved[index].shape[-1])
         buffers = [ref.at[:, :, wide] for ref in (r.left_buf, r.right_buf, r.out_buf)]
         add_stream(count, left_at, right_at, out_at, *buffers, r.stream_sems)
 
     from_half, from_quarter, from_line, ends = {}, {}, {}, []
 
-    def pair(index):
-        for slot in range(4):
-            for unit in range(4):
-                from_core[index, slot, unit].wait_recv()
-        place = lambda step: paired[index].at[step // 4, step % 4]
-        stream(
-            index, 16, lambda step: part_piece(index, step // 4, (step % 4) * 2 + core), place, place
-        )
+    def go(index):
         if index == LINE_FIRST:
             for shift in range(1, 4):
                 other = (depth + shift) % 4
                 for unit in range(4):
                     from_line[index, shift, unit] = copies.start(
-                        paired[index].at[unit, other],
+                        part_piece(index, unit, other),
                         lined[index].at[shift - 1, unit],
                         (column, other * 2 + core),
                     )
@@ -886,7 +1004,7 @@
             near = across_x if slot < 2 else across_y
             for which, unit in enumerate((near, far)):
                 from_half[index, slot, which] = copies.start(
-                    paired[index].at[unit, slot], halved[index].at[slot, which], (near, frame)
+                    part_piece(index, unit, slot), halved[index].at[slot, which], (near, frame)
                 )
 
     def half(index):
@@ -900,7 +1018,7 @@
             unit = column + which * (
                 (1 - late) * (across_y - column) + late * (across_x - column)
             )
-            return paired[index].at[unit, slot]
+            return part_piece(index, unit, slot)
 
         place = lambda step: halved[index].at[step // 2, step % 2]
         stream(index, 8, source, place, place)
@@ -921,35 +1039,54 @@
                 quartered[index].at[other], lined[index].at[shift - 1], (column, other * 2 + core)
             )
 
+    def totals_of_four(count, sources, target, height, width):
+        box = (pl.ds(0, height), pl.ds(0, width))
+
+        def loads(index):
+            slot = index % 2
+            return [
+                pltpu.make_async_copy(
+                    source, r.four_buf.at[(slot, place) + box], r.four_sems.at[slot, place]
+                )
+                for place, source in enumerate(sources(index))
+            ]
+
+        def store(index):
+            slot = index % 2
+            return pltpu.make_async_copy(
+                r.out_buf.at[(slot,) + box], target(index), r.stream_sems.at[2, slot]
+            )
+
+        waiting = loads(0)
+        for copy in waiting:
+            copy.start()
+        for index in range(count):
+            ahead = loads(index + 1) if index + 1 < count else []
+            for copy in ahead:
+                copy.start()
+            for copy in waiting:
+                copy.wait()
+            waiting = ahead
+            if index >= 2:
+                store(index - 2).wait()
+            slot = index % 2
+            total = r.four_buf[slot, 0, 0:height, 0:width].astype(jnp.float32)
+            for place in range(1, 4):
+                total = total + r.four_buf[slot, place, 0:height, 0:width].astype(jnp.float32)
+            r.out_buf[slot, 0:height, 0:width] = total.astype(jnp.bfloat16)
+            store(index).start()
+        for index in range(max(0, count - 2), count):
+            store(index).wait()
+
     def total_of_four(own, others, target, height, width):
-        loads = [
-            pltpu.make_async_copy(
-                source,
-                r.four_buf.at[slot, pl.ds(0, height), pl.ds(0, width)],
-                r.stream_sems.at[0, slot],
-            )
-            for slot, source in enumerate([own] + others)
-        ]
-        for copy in loads:
-            copy.start()
-        for copy in loads:
-            copy.wait()
-        total = r.four_buf[0, 0:height, 0:width].astype(jnp.float32)
-        for slot in range(1, 4):
-            total = total + r.four_buf[slot, 0:height, 0:width].astype(jnp.float32)
-        r.out_buf[0, 0:height, 0:width] = total.astype(jnp.bfloat16)
-        copy = pltpu.make_async_copy(
-            r.out_buf.at[0, pl.ds(0, height), pl.ds(0, width)], target, r.stream_sems.at[2, 0]
-        )
-        copy.start()
-        copy.wait()
+        totals_of_four(1, lambda index: [own] + others, lambda index: target, height, width)
 
     spread, relayed = {}, []
 
     def hand_out(index):
         target = share_unit(outs[index], talls[index], column)
         spread[index] = [copies.start(target, target, peer) for peer in plane_peers[:2]]
-        if index >= bundles - 2:
+        if index >= bundles - 3:
             ends.extend(spread[index])
             ends.append(copies.start(target, target, plane_peers[2]))
 
@@ -966,13 +1103,13 @@
         for shift in range(1, 4):
             for unit in range(4):
                 from_line[index, shift, unit].wait_recv()
-        for unit in range(4):
-            total_of_four(
-                paired[index].at[unit, depth],
-                [lined[index].at[slot, unit] for slot in range(3)],
-                summed[index].at[unit],
-                *paired[index].shape[2:],
-            )
+        totals_of_four(
+            4,
+            lambda unit: [part_piece(index, unit, depth)]
+            + [lined[index].at[slot, unit] for slot in range(3)],
+            lambda unit: summed[index].at[unit],
+            *lined[index].shape[2:],
+        )
         for slot, peer in enumerate(plane_peers):
             from_half[index, slot] = copies.start(
                 summed[index].at[peer[0]], crossed[index].at[slot], peer
@@ -986,7 +1123,7 @@
             summed[index].at[column],
             [crossed[index].at[slot] for slot in range(3)],
             share_unit(outs[index], talls[index], column),
-            *paired[index].shape[2:],
+            *lined[index].shape[2:],
         )
         hand_out(index)
 
@@ -1081,10 +1218,6 @@
         for peer in frame_peers:
             got.append(copies.start(source.at[:, peer[1]], target.at[frame], peer))
         move(source.at[:, frame], r.held_cols, target.at[frame])
-
-    def arrive(got):
-        for copy in got:
-            copy.wait_recv()
 
     def rows_send():
         for peer in line_peers:
@@ -1113,99 +1246,131 @@
         for copy in own:
             copy.wait()
 
+    wide = r.low.shape[1]
+    third = wide // 3
     cols_send(r.cot_rows, r.cot_cols, cots_got)
+    hidden_got = swap_rows(r.hidden_turned, r.other_hidden)
+    feed_got = swap_rows(r.feed_turned, r.other_feed)
+    cross_got = swap_rows(r.cross_turned, r.other_cross)
+    after_got = swap_rows(r.after_turned, r.other_after)
+    text_got = swap_rows(r.context_turned, r.other_context)
+    spatial_got = swap_rows(r.spatial_turned, r.other_spatial)
+    attend_got = swap_rows(r.attend_turned, r.other_attend)
     do.clear()
     r.row_sums[ROW.condition : ROW.condition + 1, :] = r.vectors[6:7, :]
     do.time_first()
+    time_got = swap_rows(r.time_turned, r.other_time)
     do.time_heads()
     do.time_attention()
+    middle_got = swap_rows(r.middle_turned, r.other_middle)
     arrive(cots_got)
     do.time_given()
+    time_out = swap(r.low, r.given_time_out)
     do.time_attention_back()
+    time_in = swap(r.broad.at[:, pl.ds(0, 3 * wide)], r.given_time_in)
     do.time_normed()
     do.time_last()
     return_send(r.time_back, r.back_sent_cols, back_got)
-    do.time_in_part()
-    do.time_out_part()
-    send(0)
+    held = left_start(r.middle_turned, r.other_middle, middle_got)
+    part(held, r.low, time_out, r.given_time_out, r.part_time, third, 3, 9)
+    held = left_start(r.time_turned, r.other_time, time_got)
+    part(held, r.broad, time_in, r.given_time_in, r.part_time, third, 9, 0)
+    go(0)
+    held = left_start(r.feed_turned, r.other_feed, feed_got)
     do.time_result()
     arrive(back_got)
     return_send(r.time_result, r.returned_cols, result_got)
+    copies.release(time_out)
     do.feed_first()
-    pair(0)
-    do.reduce_part()
-    send(1)
+    feed = swap(r.low, r.given_feed)
+    part_reduce(feed)
+    go(1)
+    half(0)
+    copies.release(time_in)
     do.feed_hidden()
-    pair(1)
-    half(0)
-    do.expand_part()
-    send(2)
-    send(3)
+    hidden = swap(r.broad, r.given_hidden)
     do.feed_normed()
-    pair(2)
-    pair(3)
+    part(held, r.broad, hidden, r.given_hidden, r.part_expand, 512, 9, 0)
+    go(2)
+    go(3)
+    quarter(0)
+    half(1)
+    held = left_start(r.cross_turned, r.other_cross, cross_got)
+    copies.release(feed)
     do.feed_last()
-    half(1)
-    do.cross_part()
+    cross = swap(r.low, r.given_cross)
+    copies.release(hidden)
     do.cross_given()
-    quarter(0)
+    part(held, r.low, cross, r.given_cross, r.part_text, third, 3, 9)
+    held = left_start(r.after_turned, r.other_after, after_got)
+    do.cross_attention()
+    query = swap(r.broad.at[:, pl.ds(0, wide)], r.given_query)
+    memory = swap(r.memory, r.given_memory)
+    half(2)
+    quarter(1)
+    do.context_back()
+    context_send()
+    part(held, r.broad, query, r.given_query, r.part_text, third, 3, 0)
+    held = left_start(r.context_turned, r.other_context, text_got)
+    do.query_back()
+    deep = r.memory.shape[0]
+    part(held, r.memory, memory, r.given_memory, r.part_text, third, 6, 3, 0, deep)
+    go(4)
+    held = left_start(r.spatial_turned, r.other_spatial, spatial_got)
+    line(0)
+    copies.release(cross)
+    do.spatial_first()
+    output = swap(r.low, r.given_output)
+    quarter(2)
+    copies.release(query)
+    do.spatial_given()
+    part_output(held, output)
+    go(5)
+    held = left_start(r.attend_turned, r.other_attend, attend_got)
+    line_sums()
+    relay(0)
+    line(1)
+    do.spatial_attention()
+    inputs = swap(r.broad.at[:, pl.ds(0, r.given_input.shape[1])], r.given_input)
+    half(4)
+    line_last()
+    context_pair()
+    do.attend_normed()
+    part(held, r.broad, inputs, r.given_input, r.part_input, 512, 4, 0)
+    go(6)
+    part([], r.broad, None, r.given_input, r.part_input, 512, 3, 4, 4)
+    go(7)
+    half(5)
+    quarter(4)
     arrive(result_got)
     do.block_last()
-    do.cross_attention()
-    half(2)
-    line_sums()
-    line(0)
-    quarter(1)
-    do.query_part()
-    do.memory_part()
-    do.context_back()
-    context_send()
-    do.query_back()
-    do.spatial_first()
-    do.output_part()
-    send(4)
-    relay(0)
-    line(1)
-    line_last()
-    quarter(2)
-    do.spatial_given()
-    pair(4)
-    do.spatial_attention()
-    context_pair()
-    relay(1)
-    line(2)
-    half(4)
-    do.input_part(0, 4)
-    send(5)
-    do.input_part(4, 3)
-    send(6)
-    text_part()
-    relay(3)
-    quarter(4)
-    pair(5)
-    pair(6)
-    do.attend_normed()
     do.attend_last()
     rows_send()
+    line(2)
+    relay(1)
+    half(6)
+    quarter(5)
+    half(7)
+    rows_pair()
+    text_part()
+    quarter(6)
+    quarter(7)
+    line(4)
     relay(2)
-    half(5)
-    half(6)
-    rows_pair()
+    relay(3)
+    rows_plane()
     text_line()
-    line(4)
-    quarter(5)
-    quarter(6)
-    rows_plane()
-    relay(4)
     line(5)
     line(6)
+    line(7)
+    relay(4)
     for copy in ends:
         copy.wait_recv()
     copies.finish()
 
 
-LANDING = ("paired", "halved", "quartered", "lined")
-PART_TALLS = (False, True, False, False, False, False, False)
+LANDING = ("halved", "quartered", "lined")
+PART_TALLS = (False, True, False, False, False, False, False, False)
 LINE_FIRST = 3
 
 
@@ -1287,7 +1452,32 @@
         rows = o.cot_rows.shape
         cols = (rows[1], rows[0]) + rows[2:]
         hbm_out.update(cot_cols=shape(cols, low))
-        hbm_out.update(part_time=shape((width, 4 * width), low))
+        half = lambda full: shape((full.shape[0] // 2, full.shape[1]), low)
+        hbm_out.update(
+            part_time=shape((width // 2, 4 * width), low),
+            part_reduce=half(hbm_out["part_reduce"]),
+            part_expand=half(hbm_out["part_expand"]),
+            part_text=half(hbm_out["part_text"]),
+            part_input=half(hbm_out["part_input"]),
+            other_time=shape((width // 2, tokens), low),
+            other_middle=shape((width // 2, tokens), low),
+            other_hidden=half(o.hidden_turned),
+            other_feed=half(o.feed_turned),
+            other_cross=half(o.cross_turned),
+            other_after=half(o.after_turned),
+            other_context=half(o.context_turned),
+            other_spatial=half(o.spatial_turned),
+            other_attend=half(o.attend_turned),
+            given_time_out=shape((tokens, width), low),
+            given_time_in=shape((tokens, 3 * width), low),
+            given_feed=shape((tokens, width), low),
+            given_hidden=shape((tokens, hidden), low),
+            given_cross=shape((tokens, width), low),
+            given_query=shape((tokens, width), low),
+            given_memory=shape((text_count, 2 * width), low),
+            given_output=shape((tokens, width), low),
+            given_input=shape((tokens, 3 * width + LANES), low),
+        )
         hbm_out.update(time_result=shape(cols, low))
         hbm_out.update(time_back=shape(cols, low))
         hbm_out.update(back_sent_cols=shape(rows, low))
@@ -1296,12 +1486,12 @@
         hbm_out.update(mods_out=shape((4, 8, 8, width), full))
         hbm_out.update(sums_out=shape((4, ROW.high - 8, width), full))
         high = width // 8
-        wides = (width, width, 896, 256, width + third, 512, 384)
+        wides = (width, width, 896, 256, width, third, 512, 384)
         high = width // 8
         for index, wide in enumerate(wides):
             piece = (high, wide)
             first = index == LINE_FIRST
-            landing = [(4, 4), (4,) if first else (4, 2), (4,), (3, 4) if first else (3,)]
+            landing = [(4,) if first else (4, 2), (4,), (3, 4) if first else (3,)]
             for name, lead in zip(LANDING, landing):
                 hbm_out[f"{name}_{index}"] = shape(lead + piece, low)
         hbm_out.update(
@@ -1316,17 +1506,21 @@
         hbm_out.update(text_part=shape(text_shape, low))
         hbm_out.update(text_got=shape((3, text_shape[0] // 4, width), low))
         hbm_out.update(text_out=shape(text_shape, low))
-        remote = len(PART_TALLS) * (16 + 8 + 4 + 3 + 3) + 7 + 3 + 3 + 4 * 7 + 6
+        remote = 240
         piece = (high, width + third)
         scratch.update(
             send_sems=pltpu.SemaphoreType.DMA((remote,)),
             recv_sems=pltpu.SemaphoreType.DMA((remote,)),
             stream_sems=pltpu.SemaphoreType.DMA((3, PIECE_SLOTS)),
             local_sems=pltpu.SemaphoreType.DMA((2,)),
+            left_own=pltpu.VMEM((width // 2, tokens), low),
+            left_other=pltpu.VMEM((width // 2, tokens), low),
+            left_sems=pltpu.SemaphoreType.DMA((5,)),
             left_buf=pltpu.VMEM((PIECE_SLOTS,) + piece, low),
             right_buf=pltpu.VMEM((PIECE_SLOTS,) + piece, low),
             out_buf=pltpu.VMEM((PIECE_SLOTS,) + piece, low),
-            four_buf=pltpu.VMEM((4,) + piece, low),
+            four_buf=pltpu.VMEM((2, 4) + piece, low),
+            four_sems=pltpu.SemaphoreType.DMA((2, 4)),
             rows_all=pltpu.VMEM((8, ROW.high, width), full),
             sums=pltpu.VMEM((ROW.high - 8, width), full),
             time_normal=pltpu.VMEM((tokens, width), low),

time: 799 us -> 774 us (0.969)
  Pallas kernels: 729 us -> 702 us
    pallas_call x1, Pallas kernels: 474 us -> 447 us  [backward(): pl.pallas_call(functools.partial(back_kernel, together, att_scale, names)...]
where the time goes in v3:
time: 774 us; the launch traced here: 762 us
  Pallas kernels  702 us (91%)
  other arithmetic  30.2 us (4%)
  local copies, waits for them, and re-layouts  19.6 us (3%)
    pallas_call x1, Pallas kernels, backward(): pl.pallas_call(functools.partial(back_kernel, together, att_scale, names)...  447 us
    pallas_call x1, Pallas kernels, forward(): pl.pallas_call(functools.partial(forward_kernel, att_scale, names), out_s...  255 us

profile of v3, /device:TPU:27, one launch (start us, length us, event | category | flops | bytes accessed | tf_op | source)
XLA Modules:
  0.0 762.4 jit_solution(10968302522968071004)
XLA Ops:
  0.7 1.4 reduce_max.9
  3.2 1.9 fusion.17
  5.2 1.3 fusion.16
  6.8 1.4 fusion.15
  9.8 0.8 convert_dynamic-update-slice_fusion
  14.0 1.3 dynamic-slice_bitcast_fusion
  15.4 1.1 pad.18.refs_9_
  16.5 1.3 fusion.18
  20.6 1.7 pad_maximum_fusion
  22.3 1.2 pad_maximum_fusion.2.refs_5_
  23.5 255.2 %forward.1 = (bf16[1152,4608]{1,0:T(8,128)(2,1)}, bf16[4096,1152]{1,0:T(8,128)(2,1)}, bf16[1152,4608]{1,0:T(8,128)(2,1)}, bf16[1152,4608]{1,0:T(8,128)(2,1)}, bf...) custom-call(bf16[144,4608]{1,0:T(8,128)(2,1)} %get-tuple-element.123, ...), custom_call_target="tpu_custom_call" | custom-call | tf_op jit(solution)/shard_map/forward/pallas_call | solution.py:2092
  279.4 0.8 slice_multiply_fusion
  280.1 0.8 slice.61
  281.6 1.1 constant_dynamic-slice_fusion.2
  283.2 1.3 copy.58
  284.4 1.2 copy.71
  286.0 0.8 broadcast_in_dim.87.refs_35_
  287.7 446.6 %backward.1 = (bf16[2304,1152]{1,0:T(8,128)(2,1)}, bf16[576,4608]{1,0:T(8,128)(2,1)}, bf16[576,6144]{1,0:T(8,128)(2,1)}, bf16[576,3584]{1,0:T(8,128)(2,1)}, bf16...) custom-call(bf16[1152,4608]{1,0:T(8,128)(2,1)} %get-tuple-element.63, ...), custom_call_target="tpu_custom_call" | custom-call | tf_op jit(solution)/shard_map/backward/pallas_call | solution.py:1536
  734.3 1.4 copy.61
  735.8 1.9 slice_reduce_fusion
  737.8 5.2 fusion.5
  743.0 1.8 convert_element_type.133
  744.8 1.7 convert_element_type.134
  746.5 1.6 convert_element_type.129
  748.1 0.8 copy-done.2
  748.8 1.3 slice_convert_fusion.4
  750.9 1.4 slice_convert_fusion
  752.5 1.4 slice_convert_fusion.1
  753.9 1.2 slice_convert_fusion.2
  755.8 0.9 slice_convert_fusion.3
  758.7 2.5 copy.75
  761.2 1.0 copy.76
  (115 shorter events, 12.5 us)
Async XLA Ops:
  0.7 9.9 %copy-start = (bf16[144,6912]{1,0:T(8,128)(2,1)S(1)}, bf16[144,6912]{1,0:T(8,128)(2,1)}, u32[]{:S(2)}) copy-start(bf16[144,6912]{1,0:T(8,128)(2,1)} %param.34) | copy-start | bytes 5971972
  13.9 2.6 copy-start.18
  13.9 2.6 copy-start.19
  13.9 5.4 copy-start.20
  13.9 5.4 copy-start.21
  14.0 5.4 copy-start.22
  14.0 5.4 copy-start.23
  14.0 5.4 copy-start.24
  14.0 5.4 copy-start.25
  14.0 5.4 copy-start.26
  14.0 5.8 copy-start.17
  14.0 6.5 copy-start.14
  15.4 5.2 copy-start.9
  15.4 5.2 copy-start.11
  15.4 5.2 copy-start.12
  15.4 5.2 copy-start.13
  20.6 1.7 copy-start.8
  20.6 1.7 copy-start.15
  737.8 5.3 copy-start.5
  743.0 1.8 copy-start.4
  744.8 1.7 copy-start.6
  746.5 2.3 copy-start.2
  748.8 2.0 copy-start.3
  750.9 1.6 copy-start.10
  753.9 3.4 copy-start.16
  757.3 3.9 copy-start.7
  758.7 3.5 copy-start.1

commit v4 on v3

--- a/solution.py
+++ b/solution.py
@@ -1346,15 +1346,15 @@
     do.block_last()
     do.attend_last()
     rows_send()
-    line(2)
-    relay(1)
+    text_part()
     half(6)
     quarter(5)
     half(7)
-    rows_pair()
-    text_part()
+    line(2)
+    relay(1)
     quarter(6)
     quarter(7)
+    rows_pair()
     line(4)
     relay(2)
     relay(3)

time: 774 us -> 762 us (0.984)
  Pallas kernels: 702 us -> 688 us
    pallas_call x1, Pallas kernels: 447 us -> 433 us  [backward(): pl.pallas_call(functools.partial(back_kernel, together, att_scale, names)...]
where the time goes in v4:
time: 762 us; the launch traced here: 749 us
  Pallas kernels  688 us (90%)
  other arithmetic  30.2 us (4%)
  local copies, waits for them, and re-layouts  19.6 us (3%)
    pallas_call x1, Pallas kernels, backward(): pl.pallas_call(functools.partial(back_kernel, together, att_scale, names)...  433 us
    pallas_call x1, Pallas kernels, forward(): pl.pallas_call(functools.partial(forward_kernel, att_scale, names), out_s...  255 us

profile of v4, /device:TPU:27, one launch (start us, length us, event | category | flops | bytes accessed | tf_op | source)
XLA Modules:
  0.0 748.9 jit_solution(17005197427436543688)
XLA Ops:
  0.7 1.4 reduce_max.9
  3.2 1.9 fusion.17
  5.2 1.3 fusion.16
  6.8 1.4 fusion.15
  9.8 0.8 convert_dynamic-update-slice_fusion
  14.0 1.3 dynamic-slice_bitcast_fusion
  15.4 1.1 pad.18.refs_9_
  16.5 1.3 fusion.18
  20.6 1.7 pad_maximum_fusion
  22.3 1.2 pad_maximum_fusion.2.refs_5_
  23.5 255.2 %forward.1 = (bf16[1152,4608]{1,0:T(8,128)(2,1)}, bf16[4096,1152]{1,0:T(8,128)(2,1)}, bf16[1152,4608]{1,0:T(8,128)(2,1)}, bf16[1152,4608]{1,0:T(8,128)(2,1)}, bf...) custom-call(bf16[144,4608]{1,0:T(8,128)(2,1)} %get-tuple-element.123, ...), custom_call_target="tpu_custom_call" | custom-call | tf_op jit(solution)/shard_map/forward/pallas_call | solution.py:2092
  279.4 0.8 slice_multiply_fusion
  280.1 0.8 slice.61
  281.6 1.1 constant_dynamic-slice_fusion.2
  283.2 1.3 copy.58
  284.4 1.2 copy.71
  286.0 0.8 broadcast_in_dim.87.refs_35_
  287.7 433.1 %backward.1 = (bf16[2304,1152]{1,0:T(8,128)(2,1)}, bf16[576,4608]{1,0:T(8,128)(2,1)}, bf16[576,6144]{1,0:T(8,128)(2,1)}, bf16[576,3584]{1,0:T(8,128)(2,1)}, bf16...) custom-call(bf16[1152,4608]{1,0:T(8,128)(2,1)} %get-tuple-element.63, ...), custom_call_target="tpu_custom_call" | custom-call | tf_op jit(solution)/shard_map/backward/pallas_call | solution.py:1536
  720.8 1.4 copy.61
  722.2 1.9 slice_reduce_fusion
  724.2 5.2 fusion.5
  729.5 1.8 convert_element_type.133
  731.3 1.7 convert_element_type.134
  733.0 1.6 convert_element_type.129
  734.5 0.8 copy-done.2
  735.3 1.3 slice_convert_fusion.4
  737.3 1.4 slice_convert_fusion
  738.9 1.4 slice_convert_fusion.1
  740.4 1.2 slice_convert_fusion.2
  742.2 0.9 slice_convert_fusion.3
  745.1 2.5 copy.75
  747.7 1.0 copy.76
  (115 shorter events, 12.5 us)
Async XLA Ops:
  0.7 9.9 %copy-start = (bf16[144,6912]{1,0:T(8,128)(2,1)S(1)}, bf16[144,6912]{1,0:T(8,128)(2,1)}, u32[]{:S(2)}) copy-start(bf16[144,6912]{1,0:T(8,128)(2,1)} %param.34) | copy-start | bytes 5971972
  13.9 2.6 copy-start.18
  13.9 2.6 copy-start.19
  13.9 5.4 copy-start.20
  13.9 5.4 copy-start.21
  14.0 5.4 copy-start.22
  14.0 5.4 copy-start.23
  14.0 5.4 copy-start.24
  14.0 5.4 copy-start.25
  14.0 5.4 copy-start.26
  14.0 5.8 copy-start.17
  14.0 6.5 copy-start.14
  15.4 5.2 copy-start.9
  15.4 5.2 copy-start.11
  15.4 5.2 copy-start.12
  15.4 5.2 copy-start.13
  20.6 1.7 copy-start.8
  20.6 1.7 copy-start.15
  724.2 5.3 copy-start.5
  729.5 1.8 copy-start.4
  731.3 1.7 copy-start.6
  733.0 2.3 copy-start.2
  735.3 2.0 copy-start.3
  737.3 1.6 copy-start.10
  740.4 3.4 copy-start.16
  743.8 3.9 copy-start.7
  745.1 3.5 copy-start.1
